TPU v7x, 128 devices: a whole 4x4x4 slice. The times are simulated.
128 devices in a mesh: node: 32 (over y, z, core), head: 4 (over x).
Axes of the slice: x: 4, y: 4, z: 4, core: 2. Of those that a mesh axis runs over, the one named last changes fastest.
Arguments:
- queries: bfloat16 [8192, 5120], P(('node', 'head')), may hold values from -100 to 100
- keys: bfloat16 [8192, 1024], P(('node', 'head')), may hold values from -6 to 6
- values: bfloat16 [8192, 1024], P(('node', 'head')), may hold values from -6 to 6
- out_grad: bfloat16 [8192, 5120], P(('node', 'head')), may hold values from -6 to 6
- parent: int32 [32], replicated, may hold values from -1 to 7, as said below
- node_of_slot: int32 [32], replicated, may hold values from 0 to 31, each once
- live_tiles: int32 [32], replicated, may hold values from 1 to 2, as said below
Outputs:
- attended: bfloat16 [8192, 5120], P(('node', 'head'))
- query_grad: bfloat16 [8192, 5120], P(('node', 'head'))
- key_grad: bfloat16 [8192, 1024], P(('node', 'head'))
- value_grad: bfloat16 [8192, 1024], P(('node', 'head'))
Inputs may be any that keep to these rules, and one draw needn't show every extreme that they name: Node 0 is the root with parent -1; every other node's parent has a smaller index and is below 8, so only nodes 0 to 7 have children; a path from the root holds at most four nodes. `live_tiles`: the root's segment is full.
All inputs are finite; a program needn't handle non-finite values.
Results may differ from a plain program's by a relative error of at most 0.0085.
Values may be sent and summed in bfloat16 or wider, within the bound.
No kernel may reach another device: no remote copies, remote signals or barrier semaphores. Data moves between devices by JAX's collectives and lax.ppermute only.
A program may use at most 128 MiB of HBM per device.

v0:
```python
import jax
import jax.numpy as jnp
from jax import lax
from jax.sharding import PartitionSpec as P

HD = 128
TILE = 128


def lineage(start_node, parent):
    chain = [start_node]
    current = start_node
    for _ in range(3):
        upper = jnp.where(current >= 0, parent[jnp.maximum(current, 0)], -1)
        chain.append(upper)
        current = upper
    return jnp.stack(chain)


def build_mask(valid, live, seg_len, tile_len):
    rows = jnp.arange(seg_len)[:, None]
    columns = jnp.arange(4 * seg_len)[None, :]
    block = columns // seg_len
    position = columns % seg_len
    own = (block == 0) & (position <= rows)
    far = (block > 0) & valid[block] & (position // tile_len < live[block])
    return own | far


def local_pass(query_rows, grad_rows, blocks, allowed, head_size):
    seg_len = query_rows.shape[0]
    kv_width = blocks.shape[2] // 2
    kv_heads = kv_width // head_size
    group_size = query_rows.shape[1] // kv_width
    scale = head_size ** (-0.5)
    flat = blocks.reshape(4 * seg_len, 2 * kv_width)
    key_rows = flat[:, :kv_width].reshape(4 * seg_len, kv_heads, head_size)
    value_rows = flat[:, kv_width:].reshape(4 * seg_len, kv_heads, head_size)
    query_four = query_rows.reshape(seg_len, kv_heads, group_size, head_size)
    grad_four = grad_rows.reshape(seg_len, kv_heads, group_size, head_size)
    scores = (
        jnp.einsum("rkgd,tkd->kgrt", query_four, key_rows, preferred_element_type=jnp.float32)
        * scale
    )
    masked = jnp.where(allowed, scores, -jnp.inf)
    peak = jnp.max(masked, axis=-1, keepdims=True)
    total = jnp.sum(jnp.exp(masked - peak), axis=-1, keepdims=True)
    probs = jnp.exp(masked - (peak + jnp.log(total)))
    probs_b = probs.astype(jnp.bfloat16)
    attended = jnp.einsum(
        "kgrt,tkd->rkgd", probs_b, value_rows, preferred_element_type=jnp.float32
    ).astype(jnp.bfloat16)
    delta = jnp.einsum(
        "rkgd,rkgd->kgr", grad_four.astype(jnp.float32), attended.astype(jnp.float32)
    )
    dprobs = jnp.einsum("rkgd,tkd->kgrt", grad_four, value_rows, preferred_element_type=jnp.float32)
    dscores = (probs * (dprobs - delta[..., None])).astype(jnp.bfloat16)
    query_grad = (
        scale * jnp.einsum("kgrt,tkd->rkgd", dscores, key_rows, preferred_element_type=jnp.float32)
    ).astype(jnp.bfloat16)
    key_terms = jnp.einsum(
        "kgrt,rkgd->tkd", dscores, query_four, preferred_element_type=jnp.float32
    ).reshape(4 * seg_len, kv_width)
    value_terms = jnp.einsum(
        "kgrt,rkgd->tkd", probs_b, grad_four, preferred_element_type=jnp.float32
    ).reshape(4 * seg_len, kv_width)
    terms = jnp.concatenate([key_terms, value_terms], 1).reshape(4, seg_len, 2 * kv_width)
    return (attended.reshape(seg_len, -1), query_grad.reshape(seg_len, -1), terms)


def on_device(queries, keys, values, out_grad, parent, node_of_slot, live_tiles):
    query_rows, key_rows, value_rows, grad_rows = (
        lax.all_to_all(queries, "head", split_axis=1, concat_axis=0, tiled=True),
        lax.all_to_all(keys, "head", split_axis=1, concat_axis=0, tiled=True),
        lax.all_to_all(values, "head", split_axis=1, concat_axis=0, tiled=True),
        lax.all_to_all(out_grad, "head", split_axis=1, concat_axis=0, tiled=True),
    )
    seg_len = query_rows.shape[0]
    kv_width = key_rows.shape[1]
    node_count = lax.axis_size("node")
    here = lax.axis_index("node")
    paired = jnp.concatenate([key_rows, value_rows], 1)
    node_ids = jnp.arange(node_count, dtype=jnp.int32)
    slot_of_node = jnp.sum(node_ids[None, :] * (node_of_slot[None, :] == node_ids[:, None]), axis=1)
    my_node = node_of_slot[here]
    chain = lineage(my_node, parent)
    valid = chain >= 0
    safe = jnp.maximum(chain, 0)
    slots = jnp.where(valid, slot_of_node[safe], 0)
    live = jnp.where(valid, live_tiles[safe], 0)
    everything = lax.all_gather(paired, "node", axis=0, tiled=True).reshape(
        node_count, seg_len, 2 * kv_width
    )
    blocks = everything[slots]
    allowed = build_mask(valid, live, seg_len, TILE)
    attended, query_grad, terms = local_pass(query_rows, grad_rows, blocks, allowed, HD)
    terms = terms * valid.astype(jnp.float32)[:, None, None]
    row_slots = jnp.arange(lax.axis_size("node") * seg_len // seg_len)
    pick = ((row_slots[:, None] == slots[None, :]) & valid[None, :]).astype(jnp.float32)
    total = lax.psum_scatter(
        jnp.einsum("ka,asc->ksc", pick, terms, precision=lax.Precision.HIGHEST).reshape(
            lax.axis_size("node") * seg_len, 2 * kv_width
        ),
        "node",
        scatter_dimension=0,
        tiled=True,
    )
    key_grad = (HD ** (-0.5) * total[:, :kv_width]).astype(jnp.bfloat16)
    value_grad = total[:, kv_width:].astype(jnp.bfloat16)
    return (
        lax.all_to_all(attended, "head", split_axis=0, concat_axis=1, tiled=True),
        lax.all_to_all(query_grad, "head", split_axis=0, concat_axis=1, tiled=True),
        lax.all_to_all(key_grad, "head", split_axis=0, concat_axis=1, tiled=True),
        lax.all_to_all(value_grad, "head", split_axis=0, concat_axis=1, tiled=True),
    )


def solution(mesh):
    in_specs = (
        P(("node", "head"), None),
        P(("node", "head"), None),
        P(("node", "head"), None),
        P(("node", "head"), None),
        P(),
        P(),
        P(),
    )
    out_specs = (
        P(("node", "head"), None),
        P(("node", "head"), None),
        P(("node", "head"), None),
        P(("node", "head"), None),
    )
    return jax.shard_map(
        on_device, mesh=mesh, in_specs=in_specs, out_specs=out_specs, check_vma=False
    )
```

profile of v0, /device:TPU:0, one launch (start us, length us, event | category | flops | bytes accessed | tf_op | source)
XLA Modules:
  0.0 308.3 jit_solution(12782716277143337853)
XLA Ops:
  8.8 4.4 %all-to-all-start = ((bf16[64,4,256]{2,0,1:T(8,128)(2,1)}), bf16[64,4,256]{2,0,1:T(8,128)(2,1)S(1)}, u32[]{:S(2)}, u32[]{:S(2)}) async-start(bf16[64,4,256]{2,0,1:T(8,128)(2,1)} %bitcast.127), calls=%async_computation | async-start | bytes 262144 | tf_op jit(solution)/shard_map/all_to_all | solution.py:74
  14.1 5.1 %all-to-all-done = bf16[64,4,256]{2,0,1:T(8,128)(2,1)S(1)} async-done(((bf16[64,4,256]{2,0,1:T(8,128)(2,1)}), bf16[64,4,256]{2,0,1:T(8,128)(2,1)S(1)}, u32[]{:S(2)}, u32[]{:S(2)}) %all-to-all-start) | async-done | bytes 131104 | tf_op jit(solution)/shard_map/all_to_all | solution.py:74
  19.1 8.3 %all_to_all.146 = bf16[64,4,256]{2,0,1:T(8,128)(2,1)S(1)} all-to-all(bf16[64,4,256]{2,0,1:T(8,128)(2,1)S(1)} %bitcast.144), channel_id=1, replica_groups=mesh['node'=32,'head'=4] {'head'}, dimensions={1} | all-to-all | bytes 262144 | tf_op jit(solution)/shard_map/all_to_all | solution.py:75
  30.2 3.5 %all-to-all-start.2 = ((bf16[64,4,1280]{2,0,1:T(8,128)(2,1)}), bf16[64,4,1280]{2,0,1:T(8,128)(2,1)S(1)}, u32[]{:S(2)}, u32[]{:S(2)}) async-start(bf16[64,4,1280]{2,0,1:T(8,128)(2,1)} %bitcast.125), calls=%async_computation.2 | async-start | bytes 1310720 | tf_op jit(solution)/shard_map/all_to_all | solution.py:73
  48.8 4.8 %all-to-all-start.4 = ((bf16[64,4,1280]{2,0,1:T(8,128)(2,1)}), bf16[64,4,1280]{2,0,1:T(8,128)(2,1)}, u32[]{:S(2)}, u32[]{:S(2)}) async-start(bf16[64,4,1280]{2,0,1:T(8,128)(2,1)} %bitcast.124), calls=%async_computation.4 | async-start | bytes 1310720 | tf_op jit(solution)/shard_map/all_to_all | solution.py:76
  53.6 2.6 compare_select_fusion.1
  56.2 2.6 select_reduce_fusion.1
  64.8 17.2 %all-gather.2.cloned.1.call-done = bf16[8192,512]{1,0:T(8,128)(2,1)} async-done(((bf16[256,512]{1,0:T(8,128)(2,1)}), bf16[8192,512]{1,0:T(8,128)(2,1)}) %all-gather.2.cloned.1.call-update) | async-done | bytes 8388624 | tf_op jit(solution)/shard_map/all_gather | solution.py:91
  82.0 4.0 %gather_fusion.1 = bf16[4,256,512]{2,1,0:T(8,128)(2,1)S(1)} fusion(bf16[32,256,512]{2,1,0:T(8,128)(2,1)} %bitcast.147, s32[1024]{0:T(1024)S(1)} %pad_clamp_fusion), kind=kCustom, calls=%fused_computation.1 | custom fusion | bytes 2097168 | tf_op jit(solution)/shard_map/gather | solution.py:94
  94.7 2.4 convolution_bitcast_fusion
  99.8 8.1 %bitcast_convert_fusion = (f32[2,5,256,128]{2,3,1,0:T(8,128)}, bf16[2,128,5,256]{3,1,2,0:T(8,128)(2,1)}) fusion(bf16[1024,2,128,1]{0,2,3,1:T(8,128)(2,1)} %bitcast.140, f32[2,1024,256,5]{2,1,3,0:T(8,128)} %copy-done.2, f32[2,5,256]{2,1,0:T(8,128)S(1)} %log_add_fusion, pred[256,1024]{0,1:T(8,128)(4,1)S(1)} %fusion.9), kind=kOutput, calls=%fused_computation.26 | convolution fusion | flops 682229760 | bytes 13248512 | tf_op jit(solution)/shard_map/kgrt,tkd->rkgd/dot_general | solution.py:50
  110.1 2.7 multiply_reduce_fusion
  113.9 7.9 %fusion.1 = bf16[2,5,256,1024]{2,3,1,0:T(8,128)(2,1)S(1)} fusion(f32[2,1024,256,5]{2,1,3,0:T(8,128)} %copy-done.2, f32[2,5,256]{2,1,0:T(8,128)S(1)} %copy.117, f32[2,5,256]{2,1,0:T(8,128)S(1)} %log_add_fusion, pred[256,1024]{0,1:T(8,128)(4,1)S(1)} %fusion.9, bf16[1024,2,128,1]{0,2,3,1:T(8,128)(2,1)} %bitcast.141, bf16[256,2,5,128]{3,2,1,0:T(8,128)(2,1)} %copy-done.7), kind=kOutput, calls=%fused_computation.5 | convolution fusion | flops 686817280 | bytes 17190912 | tf_op jit(solution)/shard_map/rkgd,tkd->kgrt/dot_general | solution.py:56
  127.6 17.6 %fusion.4 = f32[32,256,512]{2,0,1:T(8,128)S(1)} fusion(f32[4,256,512]{2,1,0:T(8,128)S(1)} %maximum_multiply_fusion, s32[4]{0:T(128)S(1)} %get-tuple-element.4, pred[4]{0:T(512)(128)(4,1)S(1)} %get-tuple-element.5), kind=kOutput, calls=%fused_computation.13 | convolution fusion | flops 201326848 | bytes 18874388 | tf_op jit(solution)/shard_map/ka,asc->ksc/dot_general | solution.py:101
  145.2 19.1 %copy.104 = f32[32,256,512]{2,1,0:T(8,128)} copy(f32[32,256,512]{2,0,1:T(8,128)S(1)} %fusion.4) | data formatting | bytes 33554432 | tf_op jit(solution)/shard_map/ka,asc->ksc/dot_general | solution.py:101
  168.0 4.5 %all-to-all-start.3 = ((bf16[4,64,1280]{2,1,0:T(8,128)(2,1)}), bf16[4,64,1280]{2,1,0:T(8,128)(2,1)S(1)}, u32[]{:S(2)}, u32[]{:S(2)}) async-start(bf16[4,64,1280]{2,1,0:T(8,128)(2,1)} %all_to_all.119), calls=%async_computation.3 | async-start | bytes 1310720 | tf_op jit(solution)/shard_map/all_to_all | solution.py:111
  172.5 3.8 %fusion.7 = bf16[256,2,5,128]{0,3,2,1:T(8,128)(2,1)S(1)} fusion(bf16[1024,2,128,1]{0,2,3,1:T(8,128)(2,1)S(1)} %bitcast.130, bf16[2,5,256,1024]{2,3,1,0:T(8,128)(2,1)} %copy-done.3), kind=kOutput, calls=%fused_computation.20 | convolution fusion | flops 671744000 | bytes 6422528 | tf_op jit(solution)/shard_map/kgrt,tkd->rkgd/dot_general | solution.py:59
  178.9 4.9 %all-to-all-done.3 = bf16[4,64,1280]{2,1,0:T(8,128)(2,1)S(1)} async-done(((bf16[4,64,1280]{2,1,0:T(8,128)(2,1)}), bf16[4,64,1280]{2,1,0:T(8,128)(2,1)S(1)}, u32[]{:S(2)}, u32[]{:S(2)}) %all-to-all-start.3) | async-done | bytes 655392 | tf_op jit(solution)/shard_map/all_to_all | solution.py:111
  183.8 3.5 %all-to-all-start.5 = ((bf16[4,64,1280]{2,1,0:T(8,128)(2,1)}), bf16[4,64,1280]{2,1,0:T(8,128)(2,1)S(1)}, u32[]{:S(2)}, u32[]{:S(2)}) async-start(bf16[4,64,1280]{2,1,0:T(8,128)(2,1)} %all_to_all.126), calls=%async_computation.5 | async-start | bytes 1310720 | tf_op jit(solution)/shard_map/all_to_all | solution.py:112
  187.3 92.1 %reduce-scatter.2.cloned.1.call-done = f32[256,512]{1,0:T(8,128)} async-done(((f32[8192,512]{1,0:T(8,128)}), f32[256,512]{1,0:T(8,128)}) %reduce-scatter.2.cloned.1.call-update) | async-done | bytes 524304 | tf_op jit(solution)/shard_map/reduce_scatter | solution.py:100
  281.0 4.2 %all-to-all-start.7 = ((bf16[4,64,256]{2,1,0:T(8,128)(2,1)}), bf16[4,64,256]{2,1,0:T(8,128)(2,1)S(1)}, u32[]{:S(2)}, u32[]{:S(2)}) async-start(bf16[4,64,256]{2,1,0:T(8,128)(2,1)} %bitcast.54), calls=%async_computation.8 | async-start | bytes 262144 | tf_op jit(solution)/shard_map/all_to_all | solution.py:114
  286.9 4.3 %all-to-all-done.7 = bf16[4,64,256]{2,1,0:T(8,128)(2,1)S(1)} async-done(((bf16[4,64,256]{2,1,0:T(8,128)(2,1)}), bf16[4,64,256]{2,1,0:T(8,128)(2,1)S(1)}, u32[]{:S(2)}, u32[]{:S(2)}) %all-to-all-start.7) | async-done | bytes 131104 | tf_op jit(solution)/shard_map/all_to_all | solution.py:114
  291.2 3.3 %all-to-all-start.6 = ((bf16[4,64,256]{2,1,0:T(8,128)(2,1)}), bf16[4,64,256]{2,1,0:T(8,128)(2,1)S(1)}, u32[]{:S(2)}, u32[]{:S(2)}) async-start(bf16[4,64,256]{2,1,0:T(8,128)(2,1)} %bitcast.52), calls=%async_computation.7 | async-start | bytes 262144 | tf_op jit(solution)/shard_map/all_to_all | solution.py:113
  297.0 3.5 %all-to-all-done.6 = bf16[4,64,256]{2,1,0:T(8,128)(2,1)S(1)} async-done(((bf16[4,64,256]{2,1,0:T(8,128)(2,1)}), bf16[4,64,256]{2,1,0:T(8,128)(2,1)S(1)}, u32[]{:S(2)}, u32[]{:S(2)}) %all-to-all-start.6) | async-done | bytes 131104 | tf_op jit(solution)/shard_map/all_to_all | solution.py:113
  (75 shorter events, 56.0 us)
Async XLA Ops:
  7.2 37.7 %copy-start = (s32[32]{0:T(128)S(1)}, s32[32]{0:T(128)}, u32[]{:S(2)}) copy-start(s32[32]{0:T(128)} %param.13) | copy-start | bytes 388
  8.8 10.4 %all-to-all-start = ((bf16[64,4,256]{2,0,1:T(8,128)(2,1)}), bf16[64,4,256]{2,0,1:T(8,128)(2,1)S(1)}, u32[]{:S(2)}, u32[]{:S(2)}) async-start(bf16[64,4,256]{2,0,1:T(8,128)(2,1)} %bitcast.127), calls=%async_computation | async-start | bytes 262144 | tf_op jit(solution)/shard_map/all_to_all | solution.py:74
  13.1 68.9 %all-gather.2.cloned.1.call-start = ((), (), s32[]{:S(2)}) async-start(), calls=%async_computation.9 | async-start | bytes 8650752 | tf_op jit(solution)/shard_map/all_gather | solution.py:91
  30.2 18.6 %all-to-all-start.2 = ((bf16[64,4,1280]{2,0,1:T(8,128)(2,1)}), bf16[64,4,1280]{2,0,1:T(8,128)(2,1)S(1)}, u32[]{:S(2)}, u32[]{:S(2)}) async-start(bf16[64,4,1280]{2,0,1:T(8,128)(2,1)} %bitcast.125), calls=%async_computation.2 | async-start | bytes 1310720 | tf_op jit(solution)/shard_map/all_to_all | solution.py:73
  48.8 13.6 %all-to-all-start.4 = ((bf16[64,4,1280]{2,0,1:T(8,128)(2,1)}), bf16[64,4,1280]{2,0,1:T(8,128)(2,1)}, u32[]{:S(2)}, u32[]{:S(2)}) async-start(bf16[64,4,1280]{2,0,1:T(8,128)(2,1)} %bitcast.124), calls=%async_computation.4 | async-start | bytes 1310720 | tf_op jit(solution)/shard_map/all_to_all | solution.py:76
  53.6 225.8 %reduce-scatter.2.cloned.1.call-start = ((), (), s32[]{:S(2)}) async-start(), calls=%async_computation.10 | async-start | bytes 17301504 | tf_op jit(solution)/shard_map/reduce_scatter | solution.py:100
  64.8 29.9 %copy-start.7 = (bf16[256,2,5,128]{3,2,1,0:T(8,128)(2,1)}, bf16[256,2,5,128]{3,2,1,0:T(8,128)(2,1)S(1)}, u32[]{:S(2)}) copy-start(bf16[256,2,5,128]{3,2,1,0:T(8,128)(2,1)S(1)} %reshape.468) | copy-start | bytes 1966084
  88.3 6.3 %copy-start.4 = (bf16[1024,256]{0,1:T(8,128)(2,1)}, bf16[1024,256]{0,1:T(8,128)(2,1)S(1)}, u32[]{:S(2)}) copy-start(bf16[1024,256]{0,1:T(8,128)(2,1)S(1)} %copy.127) | copy-start | bytes 1572868
  92.5 4.6 %copy-start.2 = (f32[2,1024,256,5]{2,1,3,0:T(8,128)}, f32[2,1024,256,5]{2,1,3,0:T(8,128)S(1)}, u32[]{:S(2)}) copy-start(f32[2,1024,256,5]{2,1,3,0:T(8,128)S(1)} %get-tuple-element.19) | copy-start | bytes 31457284
  121.8 2.3 copy-start.3
  124.1 3.2 %copy-start.6 = (f32[4,256,256]{2,1,0:T(8,128)S(1)}, f32[4,256,256]{2,1,0:T(8,128)}, u32[]{:S(2)}) copy-start(f32[4,256,256]{2,1,0:T(8,128)} %concatenate.38) | copy-start | bytes 3145732
  164.3 1.1 copy-start.8
  164.3 8.2 %copy-start.5 = (bf16[1024,256]{0,1:T(8,128)(2,1)S(1)}, bf16[1024,256]{0,1:T(8,128)(2,1)}, u32[]{:S(2)}) copy-start(bf16[1024,256]{0,1:T(8,128)(2,1)} %copy-done.4) | copy-start | bytes 1572868
  164.4 136.8 %copy-start.1 = (s32[32]{0:T(128)S(1)}, s32[32]{0:T(128)}, u32[]{:S(2)}) copy-start(s32[32]{0:T(128)} %param.13) | copy-start | bytes 388
  168.0 15.8 %all-to-all-start.3 = ((bf16[4,64,1280]{2,1,0:T(8,128)(2,1)}), bf16[4,64,1280]{2,1,0:T(8,128)(2,1)S(1)}, u32[]{:S(2)}, u32[]{:S(2)}) async-start(bf16[4,64,1280]{2,1,0:T(8,128)(2,1)} %all_to_all.119), calls=%async_computation.3 | async-start | bytes 1310720 | tf_op jit(solution)/shard_map/all_to_all | solution.py:111
  183.8 97.2 %all-to-all-start.5 = ((bf16[4,64,1280]{2,1,0:T(8,128)(2,1)}), bf16[4,64,1280]{2,1,0:T(8,128)(2,1)S(1)}, u32[]{:S(2)}, u32[]{:S(2)}) async-start(bf16[4,64,1280]{2,1,0:T(8,128)(2,1)} %all_to_all.126), calls=%async_computation.5 | async-start | bytes 1310720 | tf_op jit(solution)/shard_map/all_to_all | solution.py:112
  281.0 10.2 %all-to-all-start.7 = ((bf16[4,64,256]{2,1,0:T(8,128)(2,1)}), bf16[4,64,256]{2,1,0:T(8,128)(2,1)S(1)}, u32[]{:S(2)}, u32[]{:S(2)}) async-start(bf16[4,64,256]{2,1,0:T(8,128)(2,1)} %bitcast.54), calls=%async_computation.8 | async-start | bytes 262144 | tf_op jit(solution)/shard_map/all_to_all | solution.py:114
  291.2 9.3 %all-to-all-start.6 = ((bf16[4,64,256]{2,1,0:T(8,128)(2,1)}), bf16[4,64,256]{2,1,0:T(8,128)(2,1)S(1)}, u32[]{:S(2)}, u32[]{:S(2)}) async-start(bf16[4,64,256]{2,1,0:T(8,128)(2,1)} %bitcast.52), calls=%async_computation.7 | async-start | bytes 262144 | tf_op jit(solution)/shard_map/all_to_all | solution.py:113
Sparse Core Ops, SparseCore 0:
  28.3 53.6 all-gather.1
  164.5 114.8 reduce-scatter.1
where the time goes:
time: 313 us; the launch traced here: 308 us
  waiting for transfers between devices  129 us (41%)
  local copies, waits for them, and re-layouts  65.6 us (21%)
  matrix products  43.3 us (14%)
  starting transfers between devices  28.2 us (9%)
  between operations  17.8 us (6%)
  other arithmetic  15.9 us (5%)
  blocking collectives  8.35 us (3%)
    reduce_scatter x1, waiting for transfers between devices, on_device(): lax.psum_scatter(jnp.einsum('ka,asc->ksc', pick, terms, precision=lax.Pre...  92.1 us
    dot_general x1, local copies, waits for them, and re-layouts, on_device(): jnp.einsum('ka,asc->ksc', pick, terms, precision=lax.Precision.HIGHEST)  19.1 us
    dot_general x1, matrix products, on_device(): jnp.einsum('ka,asc->ksc', pick, terms, precision=lax.Precision.HIGHEST)  17.6 us
    all_gather x1, waiting for transfers between devices, on_device(): lax.all_gather(paired, 'node', axis=0, tiled=True)  17.2 us
    unnamed x21, local copies, waits for them, and re-layouts  9.11 us
    all_to_all x1, blocking collectives, on_device(): lax.all_to_all(values, 'head', split_axis=1, concat_axis=0, tiled=True)  8.35 us
    dot_general x1, matrix products, local_pass(): jnp.einsum('kgrt,tkd->rkgd', probs_b, value_rows, preferred_element_type=...  8.07 us
    dot_general x1, matrix products, local_pass(): jnp.einsum('rkgd,tkd->kgrt', grad_four, value_rows, preferred_element_typ...  7.9 us
  transfers between devices with their start and end apart: 9, of which 7 were waited for; matrix products, arithmetic and copies ran while one was open for 11% of the time, Pallas kernels for 0%

commit v1 on v0

v1 whole, which is shorter than its diff:
```python
import functools

import jax
import jax.numpy as jnp
from jax import lax
from jax.experimental import pallas as pl
from jax.experimental.pallas import tpu as pltpu
from jax.sharding import Mesh
from jax.sharding import PartitionSpec as P

HD = 128
TILE = 128
SEG = 256
GROUP = 5
KV_HEADS = 8
INNER = 8
NODES = 32
CHIPS = 16
QW = GROUP * HD
WIDE = 2 * QW + 2 * HD
SCALE = HD ** (-0.5)
BF = jnp.bfloat16
F32 = jnp.float32

ALL = ("chip", "core", "head")
GROUP_AXES = ("core", "head")


def smem():
    return pl.BlockSpec(memory_space=pltpu.SMEM)


def vmem():
    return pl.BlockSpec(memory_space=pltpu.VMEM)


def nt_dot(left, right):
    return lax.dot_general(left, right, (((1,), (1,)), ((), ())), preferred_element_type=F32)


def nn_dot(left, right):
    return lax.dot_general(left, right, (((1,), (0,)), ((), ())), preferred_element_type=F32)


def select_kernel(node_of_slot, pieces, out):
    for slot in range(NODES):
        node = node_of_slot[slot]

        @pl.when(node < INNER)
        def _():
            row = pl.multiple_of(node * 32, 32)
            block = pieces[slot]
            for chip in range(CHIPS):
                out[chip, pl.ds(row, 32), :] = block


def attention_kernel(
    chip, parent, node_of_slot, live_tiles, mine, far, out, terms, key_all, value_all, bias, acc
):
    acc[...] = jnp.zeros_like(acc)

    def per_slot(core, carry):
        base = pl.multiple_of(core * SEG, SEG)
        me = node_of_slot[2 * chip[0] + core]
        key_all[0:SEG, :] = mine[pl.ds(base, SEG), 2 * QW : 2 * QW + HD]
        value_all[0:SEG, :] = mine[pl.ds(base, SEG), 2 * QW + HD : WIDE]
        token = lax.broadcasted_iota(jnp.int32, (SEG, SEG), 0)
        row = lax.broadcasted_iota(jnp.int32, (SEG, SEG), 1)
        bias[0:SEG, :] = jnp.where(token <= row, 0.0, -jnp.inf)
        tile = lax.rem(token, 32) // 16
        current = me
        starts = []
        for step in range(1, 4):
            upper = jnp.where(current >= 0, parent[jnp.maximum(current, 0)], -1)
            safe = jnp.maximum(upper, 0)
            live = jnp.where(upper >= 0, live_tiles[safe], 0)
            start = pl.multiple_of(safe * 32, 32)
            starts.append(start)
            here = slice(step * SEG, (step + 1) * SEG)
            key_all[here, :] = far[0:8, pl.ds(start, 32), :].reshape(SEG, HD)
            value_all[here, :] = far[8:16, pl.ds(start, 32), :].reshape(SEG, HD)
            bias[here, :] = jnp.where(tile < live, 0.0, -jnp.inf)
            current = upper

        keys = key_all[...]
        values = value_all[...]
        keys_t = keys.T
        values_t = values.T
        key_terms = jnp.zeros((4 * SEG, HD), F32)
        value_terms = jnp.zeros((4 * SEG, HD), F32)
        for g in range(GROUP):
            columns = slice(g * HD, (g + 1) * HD)
            grad_columns = slice(QW + g * HD, QW + (g + 1) * HD)
            query = mine[pl.ds(base, SEG), columns]
            grad = mine[pl.ds(base, SEG), grad_columns]
            scores = nt_dot(keys, query) * SCALE + bias[...]
            peak = jnp.max(scores, axis=0, keepdims=True)
            weight = jnp.exp(scores - peak)
            total = jnp.sum(weight, axis=0, keepdims=True)
            probs = weight * (1.0 / total)
            probs_b = probs.astype(BF)
            attended = nn_dot(values_t, probs_b).T.astype(BF)
            out[pl.ds(base, SEG), columns] = attended
            delta = jnp.sum(
                grad.astype(F32).T * attended.astype(F32).T, axis=0, keepdims=True
            )
            dprobs = nt_dot(values, grad)
            dscores = (probs * (dprobs - delta)).astype(BF)
            query_grad = nn_dot(keys_t, dscores) * SCALE
            out[pl.ds(base, SEG), grad_columns] = query_grad.T.astype(BF)
            key_terms = key_terms + nn_dot(dscores, query)
            value_terms = value_terms + nn_dot(probs_b, grad)
        key_terms = key_terms * SCALE
        out[pl.ds(base, SEG), 2 * QW : 2 * QW + HD] = key_terms[0:SEG].astype(BF)
        out[pl.ds(base, SEG), 2 * QW + HD : WIDE] = value_terms[0:SEG].astype(BF)
        for step in range(1, 4):
            start = starts[step - 1]
            here = slice(step * SEG, (step + 1) * SEG)
            acc[0:8, pl.ds(start, 32), :] += key_terms[here].reshape(8, 32, HD)
            acc[8:16, pl.ds(start, 32), :] += value_terms[here].reshape(8, 32, HD)

        @pl.when(me < INNER)
        def _():
            for piece in range(8):
                for quarter in range(4):
                    first = quarter * 64 + piece * 8
                    where = pl.ds(pl.multiple_of(me * 32 + quarter * 8, 8), 8)
                    acc[piece, where, :] += key_terms[first : first + 8]
                    acc[8 + piece, where, :] += value_terms[first : first + 8]

        return carry

    lax.fori_loop(0, 2, per_slot, 0)
    terms[...] = acc[...].astype(BF)


def sum_kernel(node_of_slot, parts, out, total):
    sums = parts[0].astype(F32)
    for chip in range(1, CHIPS):
        sums = sums + parts[chip].astype(F32)
    total[...] = sums.astype(BF)
    for slot in range(NODES):
        node = node_of_slot[slot]

        @pl.when(node < INNER)
        def _():
            out[slot] = total[pl.ds(pl.multiple_of(node * 32, 32), 32), :]

        @pl.when(node >= INNER)
        def _():
            out[slot] = jnp.zeros((32, HD), BF)


def on_device(queries, keys, values, out_grad, parent, node_of_slot, live_tiles):
    rows = queries.shape[0]
    chip = lax.axis_index("chip")
    core = lax.axis_index("core")

    pieces = jnp.concatenate([keys, values], 0).reshape(16, 8, KV_HEADS, HD)
    pieces = pieces.transpose(0, 2, 1, 3).reshape(CHIPS * KV_HEADS, 8, HD)
    pieces = lax.all_to_all(pieces, ALL, split_axis=0, concat_axis=0, tiled=True)
    inner = pl.pallas_call(
        select_kernel,
        out_shape=jax.ShapeDtypeStruct((CHIPS, INNER * 32, HD), BF),
        in_specs=[smem(), vmem()],
        out_specs=vmem(),
        name="select_inner",
    )(node_of_slot, pieces.reshape(NODES, 32, HD))
    far = lax.all_to_all(inner, "chip", split_axis=0, concat_axis=0, tiled=True)

    def by_head(array, width):
        return array.reshape(rows, KV_HEADS, width).transpose(1, 0, 2)

    mine = jnp.concatenate(
        [by_head(queries, QW), by_head(out_grad, QW), by_head(keys, HD), by_head(values, HD)], 2
    )
    mine = lax.all_to_all(mine, GROUP_AXES, split_axis=0, concat_axis=0, tiled=True)

    out, terms = pl.pallas_call(
        attention_kernel,
        out_shape=(
            jax.ShapeDtypeStruct((2 * SEG, WIDE), BF),
            jax.ShapeDtypeStruct((CHIPS, INNER * 32, HD), BF),
        ),
        in_specs=[smem(), smem(), smem(), smem(), vmem(), vmem()],
        out_specs=(vmem(), vmem()),
        scratch_shapes=[
            pltpu.VMEM((4 * SEG, HD), BF),
            pltpu.VMEM((4 * SEG, HD), BF),
            pltpu.VMEM((4 * SEG, SEG), F32),
            pltpu.VMEM((CHIPS, INNER * 32, HD), F32),
        ],
        compiler_params=pltpu.CompilerParams(vmem_limit_bytes=48 * 1024 * 1024),
        cost_estimate=pl.CostEstimate(
            flops=2 * 5 * 10 * SEG * 4 * SEG * HD,
            bytes_accessed=6 * 1024 * 1024,
            transcendentals=10 * SEG * 4 * SEG,
        ),
        name="attention",
    )(chip[None], parent, node_of_slot, live_tiles, mine.reshape(2 * SEG, WIDE), far)

    parts = lax.all_to_all(terms, "chip", split_axis=0, concat_axis=0, tiled=True)
    sums = pl.pallas_call(
        sum_kernel,
        out_shape=jax.ShapeDtypeStruct((NODES, 32, HD), BF),
        in_specs=[smem(), vmem()],
        out_specs=vmem(),
        scratch_shapes=[pltpu.VMEM((INNER * 32, HD), BF)],
        name="sum_terms",
    )(node_of_slot, parts)
    sums = sums.reshape(CHIPS * KV_HEADS, 8, HD)
    sums = lax.all_to_all(sums, ALL, split_axis=0, concat_axis=0, tiled=True)
    sums = sums.reshape(2, 8, KV_HEADS, 8, HD).transpose(0, 1, 3, 2, 4)
    sums = sums.reshape(2, rows, KV_HEADS * HD)

    back = lax.all_to_all(
        out.reshape(KV_HEADS, rows, WIDE), GROUP_AXES, split_axis=0, concat_axis=0, tiled=True
    )
    back = back.transpose(1, 0, 2)
    attended = back[:, :, :QW].reshape(rows, KV_HEADS * QW)
    query_grad = back[:, :, QW : 2 * QW].reshape(rows, KV_HEADS * QW)
    own_key = back[:, :, 2 * QW : 2 * QW + HD].reshape(rows, KV_HEADS * HD)
    own_value = back[:, :, 2 * QW + HD :].reshape(rows, KV_HEADS * HD)
    is_inner = node_of_slot[2 * chip + core] < INNER
    key_grad = jnp.where(is_inner, sums[0], own_key)
    value_grad = jnp.where(is_inner, sums[1], own_value)
    return attended, query_grad, key_grad, value_grad


def solution(mesh):
    devices = mesh.devices.reshape(CHIPS, 2, 4)
    inner_mesh = Mesh(devices, ALL)
    split = P(ALL, None)
    return jax.shard_map(
        on_device,
        mesh=inner_mesh,
        in_specs=(split, split, split, split, P(), P(), P()),
        out_specs=(split, split, split, split),
        check_vma=False,
    )
```

time: 313 us -> 154 us (0.49); the launches traced: 308 us -> 153 us
  waiting for transfers between devices: 129 us -> 63.3 us
  local copies, waits for them, and re-layouts: 65.6 us -> 2.88 us
  matrix products: 43.3 us -> 0 us
  blocking collectives: 8.35 us -> 42.6 us
  Pallas kernels: 0 us -> 23.2 us
  between operations: 17.8 us -> 1.41 us
  other arithmetic: 15.9 us -> 3.06 us
  starting transfers between devices: 28.2 us -> 16.2 us
    reduce_scatter x1 -> x0, waiting for transfers between devices: 92.1 us -> none  [on_device(): lax.psum_scatter(jnp.einsum('ka,asc->ksc', pick, terms, precision=lax.Pre...]
    all_to_all x7 -> x4, waiting for transfers between devices: 19.8 us -> 63.3 us  [the longest x1 20.9 us: on_device(): lax.all_to_all(mine, GROUP_AXES, split_axis=0, concat_axis=0, tiled=True)]
    dot_general x7 -> x0, matrix products: 43.3 us -> none  [the longest x1 17.6 us: on_device(): jnp.einsum('ka,asc->ksc', pick, terms, precision=lax.Precision.HIGHEST)]
    all_to_all x1 -> x2, blocking collectives: 8.35 us -> 42.6 us  [the longest x1 21.6 us: on_device(): lax.all_to_all(pieces, ALL, split_axis=0, concat_axis=0, tiled=True)]
    pallas_call x0 -> x3, Pallas kernels: none -> 23.2 us  [the longest x1 18.4 us: on_device(): pl.pallas_call(attention_kernel, out_shape=(jax.ShapeDtypeStruct((2 * SEG...]
    dot_general x2 -> x0, local copies, waits for them, and re-layouts: 20.2 us -> none  [the longest x1 19.1 us: on_device(): jnp.einsum('ka,asc->ksc', pick, terms, precision=lax.Precision.HIGHEST)]
    all_gather x1 -> x0, waiting for transfers between devices: 17.2 us -> none  [on_device(): lax.all_gather(paired, 'node', axis=0, tiled=True)]
    all_to_all x10 -> x0, local copies, waits for them, and re-layouts: 12.6 us -> none  [the longest x2 2.44 us: on_device(): lax.all_to_all(attended, 'head', split_axis=0, concat_axis=1, tiled=True)]
  transfers between devices with their start and end apart: 9 -> 4, of which waited for: 7 -> 4; matrix products, arithmetic and copies ran while one was open for 11% -> 3% of each run, Pallas kernels for 0% -> 2%
where the time goes in v1:
time: 154 us; the launch traced here: 153 us
  waiting for transfers between devices  63.3 us (41%)
  blocking collectives  42.6 us (28%)
  Pallas kernels  23.2 us (15%)
  starting transfers between devices  16.2 us (11%)
  other arithmetic  3.06 us (2%)
  local copies, waits for them, and re-layouts  2.88 us (2%)
    all_to_all x1, blocking collectives, on_device(): lax.all_to_all(pieces, ALL, split_axis=0, concat_axis=0, tiled=True)  21.6 us
    all_to_all x1, blocking collectives, on_device(): lax.all_to_all(terms, 'chip', split_axis=0, concat_axis=0, tiled=True)  21 us
    all_to_all x1, waiting for transfers between devices, on_device(): lax.all_to_all(mine, GROUP_AXES, split_axis=0, concat_axis=0, tiled=True)  20.9 us
    pallas_call x1, Pallas kernels, on_device(): pl.pallas_call(attention_kernel, out_shape=(jax.ShapeDtypeStruct((2 * SEG...  18.4 us
    all_to_all x1, waiting for transfers between devices, on_device(): lax.all_to_all(out.reshape(KV_HEADS, rows, WIDE), GROUP_AXES, split_axis=...  17.2 us
    all_to_all x1, waiting for transfers between devices, on_device(): far = lax.all_to_all(inner, 'chip', split_axis=0, concat_axis=0, tiled=True)  16.7 us
    all_to_all x1, waiting for transfers between devices, on_device(): sums = lax.all_to_all(sums, ALL, split_axis=0, concat_axis=0, tiled=True)  8.46 us
    all_to_all x1, starting transfers between devices, on_device(): sums = lax.all_to_all(sums, ALL, split_axis=0, concat_axis=0, tiled=True)  5.21 us
  transfers between devices with their start and end apart: 4, of which 4 were waited for; matrix products, arithmetic and copies ran while one was open for 3% of the time, Pallas kernels for 2%

profile of v1, /device:TPU:0, one launch (start us, length us, event | category | flops | bytes accessed | tf_op | source)
XLA Modules:
  0.0 152.6 jit_solution(6538034513460181662)
XLA Ops:
  0.6 1.0 pad_maximum_fusion.1
  1.6 21.6 %all_to_all.30 = bf16[128,8,128]{2,1,0:T(8,128)(2,1)} all-to-all(bf16[128,8,128]{2,1,0:T(8,128)(2,1)S(1)} %bitcast.66), channel_id=1, replica_groups=mesh['chip'=16,'core'=2,'head'=4] {'chip','core','head'}, dimensions={0} | all-to-all | bytes 524288 | tf_op jit(solution)/shard_map/all_to_all | solution.py:161
  23.2 2.4 %select_inner.1 = bf16[16,256,128]{2,1,0:T(8,128)(2,1)} custom-call(s32[32]{0:T(128)} %node_of_slot.5, bf16[32,32,128]{2,1,0:T(8,128)(2,1)} %bitcast.65), custom_call_target="tpu_custom_call" | custom-call | tf_op jit(solution)/shard_map/select_inner/pallas_call | solution.py:162
  25.6 3.8 %all-to-all-start.2 = ((bf16[16,256,128]{2,1,0:T(8,128)(2,1)}), bf16[16,256,128]{2,1,0:T(8,128)(2,1)S(1)}, u32[]{:S(2)}, u32[]{:S(2)}) async-start(bf16[16,256,128]{2,1,0:T(8,128)(2,1)} %select_inner.1), calls=%async_computation.2 | async-start | bytes 2097152 | tf_op jit(solution)/shard_map/all_to_all | solution.py:169
  29.4 0.0 copy-done.5
  29.5 0.1 bitcast_bitcast_fusion.2
  29.5 0.2 bitcast_bitcast_fusion
  29.7 1.3 pad_maximum_fusion
  31.1 16.7 %all-to-all-done.2.far = bf16[16,256,128]{2,1,0:T(8,128)(2,1)S(1)} async-done(((bf16[16,256,128]{2,1,0:T(8,128)(2,1)}), bf16[16,256,128]{2,1,0:T(8,128)(2,1)S(1)}, u32[]{:S(2)}, u32[]{:S(2)}) %all-to-all-start.2) | async-done | bytes 1048608 | tf_op jit(solution)/shard_map/all_to_all | solution.py:169
  47.8 3.6 %all-to-all-start = ((bf16[8,64,1536]{2,1,0:T(8,128)(2,1)}), bf16[8,64,1536]{2,1,0:T(8,128)(2,1)S(1)}, u32[]{:S(2)}, u32[]{:S(2)}) async-start(bf16[8,64,1536]{2,1,0:T(8,128)(2,1)} %pad_maximum_fusion), calls=%async_computation | async-start | bytes 3145728 | tf_op jit(solution)/shard_map/all_to_all | solution.py:177
  51.4 20.9 %all-to-all-done = bf16[8,64,1536]{2,1,0:T(8,128)(2,1)S(1)} async-done(((bf16[8,64,1536]{2,1,0:T(8,128)(2,1)}), bf16[8,64,1536]{2,1,0:T(8,128)(2,1)S(1)}, u32[]{:S(2)}, u32[]{:S(2)}) %all-to-all-start) | async-done | bytes 1572896 | tf_op jit(solution)/shard_map/all_to_all | solution.py:177
  72.3 18.4 %attention.1 = (bf16[512,1536]{1,0:T(8,128)(2,1)}, bf16[16,256,128]{2,1,0:T(8,128)(2,1)S(1)}) custom-call(s32[1]{0:T(128)} %bitcast.chip, s32[32]{0:T(128)S(1)} %copy-done.1, s32[32]{0:T(128)S(1)} %copy-done, s32[32]{0:T(128)S(1)} %copy-done.2, bf16[512,1536]{1,0:T(8,128)(2,1)S(1)} %bitcast.61, bf16[16,256,128]{2,1,0:T(8,128)(2,1)S(1)} %all-to-all-done.2.far), custom_call_target="tpu_custom_call" | custom-call | flops 3355443200 | bytes 6291456 | tf_op jit(solution)/shard_map/attention/pallas_call | solution.py:179
  90.7 21.0 %all_to_all.31.parts = bf16[16,256,128]{2,1,0:T(8,128)(2,1)} all-to-all(bf16[16,256,128]{2,1,0:T(8,128)(2,1)S(1)} %get-tuple-element.7), channel_id=1, replica_groups=mesh['chip'=16,'core'=2,'head'=4] {'chip'}, dimensions={0} | all-to-all | bytes 2097152 | tf_op jit(solution)/shard_map/all_to_all | solution.py:202
  111.7 3.6 %all-to-all-start.3 = ((bf16[8,64,1536]{2,1,0:T(8,128)(2,1)}), bf16[8,64,1536]{2,1,0:T(8,128)(2,1)S(1)}, u32[]{:S(2)}, u32[]{:S(2)}) async-start(bf16[8,64,1536]{2,1,0:T(8,128)(2,1)} %bitcast.10), calls=%async_computation.3 | async-start | bytes 3145728 | tf_op jit(solution)/shard_map/all_to_all | solution.py:216
  115.2 0.6 dynamic_slice.3
  116.5 2.5 %sum_terms.1 = bf16[32,32,128]{2,1,0:T(8,128)(2,1)} custom-call(s32[32]{0:T(128)} %node_of_slot.5, bf16[16,256,128]{2,1,0:T(8,128)(2,1)} %all_to_all.31.parts), custom_call_target="tpu_custom_call" | custom-call | tf_op jit(solution)/shard_map/sum_terms/pallas_call | solution.py:203
  118.9 17.2 %all-to-all-done.3 = bf16[8,64,1536]{2,1,0:T(8,128)(2,1)S(1)} async-done(((bf16[8,64,1536]{2,1,0:T(8,128)(2,1)}), bf16[8,64,1536]{2,1,0:T(8,128)(2,1)S(1)}, u32[]{:S(2)}, u32[]{:S(2)}) %all-to-all-start.3) | async-done | bytes 1572896 | tf_op jit(solution)/shard_map/all_to_all | solution.py:216
  136.1 5.2 %all-to-all-start.5 = ((bf16[128,8,128]{2,1,0:T(8,128)(2,1)}), bf16[128,8,128]{2,1,0:T(8,128)(2,1)S(1)}, u32[]{:S(2)}, u32[]{:S(2)}) async-start(bf16[128,8,128]{2,1,0:T(8,128)(2,1)} %bitcast.64), calls=%async_computation.5 | async-start | bytes 524288 | tf_op jit(solution)/shard_map/all_to_all | solution.py:212
  141.3 0.2 slice_bitcast_fusion
  141.5 0.9 copy.24
  142.4 0.9 copy.23
  143.3 0.1 slice_bitcast_fusion.2
  143.4 8.5 %all-to-all-done.5 = bf16[128,8,128]{2,1,0:T(8,128)(2,1)S(1)} async-done(((bf16[128,8,128]{2,1,0:T(8,128)(2,1)}), bf16[128,8,128]{2,1,0:T(8,128)(2,1)S(1)}, u32[]{:S(2)}, u32[]{:S(2)}) %all-to-all-start.5) | async-done | bytes 262176 | tf_op jit(solution)/shard_map/all_to_all | solution.py:212
  151.9 0.7 bitcast_select_fusion
  (13 shorter events, 0.0 us)
Async XLA Ops:
  23.2 6.2 %copy-start.5 = (bf16[64,1024]{1,0:T(8,128)(2,1)S(1)}, bf16[64,1024]{1,0:T(8,128)(2,1)}, u32[]{:S(2)}) copy-start(bf16[64,1024]{1,0:T(8,128)(2,1)} %param.8) | copy-start | bytes 393220
  23.2 6.3 %copy-start.6 = (bf16[64,1024]{1,0:T(8,128)(2,1)S(1)}, bf16[64,1024]{1,0:T(8,128)(2,1)}, u32[]{:S(2)}) copy-start(bf16[64,1024]{1,0:T(8,128)(2,1)} %param.9) | copy-start | bytes 393220
  25.6 3.9 %copy-start.3 = (bf16[64,5120]{1,0:T(8,128)(2,1)S(1)}, bf16[64,5120]{1,0:T(8,128)(2,1)}, u32[]{:S(2)}) copy-start(bf16[64,5120]{1,0:T(8,128)(2,1)} %param.10) | copy-start | bytes 1966084
  25.6 4.0 %copy-start.4 = (bf16[64,5120]{1,0:T(8,128)(2,1)S(1)}, bf16[64,5120]{1,0:T(8,128)(2,1)}, u32[]{:S(2)}) copy-start(bf16[64,5120]{1,0:T(8,128)(2,1)} %param.7) | copy-start | bytes 1966084
  25.6 22.2 %all-to-all-start.2 = ((bf16[16,256,128]{2,1,0:T(8,128)(2,1)}), bf16[16,256,128]{2,1,0:T(8,128)(2,1)S(1)}, u32[]{:S(2)}, u32[]{:S(2)}) async-start(bf16[16,256,128]{2,1,0:T(8,128)(2,1)} %select_inner.1), calls=%async_computation.2 | async-start | bytes 2097152 | tf_op jit(solution)/shard_map/all_to_all | solution.py:169
  31.0 41.2 %copy-start = (s32[32]{0:T(128)S(1)}, s32[32]{0:T(128)}, u32[]{:S(2)}) copy-start(s32[32]{0:T(128)} %node_of_slot.5) | copy-start | bytes 388
  31.1 41.2 %copy-start.1 = (s32[32]{0:T(128)S(1)}, s32[32]{0:T(128)}, u32[]{:S(2)}) copy-start(s32[32]{0:T(128)} %parent.1) | copy-start | bytes 388
  31.1 41.2 %copy-start.2 = (s32[32]{0:T(128)S(1)}, s32[32]{0:T(128)}, u32[]{:S(2)}) copy-start(s32[32]{0:T(128)} %live_tiles.1) | copy-start | bytes 388
  47.8 24.5 %all-to-all-start = ((bf16[8,64,1536]{2,1,0:T(8,128)(2,1)}), bf16[8,64,1536]{2,1,0:T(8,128)(2,1)S(1)}, u32[]{:S(2)}, u32[]{:S(2)}) async-start(bf16[8,64,1536]{2,1,0:T(8,128)(2,1)} %pad_maximum_fusion), calls=%async_computation | async-start | bytes 3145728 | tf_op jit(solution)/shard_map/all_to_all | solution.py:177
  111.7 24.5 %all-to-all-start.3 = ((bf16[8,64,1536]{2,1,0:T(8,128)(2,1)}), bf16[8,64,1536]{2,1,0:T(8,128)(2,1)S(1)}, u32[]{:S(2)}, u32[]{:S(2)}) async-start(bf16[8,64,1536]{2,1,0:T(8,128)(2,1)} %bitcast.10), calls=%async_computation.3 | async-start | bytes 3145728 | tf_op jit(solution)/shard_map/all_to_all | solution.py:216
  136.1 15.7 %all-to-all-start.5 = ((bf16[128,8,128]{2,1,0:T(8,128)(2,1)}), bf16[128,8,128]{2,1,0:T(8,128)(2,1)S(1)}, u32[]{:S(2)}, u32[]{:S(2)}) async-start(bf16[128,8,128]{2,1,0:T(8,128)(2,1)} %bitcast.64), calls=%async_computation.5 | async-start | bytes 524288 | tf_op jit(solution)/shard_map/all_to_all | solution.py:212

commit v2 on v1

v2 whole, which is shorter than its diff:
```python
import functools

import jax
import jax.numpy as jnp
from jax import lax
from jax.experimental import pallas as pl
from jax.experimental.pallas import tpu as pltpu
from jax.sharding import Mesh
from jax.sharding import PartitionSpec as P

HD = 128
TILE = 128
SEG = 256
GROUP = 5
KV_HEADS = 8
INNER = 8
NODES = 32
CHIPS = 16
QW = GROUP * HD
WIDE = 2 * QW + 2 * HD
SCALE = HD ** (-0.5)
BF = jnp.bfloat16
F32 = jnp.float32
MIB = 1024 * 1024
LOG2_E = 1.4426950408889634

PARENT, NODE_OF_SLOT, LIVE_TILES, PLACE = 0, 32, 64, 96

ALL = ("chip", "core", "head")
GROUP_AXES = ("core", "head")


def smem():
    return pl.BlockSpec(memory_space=pltpu.SMEM)


def vmem():
    return pl.BlockSpec(memory_space=pltpu.VMEM)


def nt_dot(left, right):
    return lax.dot_general(left, right, (((1,), (1,)), ((), ())), preferred_element_type=F32)


def nn_dot(left, right):
    return lax.dot_general(left, right, (((1,), (0,)), ((), ())), preferred_element_type=F32)


def select_kernel(info, pieces, out):
    for slot in range(NODES):
        node = info[NODE_OF_SLOT + slot]

        @pl.when(node < INNER)
        def _():
            row = pl.multiple_of(node * 32, 32)
            block = pieces[slot]
            for chip in range(CHIPS):
                out[chip, pl.ds(row, 32), :] = block


SHIFTS = (0, 2, 1, 3)
PIECES = [(dc, dx) for dc in range(2) for dx in SHIFTS]


def group_index(info, dc, dx):
    return lax.rem(info[PLACE + 1] + dc, 2) * 4 + lax.rem(info[PLACE + 2] + dx, 4)


def pack_kernel(info, queries, out_grad, keys, values, *outs):
    for (dc, dx), out in zip(PIECES, outs):
        peer = group_index(info, dc, dx)
        wide = pl.ds(pl.multiple_of(peer * QW, HD), QW)
        narrow = pl.ds(pl.multiple_of(peer * HD, HD), HD)
        out[:, 0:QW] = queries[:, wide]
        out[:, QW : 2 * QW] = out_grad[:, wide]
        out[:, 2 * QW : 2 * QW + HD] = keys[:, narrow]
        out[:, 2 * QW + HD : WIDE] = values[:, narrow]


def unpack_kernel(info, *refs):
    pieces, (attended, query_grad, own_key, own_value) = refs[:8], refs[8:]
    for (dc, dx), piece in zip(PIECES, pieces):
        peer = group_index(info, 2 - dc, 4 - dx)
        wide = pl.ds(pl.multiple_of(peer * QW, HD), QW)
        narrow = pl.ds(pl.multiple_of(peer * HD, HD), HD)
        attended[:, wide] = piece[:, 0:QW]
        query_grad[:, wide] = piece[:, QW : 2 * QW]
        own_key[:, narrow] = piece[:, 2 * QW : 2 * QW + HD]
        own_value[:, narrow] = piece[:, 2 * QW + HD : WIDE]


def exchange(pieces, shifts):
    moved = []
    for (dc, dx), piece in zip(shifts, pieces):
        if dc or dx:
            pairs = [
                (4 * c + x, 4 * ((c + dc) % 2) + (x + dx) % 4) for c in range(2) for x in range(4)
            ]
            piece = lax.ppermute(piece, GROUP_AXES, pairs)
        moved.append(piece)
    return moved


def copy_all(sources, targets, sems):
    copies = [
        pltpu.make_async_copy(source, target, sems.at[n])
        for n, (source, target) in enumerate(zip(sources, targets))
    ]
    for copy in copies:
        copy.start()
    return copies


def attention_kernel(dc, info, far, *refs):
    arrived, refs = refs[:4], refs[4:]
    if dc == 0:
        leaving, key_out, value_out, refs = refs[:4], refs[4], refs[5], refs[6:]
    else:
        first_key, first_value, leaving, terms, refs = refs[0], refs[1], refs[2:6], refs[6], refs[7:]
    mine, out, key_all, value_all, bias, probs_all, dscores_all, sems = refs[:8]
    quarters = [
        pl.ds(pl.multiple_of(lax.rem(info[PLACE + 2] + 4 - dx, 4) * 64, 64), 64) for dx in SHIFTS
    ]
    copies = copy_all(arrived, [mine.at[quarter, :] for quarter in quarters], sems)
    row = lax.broadcasted_iota(jnp.int32, (SEG, SEG), 0)
    token = lax.broadcasted_iota(jnp.int32, (SEG, SEG), 1)
    bias[:, 0:SEG] = jnp.where(token <= row, 0.0, -jnp.inf)
    tile = lax.rem(token, 32) // 16

    def lineage(which):
        me = info[NODE_OF_SLOT + 2 * info[PLACE] + lax.rem(info[PLACE + 1] + which, 2)]
        chain = [me]
        for _ in range(3):
            current = chain[-1]
            chain.append(jnp.where(current >= 0, info[PARENT + jnp.maximum(current, 0)], -1))
        return chain

    for step, node in enumerate(lineage(dc)[1:], 1):
        safe = jnp.maximum(node, 0)
        live = jnp.where(node >= 0, info[LIVE_TILES + safe], 0)
        rows = pl.ds(pl.multiple_of(safe * 32, 32), 32)
        here = slice(step * SEG, (step + 1) * SEG)
        key_all[here, :] = far[0:8, rows, :].reshape(SEG, HD)
        value_all[here, :] = far[8:16, rows, :].reshape(SEG, HD)
        bias[:, here] = jnp.where(tile < live, 0.0, -jnp.inf)
    for copy in copies:
        copy.wait()
    key_all[0:SEG, :] = mine[:, 2 * QW : 2 * QW + HD]
    value_all[0:SEG, :] = mine[:, 2 * QW + HD : WIDE]

    keys = key_all[...]
    values = value_all[...]
    queries_t = []
    grads_t = []
    for g in range(GROUP):
        columns = slice(g * HD, (g + 1) * HD)
        grad_columns = slice(QW + g * HD, QW + (g + 1) * HD)
        query = mine[:, columns]
        grad = mine[:, grad_columns]
        queries_t.append(query.T)
        grads_t.append(grad.T)
        scores = nt_dot(query, keys) * (SCALE * LOG2_E) + bias[...]
        peak = jnp.max(scores, axis=1, keepdims=True)
        weight = jnp.exp2(scores - peak)
        total = jnp.sum(weight, axis=1, keepdims=True)
        probs = weight * (1.0 / total)
        probs_b = probs.astype(BF)
        attended = nn_dot(probs_b, values).astype(BF)
        out[:, columns] = attended
        delta = jnp.sum(grad.astype(F32) * attended.astype(F32), axis=1, keepdims=True)
        dprobs = nt_dot(grad, values)
        dscores = (probs * (dprobs - delta)).astype(BF)
        query_grad = nn_dot(dscores, keys) * SCALE
        out[:, grad_columns] = query_grad.astype(BF)
        probs_all[g * SEG : (g + 1) * SEG, :] = probs_b
        dscores_all[g * SEG : (g + 1) * SEG, :] = dscores
    key_terms = nn_dot(jnp.concatenate(queries_t, 1), dscores_all[...]).T * SCALE
    value_terms = nn_dot(jnp.concatenate(grads_t, 1), probs_all[...]).T
    out[:, 2 * QW : 2 * QW + HD] = key_terms[0:SEG].astype(BF)
    out[:, 2 * QW + HD : WIDE] = value_terms[0:SEG].astype(BF)
    quarters = [
        pl.ds(pl.multiple_of(lax.rem(info[PLACE + 2] + dx, 4) * 64, 64), 64) for dx in SHIFTS
    ]
    copies = copy_all([out.at[quarter, :] for quarter in quarters], leaving, sems)

    if dc == 0:
        key_out[...] = key_terms
        value_out[...] = value_terms
    else:
        acc = refs[8]
        acc[...] = jnp.zeros_like(acc)
        for chain, key_part, value_part in (
            (lineage(0), first_key, first_value),
            (lineage(1), key_terms, value_terms),
        ):
            for step in range(1, 4):
                rows = pl.ds(pl.multiple_of(jnp.maximum(chain[step], 0) * 32, 32), 32)
                here = slice(step * SEG, (step + 1) * SEG)
                acc[0:8, rows, :] += key_part[here].reshape(8, 32, HD)
                acc[8:16, rows, :] += value_part[here].reshape(8, 32, HD)

            @pl.when(chain[0] < INNER)
            def _():
                for piece in range(8):
                    for quarter in range(4):
                        first = quarter * 64 + piece * 8
                        rows = pl.ds(pl.multiple_of(chain[0] * 32 + quarter * 8, 8), 8)
                        acc[piece, rows, :] += key_part[first : first + 8]
                        acc[8 + piece, rows, :] += value_part[first : first + 8]

        terms[...] = acc[...].astype(BF)
    for copy in copies:
        copy.wait()


def sum_kernel(info, parts, out, total):
    sums = parts[0].astype(F32)
    for chip in range(1, CHIPS):
        sums = sums + parts[chip].astype(F32)
    total[...] = sums.astype(BF)
    for slot in range(NODES):
        node = info[NODE_OF_SLOT + slot]

        @pl.when(node < INNER)
        def _():
            out[slot] = total[pl.ds(pl.multiple_of(node * 32, 32), 32), :]

        @pl.when(node >= INNER)
        def _():
            out[slot] = jnp.zeros((32, HD), BF)


def on_device(queries, keys, values, out_grad, parent, node_of_slot, live_tiles):
    rows = queries.shape[0]
    chip = lax.axis_index("chip")
    core = lax.axis_index("core")
    place = jnp.stack([chip, core, lax.axis_index("head"), 0]).astype(jnp.int32)
    info = jnp.concatenate([parent, node_of_slot, live_tiles, place])

    pieces = jnp.concatenate([keys, values], 0).reshape(16, 8, KV_HEADS, HD)
    pieces = pieces.transpose(0, 2, 1, 3).reshape(CHIPS * KV_HEADS, 8, HD)
    pieces = lax.all_to_all(pieces, ALL, split_axis=0, concat_axis=0, tiled=True)
    piece_shape = jax.ShapeDtypeStruct((rows, WIDE), BF)
    packed = pl.pallas_call(
        pack_kernel,
        out_shape=(piece_shape,) * 8,
        in_specs=[smem()] + [vmem()] * 4,
        out_specs=(vmem(),) * 8,
        compiler_params=pltpu.CompilerParams(vmem_limit_bytes=8 * MIB),
        name="pack",
    )(info, queries, out_grad, keys, values)
    pieces, packed = lax.optimization_barrier((pieces, packed))
    inner = pl.pallas_call(
        select_kernel,
        out_shape=jax.ShapeDtypeStruct((CHIPS, INNER * 32, HD), BF),
        in_specs=[smem(), vmem()],
        out_specs=vmem(),
        compiler_params=pltpu.CompilerParams(vmem_limit_bytes=6 * MIB),
        name="select_inner",
    )(info, pieces.reshape(NODES, 32, HD))
    far = lax.all_to_all(inner, "chip", split_axis=0, concat_axis=0, tiled=True)
    arrived = exchange(packed, PIECES)

    any_memory = pl.BlockSpec(memory_space=pl.ANY)
    half = jax.ShapeDtypeStruct((4 * SEG, HD), F32)

    def attend(dc, operands):
        last = dc == 1
        out_shape = (piece_shape,) * 4
        out_specs = (any_memory,) * 4
        scratch_shapes = [
            pltpu.VMEM((SEG, WIDE), BF),
            pltpu.VMEM((SEG, WIDE), BF),
            pltpu.VMEM((4 * SEG, HD), BF),
            pltpu.VMEM((4 * SEG, HD), BF),
            pltpu.VMEM((SEG, 4 * SEG), F32),
            pltpu.VMEM((GROUP * SEG, 4 * SEG), BF),
            pltpu.VMEM((GROUP * SEG, 4 * SEG), BF),
            pltpu.SemaphoreType.DMA((4,)),
        ]
        if last:
            out_shape += (jax.ShapeDtypeStruct((CHIPS, INNER * 32, HD), BF),)
            out_specs += (vmem(),)
            scratch_shapes.append(pltpu.VMEM((CHIPS, INNER * 32, HD), F32))
        else:
            out_shape += (half, half)
            out_specs += (vmem(), vmem())
        return pl.pallas_call(
            functools.partial(attention_kernel, dc),
            out_shape=out_shape,
            in_specs=[smem(), vmem()] + [any_memory] * 4 + [vmem()] * (2 if last else 0),
            out_specs=out_specs,
            scratch_shapes=scratch_shapes,
            compiler_params=pltpu.CompilerParams(vmem_limit_bytes=28 * MIB),
            cost_estimate=pl.CostEstimate(
                flops=2 * 5 * GROUP * SEG * 4 * SEG * HD * 4,
                bytes_accessed=6 * 1024 * 1024,
                transcendentals=GROUP * SEG * 4 * SEG,
            ),
            name="attention",
        )(info, far, *operands)

    *leaving, first_key, first_value = attend(0, arrived[:4])
    *others, terms = attend(1, arrived[4:] + [first_key, first_value])
    first_back = exchange(leaving, PIECES[:4])
    terms, first_back = lax.optimization_barrier((terms, first_back))

    parts = lax.all_to_all(terms, "chip", split_axis=0, concat_axis=0, tiled=True)
    back = first_back + exchange(others, PIECES[4:])
    parts, back = lax.optimization_barrier((parts, back))
    sums = pl.pallas_call(
        sum_kernel,
        out_shape=jax.ShapeDtypeStruct((NODES, 32, HD), BF),
        in_specs=[smem(), vmem()],
        out_specs=vmem(),
        scratch_shapes=[pltpu.VMEM((INNER * 32, HD), BF)],
        compiler_params=pltpu.CompilerParams(vmem_limit_bytes=6 * MIB),
        name="sum_terms",
    )(info, parts)
    sums = sums.reshape(CHIPS * KV_HEADS, 8, HD)
    sums = lax.all_to_all(sums, ALL, split_axis=0, concat_axis=0, tiled=True)

    wide_shape = jax.ShapeDtypeStruct((rows, KV_HEADS * QW), BF)
    narrow_shape = jax.ShapeDtypeStruct((rows, KV_HEADS * HD), BF)
    attended, query_grad, own_key, own_value = pl.pallas_call(
        unpack_kernel,
        out_shape=(wide_shape, wide_shape, narrow_shape, narrow_shape),
        in_specs=[smem()] + [vmem()] * 8,
        out_specs=(vmem(),) * 4,
        compiler_params=pltpu.CompilerParams(vmem_limit_bytes=8 * MIB),
        name="unpack",
    )(info, *back)
    sums, attended, query_grad, own_key, own_value = lax.optimization_barrier(
        (sums, attended, query_grad, own_key, own_value)
    )
    sums = sums.reshape(2, 8, KV_HEADS, 8, HD).transpose(0, 1, 3, 2, 4)
    sums = sums.reshape(2, rows, KV_HEADS * HD)
    is_inner = node_of_slot[2 * chip + core] < INNER
    key_grad = jnp.where(is_inner, sums[0], own_key)
    value_grad = jnp.where(is_inner, sums[1], own_value)
    return attended, query_grad, key_grad, value_grad


def solution(mesh):
    devices = mesh.devices.reshape(CHIPS, 2, 4)
    inner_mesh = Mesh(devices, ALL)
    split = P(ALL, None)
    return jax.shard_map(
        on_device,
        mesh=inner_mesh,
        in_specs=(split, split, split, split, P(), P(), P()),
        out_specs=(split, split, split, split),
        check_vma=False,
    )
```

time: 154 us -> 114 us (0.74)
  blocking collectives: 42.6 us -> 0 us
  waiting for transfers between devices: 63.3 us -> 40.2 us
  starting transfers between devices: 16.2 us -> 38.1 us
  local copies, waits for them, and re-layouts: 2.88 us -> 6.31 us
    all_to_all x2 -> x0, blocking collectives: 42.6 us -> none  [the longest x1 21.6 us: on_device(): lax.all_to_all(pieces, ALL, split_axis=0, concat_axis=0, tiled=True)]
    all_to_all x2, waiting for transfers between devices: 38.1 us -> 12.7 us  [the longest x1 7.93 us: on_device(): lax.all_to_all(pieces, ALL, split_axis=0, concat_axis=0, tiled=True)]
    ppermute x0 -> x14, waiting for transfers between devices: none -> 16.5 us  [exchange(): piece = lax.ppermute(piece, GROUP_AXES, pairs)]
    ppermute x0 -> x14, starting transfers between devices: none -> 14.2 us  [exchange(): piece = lax.ppermute(piece, GROUP_AXES, pairs)]
    all_to_all x1, waiting for transfers between devices: 16.7 us -> 3.5 us  [on_device(): far = lax.all_to_all(inner, 'chip', split_axis=0, concat_axis=0, tiled=True)]
    all_to_all x2, starting transfers between devices: 7.16 us -> 15.5 us  [the longest x1 11.1 us: on_device(): lax.all_to_all(pieces, ALL, split_axis=0, concat_axis=0, tiled=True)]
    unnamed x16 -> x26, local copies, waits for them, and re-layouts: 0.26 us -> 5.64 us
    reshape x2 -> x0, local copies, waits for them, and re-layouts: 1.8 us -> none  [the longest x1 0.9 us: on_device(): query_grad = back[:, :, QW:2 * QW].reshape(rows, KV_HEADS * QW)]
  transfers between devices with their start and end apart: 4 -> 18, of which waited for: 4 -> 8; matrix products, arithmetic and copies ran while one was open for 3% -> 1% of each run, Pallas kernels for 2% -> 18%
where the time goes in v2:
time: 114 us; the launch traced here: 112 us
  waiting for transfers between devices  40.2 us (35%)
  starting transfers between devices  38.1 us (33%)
  Pallas kernels  23.5 us (21%)
  local copies, waits for them, and re-layouts  6.31 us (6%)
  other arithmetic  2.48 us (2%)
  between operations  1.46 us (1%)
    pallas_call x2, Pallas kernels, attend(): pl.pallas_call(functools.partial(attention_kernel, dc), out_shape=out_sha...  17.3 us
    ppermute x14, waiting for transfers between devices, exchange(): piece = lax.ppermute(piece, GROUP_AXES, pairs)  16.5 us
    ppermute x14, starting transfers between devices, exchange(): piece = lax.ppermute(piece, GROUP_AXES, pairs)  14.2 us
    all_to_all x1, starting transfers between devices, on_device(): lax.all_to_all(pieces, ALL, split_axis=0, concat_axis=0, tiled=True)  11.1 us
    all_to_all x1, waiting for transfers between devices, on_device(): lax.all_to_all(pieces, ALL, split_axis=0, concat_axis=0, tiled=True)  7.93 us
    all_to_all x1, waiting for transfers between devices, on_device(): sums = lax.all_to_all(sums, ALL, split_axis=0, concat_axis=0, tiled=True)  7.5 us
    unnamed x26, local copies, waits for them, and re-layouts  5.64 us
    all_to_all x1, waiting for transfers between devices, on_device(): lax.all_to_all(terms, 'chip', split_axis=0, concat_axis=0, tiled=True)  4.75 us
  transfers between devices with their start and end apart: 18, of which 8 were waited for; matrix products, arithmetic and copies ran while one was open for 1% of the time, Pallas kernels for 18%

profile of v2, /device:TPU:0, one launch (start us, length us, event | category | flops | bytes accessed | tf_op | source)
XLA Modules:
  0.0 112.0 jit_solution(8174717315972879209)
XLA Ops:
  0.6 1.8 %pad_maximum_fusion = bf16[128,1024]{1,0:T(8,128)(2,1)} fusion(bf16[64,1024]{1,0:T(8,128)(2,1)} %values.1, bf16[64,1024]{1,0:T(8,128)(2,1)} %keys.1), kind=kLoop, calls=%fused_computation | loop fusion | flops 524288 | bytes 524288 | tf_op jit(solution)/shard_map/concatenate | solution.py:240
  2.4 11.1 %all-to-all-start = ((bf16[128,8,128]{2,1,0:T(8,128)(2,1)}), bf16[128,8,128]{2,1,0:T(8,128)(2,1)S(1)}, u32[]{:S(2)}, u32[]{:S(2)}) async-start(bf16[128,8,128]{2,1,0:T(8,128)(2,1)} %bitcast.5), calls=%async_computation | async-start | bytes 524288 | tf_op jit(solution)/shard_map/all_to_all | solution.py:242
  16.1 7.9 %all-to-all-done = bf16[128,8,128]{2,1,0:T(8,128)(2,1)S(1)} async-done(((bf16[128,8,128]{2,1,0:T(8,128)(2,1)}), bf16[128,8,128]{2,1,0:T(8,128)(2,1)S(1)}, u32[]{:S(2)}, u32[]{:S(2)}) %all-to-all-start) | async-done | bytes 262176 | tf_op jit(solution)/shard_map/all_to_all | solution.py:242
  24.1 1.9 %select_inner.1 = bf16[16,256,128]{2,1,0:T(8,128)(2,1)} custom-call(s32[100]{0:T(128)S(1)} %concatenate.6.info, bf16[32,32,128]{2,1,0:T(8,128)(2,1)S(1)} %bitcast.22), custom_call_target="tpu_custom_call" | custom-call | tf_op jit(solution)/shard_map/select_inner/pallas_call | solution.py:253
  26.0 3.7 %all-to-all-start.1 = ((bf16[16,256,128]{2,1,0:T(8,128)(2,1)}), bf16[16,256,128]{2,1,0:T(8,128)(2,1)S(1)}, u32[]{:S(2)}, u32[]{:S(2)}) async-start(bf16[16,256,128]{2,1,0:T(8,128)(2,1)} %select_inner.1), calls=%async_computation.1 | async-start | bytes 2097152 | tf_op jit(solution)/shard_map/all_to_all | solution.py:261
  29.7 1.3 %collective-permute-start.4 = (bf16[64,1536]{1,0:T(8,128)(2,1)S(1)}, bf16[64,1536]{1,0:T(8,128)(2,1)S(1)}, u32[]{:S(2)}, u32[]{:S(2)}) collective-permute-start(bf16[64,1536]{1,0:T(8,128)(2,1)S(1)} %get-tuple-element.69), channel_id=1, source_target_pairs={{0,2},{1,3},{2,0},{3,1},{4,6},{5,7},{6,4},{7,5},{8,10},{9,11},{10,... | collective-permute-start | bytes 589832 | tf_op jit(solution)/shard_map/ppermute | solution.py:99
  32.2 2.1 %collective-permute-start.6 = (bf16[64,1536]{1,0:T(8,128)(2,1)S(1)}, bf16[64,1536]{1,0:T(8,128)(2,1)S(1)}, u32[]{:S(2)}, u32[]{:S(2)}) collective-permute-start(bf16[64,1536]{1,0:T(8,128)(2,1)S(1)} %get-tuple-element.71), channel_id=1, source_target_pairs={{0,3},{1,0},{2,1},{3,2},{4,7},{5,4},{6,5},{7,6},{8,11},{9,8},{10,9... | collective-permute-start | bytes 589832 | tf_op jit(solution)/shard_map/ppermute | solution.py:99
  34.2 1.2 %collective-permute-start.1 = (bf16[64,1536]{1,0:T(8,128)(2,1)S(1)}, bf16[64,1536]{1,0:T(8,128)(2,1)S(1)}, u32[]{:S(2)}, u32[]{:S(2)}) collective-permute-start(bf16[64,1536]{1,0:T(8,128)(2,1)S(1)} %get-tuple-element.65), channel_id=1, source_target_pairs={{0,6},{1,7},{2,4},{3,5},{4,2},{5,3},{6,0},{7,1},{8,14},{9,15},{10,... | collective-permute-start | bytes 589832 | tf_op jit(solution)/shard_map/ppermute | solution.py:99
  35.5 3.6 %collective-permute-done.4.refs_1_ = bf16[64,1536]{1,0:T(8,128)(2,1)S(1)} collective-permute-done((bf16[64,1536]{1,0:T(8,128)(2,1)S(1)}, bf16[64,1536]{1,0:T(8,128)(2,1)S(1)}, u32[]{:S(2)}, u32[]{:S(2)}) %collective-permute-start.4) | collective-permute-done | bytes 196640 | tf_op jit(solution)/shard_map/ppermute | solution.py:99
  39.1 4.1 %collective-permute-done.5.refs_2_ = bf16[64,1536]{1,0:T(8,128)(2,1)S(1)} collective-permute-done((bf16[64,1536]{1,0:T(8,128)(2,1)S(1)}, bf16[64,1536]{1,0:T(8,128)(2,1)S(1)}, u32[]{:S(2)}, u32[]{:S(2)}) %collective-permute-start.5) | collective-permute-done | bytes 196640 | tf_op jit(solution)/shard_map/ppermute | solution.py:99
  44.6 3.5 %all-to-all-done.1.far = bf16[16,256,128]{2,1,0:T(8,128)(2,1)S(1)} async-done(((bf16[16,256,128]{2,1,0:T(8,128)(2,1)}), bf16[16,256,128]{2,1,0:T(8,128)(2,1)S(1)}, u32[]{:S(2)}, u32[]{:S(2)}) %all-to-all-start.1) | async-done | bytes 1048608 | tf_op jit(solution)/shard_map/all_to_all | solution.py:261
  49.9 8.1 %attention.2 = (bf16[64,1536]{1,0:T(8,128)(2,1)S(1)}, bf16[64,1536]{1,0:T(8,128)(2,1)S(1)}, bf16[64,1536]{1,0:T(8,128)(2,1)S(1)}, bf16[64,1536]{1,0:T(8,128)(2,1...) custom-call(s32[100]{0:T(128)S(1)} %concatenate.6.info, bf16[16,256,128]{2,1,0:T(8,128)(2,1)S(1)} %all-to-all-done.1.far, ...), custom_call_target="tpu_custom_call" | custom-call | flops 6710886400 | bytes 6291456 | tf_op jit(solution)/shard_map/attention/pallas_call | solution.py:288
  60.2 2.1 %collective-permute-start.9 = (bf16[64,1536]{1,0:T(8,128)(2,1)S(1)}, bf16[64,1536]{1,0:T(8,128)(2,1)S(1)}, u32[]{:S(2)}, u32[]{:S(2)}) collective-permute-start(bf16[64,1536]{1,0:T(8,128)(2,1)S(1)} %get-tuple-element.78), channel_id=1, source_target_pairs={{0,3},{1,0},{2,1},{3,2},{4,7},{5,4},{6,5},{7,6},{8,11},{9,8},{10,9... | collective-permute-start | bytes 589832 | tf_op jit(solution)/shard_map/ppermute | solution.py:99
  62.2 9.2 %attention.3 = (bf16[64,1536]{1,0:T(8,128)(2,1)}, bf16[64,1536]{1,0:T(8,128)(2,1)S(1)}, bf16[64,1536]{1,0:T(8,128)(2,1)S(1)}, bf16[64,1536]{1,0:T(8,128)(2,1)S(1)}, bf16[16,256,128]{2,1,0:T(8,128)(2,1)}) custom-call(s32[100]{0:T(128)S(1)} %concatenate.6.info, bf16[16,256,128]{2,1,0:T(8,128)(2,1)S(1)} %all-to-all-done.1.far, ...), custom_call_target="tpu_custom_call" | custom-call | flops 6710886400 | bytes 6291456 | tf_op jit(solution)/shard_map/attention/pallas_call | solution.py:288
  72.2 4.3 %all-to-all-start.2 = ((bf16[16,256,128]{2,1,0:T(8,128)(2,1)}), bf16[16,256,128]{2,1,0:T(8,128)(2,1)S(1)}, u32[]{:S(2)}, u32[]{:S(2)}) async-start(bf16[16,256,128]{2,1,0:T(8,128)(2,1)} %get-tuple-element.79), calls=%async_computation.2 | async-start | bytes 2097152 | tf_op jit(solution)/shard_map/all_to_all | solution.py:308
  76.6 1.2 %collective-permute-start.11 = (bf16[64,1536]{1,0:T(8,128)(2,1)S(1)}, bf16[64,1536]{1,0:T(8,128)(2,1)S(1)}, u32[]{:S(2)}, u32[]{:S(2)}) collective-permute-start(bf16[64,1536]{1,0:T(8,128)(2,1)S(1)} %copy-done.5), channel_id=1, source_target_pairs={{0,6},{1,7},{2,4},{3,5},{4,2},{5,3},{6,0},{7,1},{8,14},{9,15},{10,... | collective-permute-start | bytes 589832 | tf_op jit(solution)/shard_map/ppermute | solution.py:99
  78.9 1.9 %collective-permute-start.13 = (bf16[64,1536]{1,0:T(8,128)(2,1)S(1)}, bf16[64,1536]{1,0:T(8,128)(2,1)S(1)}, u32[]{:S(2)}, u32[]{:S(2)}) collective-permute-start(bf16[64,1536]{1,0:T(8,128)(2,1)S(1)} %get-tuple-element.87), channel_id=1, source_target_pairs={{0,7},{1,4},{2,5},{3,6},{4,3},{5,0},{6,1},{7,2},{8,15},{9,12},{10,... | collective-permute-start | bytes 589832 | tf_op jit(solution)/shard_map/ppermute | solution.py:99
  80.8 4.1 %collective-permute-done.11.refs_5_ = bf16[64,1536]{1,0:T(8,128)(2,1)S(1)} collective-permute-done((bf16[64,1536]{1,0:T(8,128)(2,1)S(1)}, bf16[64,1536]{1,0:T(8,128)(2,1)S(1)}, u32[]{:S(2)}, u32[]{:S(2)}) %collective-permute-start.11) | collective-permute-done | bytes 196640 | tf_op jit(solution)/shard_map/ppermute | solution.py:99
  84.9 4.6 %collective-permute-done.12.refs_6_ = bf16[64,1536]{1,0:T(8,128)(2,1)S(1)} collective-permute-done((bf16[64,1536]{1,0:T(8,128)(2,1)S(1)}, bf16[64,1536]{1,0:T(8,128)(2,1)S(1)}, u32[]{:S(2)}, u32[]{:S(2)}) %collective-permute-start.12) | collective-permute-done | bytes 196640 | tf_op jit(solution)/shard_map/ppermute | solution.py:99
  89.6 4.7 %all-to-all-done.2.parts = bf16[16,256,128]{2,1,0:T(8,128)(2,1)S(1)} async-done(((bf16[16,256,128]{2,1,0:T(8,128)(2,1)}), bf16[16,256,128]{2,1,0:T(8,128)(2,1)S(1)}, u32[]{:S(2)}, u32[]{:S(2)}) %all-to-all-start.2) | async-done | bytes 1048608 | tf_op jit(solution)/shard_map/all_to_all | solution.py:308
  94.3 1.7 %sum_terms.1 = bf16[32,32,128]{2,1,0:T(8,128)(2,1)} custom-call(s32[100]{0:T(128)S(1)} %concatenate.6.info, bf16[16,256,128]{2,1,0:T(8,128)(2,1)S(1)} %all-to-all-done.2.parts), custom_call_target="tpu_custom_call" | custom-call | tf_op jit(solution)/shard_map/sum_terms/pallas_call | solution.py:311
  96.1 4.7 %all-to-all-start.3 = ((bf16[128,8,128]{2,1,0:T(8,128)(2,1)}), bf16[128,8,128]{2,1,0:T(8,128)(2,1)S(1)}, u32[]{:S(2)}, u32[]{:S(2)}) async-start(bf16[128,8,128]{2,1,0:T(8,128)(2,1)} %bitcast.7), calls=%async_computation.3 | async-start | bytes 524288 | tf_op jit(solution)/shard_map/all_to_all | solution.py:321
  102.0 1.8 %unpack.1 = (bf16[64,5120]{1,0:T(8,128)(2,1)}, bf16[64,5120]{1,0:T(8,128)(2,1)}, bf16[64,1024]{1,0:T(8,128)(2,1)S(1)}, bf16[64,1024]{1,0:T(8,128)(2,1)S(1)}) custom-call(s32[100]{0:T(128)S(1)} %concatenate.6.info, bf16[64,1536]{1,0:T(8,128)(2,1)S(1)} %get-tuple-element.89.refs_0_, bf16[64,1536]{1,0:T(8,128)(2,1)S(1)} %collective-permute-done.7.refs_1_, ...), custom_call_target="tpu_custom_call" | custom-call | tf_op jit(solution)/shard_map/unpack/pallas_call | solution.py:325
  103.8 7.5 %all-to-all-done.3 = bf16[128,8,128]{2,1,0:T(8,128)(2,1)S(1)} async-done(((bf16[128,8,128]{2,1,0:T(8,128)(2,1)}), bf16[128,8,128]{2,1,0:T(8,128)(2,1)S(1)}, u32[]{:S(2)}, u32[]{:S(2)}) %all-to-all-start.3) | async-done | bytes 262176 | tf_op jit(solution)/shard_map/all_to_all | solution.py:321
  (48 shorter events, 12.2 us)
Async XLA Ops:
  0.6 13.7 %copy-start = (bf16[64,5120]{1,0:T(8,128)(2,1)S(1)}, bf16[64,5120]{1,0:T(8,128)(2,1)}, u32[]{:S(2)}) copy-start(bf16[64,5120]{1,0:T(8,128)(2,1)} %queries.1) | copy-start | bytes 1966084
  2.4 11.9 %copy-start.2 = (bf16[64,1024]{1,0:T(8,128)(2,1)S(1)}, bf16[64,1024]{1,0:T(8,128)(2,1)}, u32[]{:S(2)}) copy-start(bf16[64,1024]{1,0:T(8,128)(2,1)} %values.1) | copy-start | bytes 393220
  2.4 11.9 %copy-start.3 = (bf16[64,1024]{1,0:T(8,128)(2,1)S(1)}, bf16[64,1024]{1,0:T(8,128)(2,1)}, u32[]{:S(2)}) copy-start(bf16[64,1024]{1,0:T(8,128)(2,1)} %keys.1) | copy-start | bytes 393220
  2.4 21.7 %all-to-all-start = ((bf16[128,8,128]{2,1,0:T(8,128)(2,1)}), bf16[128,8,128]{2,1,0:T(8,128)(2,1)S(1)}, u32[]{:S(2)}, u32[]{:S(2)}) async-start(bf16[128,8,128]{2,1,0:T(8,128)(2,1)} %bitcast.5), calls=%async_computation | async-start | bytes 524288 | tf_op jit(solution)/shard_map/all_to_all | solution.py:242
  14.3 1.1 copy-start.1
  26.0 22.1 %all-to-all-start.1 = ((bf16[16,256,128]{2,1,0:T(8,128)(2,1)}), bf16[16,256,128]{2,1,0:T(8,128)(2,1)S(1)}, u32[]{:S(2)}, u32[]{:S(2)}) async-start(bf16[16,256,128]{2,1,0:T(8,128)(2,1)} %select_inner.1), calls=%async_computation.1 | async-start | bytes 2097152 | tf_op jit(solution)/shard_map/all_to_all | solution.py:261
  29.7 9.4 %collective-permute-start.4 = (bf16[64,1536]{1,0:T(8,128)(2,1)S(1)}, bf16[64,1536]{1,0:T(8,128)(2,1)S(1)}, u32[]{:S(2)}, u32[]{:S(2)}) collective-permute-start(bf16[64,1536]{1,0:T(8,128)(2,1)S(1)} %get-tuple-element.69), channel_id=1, source_target_pairs={{0,2},{1,3},{2,0},{3,1},{4,6},{5,7},{6,4},{7,5},{8,10},{9,11},{10,... | collective-permute-start | bytes 589832 | tf_op jit(solution)/shard_map/ppermute | solution.py:99
  31.0 12.2 %collective-permute-start.5 = (bf16[64,1536]{1,0:T(8,128)(2,1)S(1)}, bf16[64,1536]{1,0:T(8,128)(2,1)S(1)}, u32[]{:S(2)}, u32[]{:S(2)}) collective-permute-start(bf16[64,1536]{1,0:T(8,128)(2,1)S(1)} %get-tuple-element.70), channel_id=1, source_target_pairs={{0,1},{1,2},{2,3},{3,0},{4,5},{5,6},{6,7},{7,4},{8,9},{9,10},{10,1... | collective-permute-start | bytes 589832 | tf_op jit(solution)/shard_map/ppermute | solution.py:99
  32.2 11.7 %collective-permute-start.6 = (bf16[64,1536]{1,0:T(8,128)(2,1)S(1)}, bf16[64,1536]{1,0:T(8,128)(2,1)S(1)}, u32[]{:S(2)}, u32[]{:S(2)}) collective-permute-start(bf16[64,1536]{1,0:T(8,128)(2,1)S(1)} %get-tuple-element.71), channel_id=1, source_target_pairs={{0,3},{1,0},{2,1},{3,2},{4,7},{5,4},{6,5},{7,6},{8,11},{9,8},{10,9... | collective-permute-start | bytes 589832 | tf_op jit(solution)/shard_map/ppermute | solution.py:99
  34.2 24.8 %collective-permute-start = (bf16[64,1536]{1,0:T(8,128)(2,1)S(1)}, bf16[64,1536]{1,0:T(8,128)(2,1)S(1)}, u32[]{:S(2)}, u32[]{:S(2)}) collective-permute-start(bf16[64,1536]{1,0:T(8,128)(2,1)S(1)} %get-tuple-element.64), channel_id=1, source_target_pairs={{0,4},{1,5},{2,6},{3,7},{4,0},{5,1},{6,2},{7,3},{8,12},{9,13},{10,... | collective-permute-start | bytes 589832 | tf_op jit(solution)/shard_map/ppermute | solution.py:99
  34.2 25.9 %collective-permute-start.1 = (bf16[64,1536]{1,0:T(8,128)(2,1)S(1)}, bf16[64,1536]{1,0:T(8,128)(2,1)S(1)}, u32[]{:S(2)}, u32[]{:S(2)}) collective-permute-start(bf16[64,1536]{1,0:T(8,128)(2,1)S(1)} %get-tuple-element.65), channel_id=1, source_target_pairs={{0,6},{1,7},{2,4},{3,5},{4,2},{5,3},{6,0},{7,1},{8,14},{9,15},{10,... | collective-permute-start | bytes 589832 | tf_op jit(solution)/shard_map/ppermute | solution.py:99
  39.1 23.2 %collective-permute-start.2 = (bf16[64,1536]{1,0:T(8,128)(2,1)S(1)}, bf16[64,1536]{1,0:T(8,128)(2,1)S(1)}, u32[]{:S(2)}, u32[]{:S(2)}) collective-permute-start(bf16[64,1536]{1,0:T(8,128)(2,1)S(1)} %get-tuple-element.66), channel_id=1, source_target_pairs={{0,5},{1,6},{2,7},{3,4},{4,1},{5,2},{6,3},{7,0},{8,13},{9,14},{10,... | collective-permute-start | bytes 589832 | tf_op jit(solution)/shard_map/ppermute | solution.py:99
  43.9 18.4 %collective-permute-start.3 = (bf16[64,1536]{1,0:T(8,128)(2,1)S(1)}, bf16[64,1536]{1,0:T(8,128)(2,1)S(1)}, u32[]{:S(2)}, u32[]{:S(2)}) collective-permute-start(bf16[64,1536]{1,0:T(8,128)(2,1)S(1)} %get-tuple-element.67), channel_id=1, source_target_pairs={{0,7},{1,4},{2,5},{3,6},{4,3},{5,0},{6,1},{7,2},{8,15},{9,12},{10,... | collective-permute-start | bytes 589832 | tf_op jit(solution)/shard_map/ppermute | solution.py:99
  48.1 0.9 copy-start.7
  58.1 14.1 %collective-permute-start.7 = (bf16[64,1536]{1,0:T(8,128)(2,1)S(1)}, bf16[64,1536]{1,0:T(8,128)(2,1)S(1)}, u32[]{:S(2)}, u32[]{:S(2)}) collective-permute-start(bf16[64,1536]{1,0:T(8,128)(2,1)S(1)} %get-tuple-element.76), channel_id=1, source_target_pairs={{0,2},{1,3},{2,0},{3,1},{4,6},{5,7},{6,4},{7,5},{8,10},{9,11},{10,... | collective-permute-start | bytes 589832 | tf_op jit(solution)/shard_map/ppermute | solution.py:99
  59.0 13.2 %collective-permute-start.8 = (bf16[64,1536]{1,0:T(8,128)(2,1)S(1)}, bf16[64,1536]{1,0:T(8,128)(2,1)S(1)}, u32[]{:S(2)}, u32[]{:S(2)}) collective-permute-start(bf16[64,1536]{1,0:T(8,128)(2,1)S(1)} %get-tuple-element.77), channel_id=1, source_target_pairs={{0,1},{1,2},{2,3},{3,0},{4,5},{5,6},{6,7},{7,4},{8,9},{9,10},{10,1... | collective-permute-start | bytes 589832 | tf_op jit(solution)/shard_map/ppermute | solution.py:99
  60.2 12.0 %collective-permute-start.9 = (bf16[64,1536]{1,0:T(8,128)(2,1)S(1)}, bf16[64,1536]{1,0:T(8,128)(2,1)S(1)}, u32[]{:S(2)}, u32[]{:S(2)}) collective-permute-start(bf16[64,1536]{1,0:T(8,128)(2,1)S(1)} %get-tuple-element.78), channel_id=1, source_target_pairs={{0,3},{1,0},{2,1},{3,2},{4,7},{5,4},{6,5},{7,6},{8,11},{9,8},{10,9... | collective-permute-start | bytes 589832 | tf_op jit(solution)/shard_map/ppermute | solution.py:99
  72.2 4.4 %copy-start.5 = (bf16[64,1536]{1,0:T(8,128)(2,1)S(1)}, bf16[64,1536]{1,0:T(8,128)(2,1)}, u32[]{:S(2)}) copy-start(bf16[64,1536]{1,0:T(8,128)(2,1)} %copy-done.4) | copy-start | bytes 589828
  72.2 22.2 %all-to-all-start.2 = ((bf16[16,256,128]{2,1,0:T(8,128)(2,1)}), bf16[16,256,128]{2,1,0:T(8,128)(2,1)S(1)}, u32[]{:S(2)}, u32[]{:S(2)}) async-start(bf16[16,256,128]{2,1,0:T(8,128)(2,1)} %get-tuple-element.79), calls=%async_computation.2 | async-start | bytes 2097152 | tf_op jit(solution)/shard_map/all_to_all | solution.py:308
  76.5 4.3 %collective-permute-start.10 = (bf16[64,1536]{1,0:T(8,128)(2,1)}, bf16[64,1536]{1,0:T(8,128)(2,1)S(1)}, u32[]{:S(2)}, u32[]{:S(2)}) collective-permute-start(bf16[64,1536]{1,0:T(8,128)(2,1)} %get-tuple-element.84), channel_id=1, source_target_pairs={{0,4},{1,5},{2,6},{3,7},{4,0},{5,1},{6,2},{7,3},{8,12},{9,13},{10,... | collective-permute-start | bytes 589832 | tf_op jit(solution)/shard_map/ppermute | solution.py:99
  76.6 8.3 %collective-permute-start.11 = (bf16[64,1536]{1,0:T(8,128)(2,1)S(1)}, bf16[64,1536]{1,0:T(8,128)(2,1)S(1)}, u32[]{:S(2)}, u32[]{:S(2)}) collective-permute-start(bf16[64,1536]{1,0:T(8,128)(2,1)S(1)} %copy-done.5), channel_id=1, source_target_pairs={{0,6},{1,7},{2,4},{3,5},{4,2},{5,3},{6,0},{7,1},{8,14},{9,15},{10,... | collective-permute-start | bytes 589832 | tf_op jit(solution)/shard_map/ppermute | solution.py:99
  77.9 11.7 %collective-permute-start.12 = (bf16[64,1536]{1,0:T(8,128)(2,1)S(1)}, bf16[64,1536]{1,0:T(8,128)(2,1)S(1)}, u32[]{:S(2)}, u32[]{:S(2)}) collective-permute-start(bf16[64,1536]{1,0:T(8,128)(2,1)S(1)} %get-tuple-element.86), channel_id=1, source_target_pairs={{0,5},{1,6},{2,7},{3,4},{4,1},{5,2},{6,3},{7,0},{8,13},{9,14},{10,... | collective-permute-start | bytes 589832 | tf_op jit(solution)/shard_map/ppermute | solution.py:99
  78.9 10.7 %collective-permute-start.13 = (bf16[64,1536]{1,0:T(8,128)(2,1)S(1)}, bf16[64,1536]{1,0:T(8,128)(2,1)S(1)}, u32[]{:S(2)}, u32[]{:S(2)}) collective-permute-start(bf16[64,1536]{1,0:T(8,128)(2,1)S(1)} %get-tuple-element.87), channel_id=1, source_target_pairs={{0,7},{1,4},{2,5},{3,6},{4,3},{5,0},{6,1},{7,2},{8,15},{9,12},{10,... | collective-permute-start | bytes 589832 | tf_op jit(solution)/shard_map/ppermute | solution.py:99
  96.1 15.2 %all-to-all-start.3 = ((bf16[128,8,128]{2,1,0:T(8,128)(2,1)}), bf16[128,8,128]{2,1,0:T(8,128)(2,1)S(1)}, u32[]{:S(2)}, u32[]{:S(2)}) async-start(bf16[128,8,128]{2,1,0:T(8,128)(2,1)} %bitcast.7), calls=%async_computation.3 | async-start | bytes 524288 | tf_op jit(solution)/shard_map/all_to_all | solution.py:321
  (7 other events, 4.9 us)

commit v3 on v2

--- a/solution.py
+++ b/solution.py
@@ -24,7 +24,8 @@
 MIB = 1024 * 1024
 LOG2_E = 1.4426950408889634
 
-PARENT, NODE_OF_SLOT, LIVE_TILES, PLACE = 0, 32, 64, 96
+PARENT, NODE_OF_SLOT, LIVE_TILES, SLOT_OF_NODE, PLACE = 0, 32, 64, 96, 128
+INFO_SIZE = 131
 
 ALL = ("chip", "core", "head")
 GROUP_AXES = ("core", "head")
@@ -38,6 +39,10 @@
     return pl.BlockSpec(memory_space=pltpu.VMEM)
 
 
+def hbm():
+    return pl.BlockSpec(memory_space=pltpu.HBM)
+
+
 def nt_dot(left, right):
     return lax.dot_general(left, right, (((1,), (1,)), ((), ())), preferred_element_type=F32)
 
@@ -46,16 +51,22 @@
     return lax.dot_general(left, right, (((1,), (0,)), ((), ())), preferred_element_type=F32)
 
 
+def info_kernel(parent, node_of_slot, live_tiles, info):
+    for n in range(NODES):
+        info[PARENT + n] = parent[n]
+        info[NODE_OF_SLOT + n] = node_of_slot[n]
+        info[LIVE_TILES + n] = live_tiles[n]
+    for slot in range(NODES):
+        info[SLOT_OF_NODE + node_of_slot[slot]] = slot
+    for n, axis in enumerate(ALL):
+        info[PLACE + n] = lax.axis_index(axis)
+
+
 def select_kernel(info, pieces, out):
-    for slot in range(NODES):
-        node = info[NODE_OF_SLOT + slot]
-
-        @pl.when(node < INNER)
-        def _():
-            row = pl.multiple_of(node * 32, 32)
-            block = pieces[slot]
-            for chip in range(CHIPS):
-                out[chip, pl.ds(row, 32), :] = block
+    for node in range(INNER):
+        block = pieces[info[SLOT_OF_NODE + node]]
+        for chip in range(CHIPS):
+            out[chip, node * 32 : node * 32 + 32, :] = block
 
 
 SHIFTS = (0, 2, 1, 3)
@@ -101,31 +112,28 @@
     return moved
 
 
-def copy_all(sources, targets, sems):
-    copies = [
-        pltpu.make_async_copy(source, target, sems.at[n])
-        for n, (source, target) in enumerate(zip(sources, targets))
-    ]
-    for copy in copies:
-        copy.start()
-    return copies
-
-
 def attention_kernel(dc, info, far, *refs):
     arrived, refs = refs[:4], refs[4:]
     if dc == 0:
         leaving, key_out, value_out, refs = refs[:4], refs[4], refs[5], refs[6:]
     else:
         first_key, first_value, leaving, terms, refs = refs[0], refs[1], refs[2:6], refs[6], refs[7:]
-    mine, out, key_all, value_all, bias, probs_all, dscores_all, sems = refs[:8]
+    mine, out, key_all, value_all, bias, probs_all, dscores_all = refs[:7]
+    sems = refs[7]
     quarters = [
         pl.ds(pl.multiple_of(lax.rem(info[PLACE + 2] + 4 - dx, 4) * 64, 64), 64) for dx in SHIFTS
     ]
-    copies = copy_all(arrived, [mine.at[quarter, :] for quarter in quarters], sems)
+    copies = []
+    for n, (quarter, piece) in enumerate(zip(quarters, arrived)):
+        if dc == 0:
+            copies.append(pltpu.make_async_copy(piece, mine.at[quarter, :], sems.at[n]))
+            copies[-1].start()
+        else:
+            mine[quarter, :] = piece[...]
     row = lax.broadcasted_iota(jnp.int32, (SEG, SEG), 0)
     token = lax.broadcasted_iota(jnp.int32, (SEG, SEG), 1)
     bias[:, 0:SEG] = jnp.where(token <= row, 0.0, -jnp.inf)
-    tile = lax.rem(token, 32) // 16
+    tile = (token >> 4) & 1
 
     def lineage(which):
         me = info[NODE_OF_SLOT + 2 * info[PLACE] + lax.rem(info[PLACE + 1] + which, 2)]
@@ -134,6 +142,27 @@
             current = chain[-1]
             chain.append(jnp.where(current >= 0, info[PARENT + jnp.maximum(current, 0)], -1))
         return chain
+
+    def accumulate(chain, key_part, value_part):
+        for step in range(1, 4):
+            rows = pl.ds(pl.multiple_of(jnp.maximum(chain[step], 0) * 32, 32), 32)
+            here = slice(step * SEG, (step + 1) * SEG)
+            acc[0:8, rows, :] += key_part[here].reshape(8, 32, HD)
+            acc[8:16, rows, :] += value_part[here].reshape(8, 32, HD)
+
+        @pl.when(chain[0] < INNER)
+        def _():
+            for piece in range(8):
+                for quarter in range(4):
+                    first = quarter * 64 + piece * 8
+                    rows = pl.ds(pl.multiple_of(chain[0] * 32 + quarter * 8, 8), 8)
+                    acc[piece, rows, :] += key_part[first : first + 8]
+                    acc[8 + piece, rows, :] += value_part[first : first + 8]
+
+    if dc == 1:
+        acc = refs[8]
+        acc[...] = jnp.zeros_like(acc)
+        accumulate(lineage(0), first_key, first_value)
 
     for step, node in enumerate(lineage(dc)[1:], 1):
         safe = jnp.maximum(node, 0)
@@ -181,61 +210,38 @@
     quarters = [
         pl.ds(pl.multiple_of(lax.rem(info[PLACE + 2] + dx, 4) * 64, 64), 64) for dx in SHIFTS
     ]
-    copies = copy_all([out.at[quarter, :] for quarter in quarters], leaving, sems)
+    for quarter, piece in zip(quarters, leaving):
+        piece[...] = out[quarter, :]
 
     if dc == 0:
         key_out[...] = key_terms
         value_out[...] = value_terms
     else:
-        acc = refs[8]
-        acc[...] = jnp.zeros_like(acc)
-        for chain, key_part, value_part in (
-            (lineage(0), first_key, first_value),
-            (lineage(1), key_terms, value_terms),
-        ):
-            for step in range(1, 4):
-                rows = pl.ds(pl.multiple_of(jnp.maximum(chain[step], 0) * 32, 32), 32)
-                here = slice(step * SEG, (step + 1) * SEG)
-                acc[0:8, rows, :] += key_part[here].reshape(8, 32, HD)
-                acc[8:16, rows, :] += value_part[here].reshape(8, 32, HD)
-
-            @pl.when(chain[0] < INNER)
-            def _():
-                for piece in range(8):
-                    for quarter in range(4):
-                        first = quarter * 64 + piece * 8
-                        rows = pl.ds(pl.multiple_of(chain[0] * 32 + quarter * 8, 8), 8)
-                        acc[piece, rows, :] += key_part[first : first + 8]
-                        acc[8 + piece, rows, :] += value_part[first : first + 8]
-
+        accumulate(lineage(1), key_terms, value_terms)
         terms[...] = acc[...].astype(BF)
-    for copy in copies:
-        copy.wait()
-
-
-def sum_kernel(info, parts, out, total):
-    sums = parts[0].astype(F32)
-    for chip in range(1, CHIPS):
-        sums = sums + parts[chip].astype(F32)
-    total[...] = sums.astype(BF)
-    for slot in range(NODES):
-        node = info[NODE_OF_SLOT + slot]
-
-        @pl.when(node < INNER)
-        def _():
-            out[slot] = total[pl.ds(pl.multiple_of(node * 32, 32), 32), :]
-
-        @pl.when(node >= INNER)
-        def _():
-            out[slot] = jnp.zeros((32, HD), BF)
+
+
+def sum_kernel(info, parts, out):
+    out[...] = jnp.zeros_like(out)
+    for node in range(INNER):
+        rows = slice(node * 32, node * 32 + 32)
+        sums = parts[0, rows, :].astype(F32)
+        for chip in range(1, CHIPS):
+            sums = sums + parts[chip, rows, :].astype(F32)
+        out[info[SLOT_OF_NODE + node]] = sums.astype(BF)
 
 
 def on_device(queries, keys, values, out_grad, parent, node_of_slot, live_tiles):
     rows = queries.shape[0]
     chip = lax.axis_index("chip")
     core = lax.axis_index("core")
-    place = jnp.stack([chip, core, lax.axis_index("head"), 0]).astype(jnp.int32)
-    info = jnp.concatenate([parent, node_of_slot, live_tiles, place])
+    info = pl.pallas_call(
+        info_kernel,
+        out_shape=pltpu.SMEM((INFO_SIZE,), jnp.int32),
+        in_specs=[smem()] * 3,
+        out_specs=smem(),
+        name="info",
+    )(parent, node_of_slot, live_tiles)
 
     pieces = jnp.concatenate([keys, values], 0).reshape(16, 8, KV_HEADS, HD)
     pieces = pieces.transpose(0, 2, 1, 3).reshape(CHIPS * KV_HEADS, 8, HD)
@@ -243,7 +249,7 @@
     piece_shape = jax.ShapeDtypeStruct((rows, WIDE), BF)
     packed = pl.pallas_call(
         pack_kernel,
-        out_shape=(piece_shape,) * 8,
+        out_shape=(pltpu.HBM((rows, WIDE), BF),) * 8,
         in_specs=[smem()] + [vmem()] * 4,
         out_specs=(vmem(),) * 8,
         compiler_params=pltpu.CompilerParams(vmem_limit_bytes=8 * MIB),
@@ -260,14 +266,14 @@
     )(info, pieces.reshape(NODES, 32, HD))
     far = lax.all_to_all(inner, "chip", split_axis=0, concat_axis=0, tiled=True)
     arrived = exchange(packed, PIECES)
-
-    any_memory = pl.BlockSpec(memory_space=pl.ANY)
+    arrived[:4] = [pltpu.with_memory_space_constraint(piece, pltpu.HBM) for piece in arrived[:4]]
+
     half = jax.ShapeDtypeStruct((4 * SEG, HD), F32)
 
     def attend(dc, operands):
         last = dc == 1
         out_shape = (piece_shape,) * 4
-        out_specs = (any_memory,) * 4
+        out_specs = (vmem(),) * 4
         scratch_shapes = [
             pltpu.VMEM((SEG, WIDE), BF),
             pltpu.VMEM((SEG, WIDE), BF),
@@ -288,10 +294,10 @@
         return pl.pallas_call(
             functools.partial(attention_kernel, dc),
             out_shape=out_shape,
-            in_specs=[smem(), vmem()] + [any_memory] * 4 + [vmem()] * (2 if last else 0),
+            in_specs=[smem(), vmem()] + ([vmem()] * 6 if last else [hbm()] * 4),
             out_specs=out_specs,
             scratch_shapes=scratch_shapes,
-            compiler_params=pltpu.CompilerParams(vmem_limit_bytes=28 * MIB),
+            compiler_params=pltpu.CompilerParams(vmem_limit_bytes=20 * MIB),
             cost_estimate=pl.CostEstimate(
                 flops=2 * 5 * GROUP * SEG * 4 * SEG * HD * 4,
                 bytes_accessed=6 * 1024 * 1024,
@@ -313,7 +319,6 @@
         out_shape=jax.ShapeDtypeStruct((NODES, 32, HD), BF),
         in_specs=[smem(), vmem()],
         out_specs=vmem(),
-        scratch_shapes=[pltpu.VMEM((INNER * 32, HD), BF)],
         compiler_params=pltpu.CompilerParams(vmem_limit_bytes=6 * MIB),
         name="sum_terms",
     )(info, parts)

time: 114 us -> 108 us (0.947)
  Pallas kernels: 23.5 us -> 19.5 us
  local copies, waits for them, and re-layouts: 6.31 us -> 2.37 us
  starting transfers between devices: 38.1 us -> 40.1 us
    unnamed x26 -> x30, local copies, waits for them, and re-layouts: 5.64 us -> 1.78 us
    pallas_call x2, Pallas kernels: 17.3 us -> 14 us  [attend(): pl.pallas_call(functools.partial(attention_kernel, dc), out_shape=out_sha...]
    pallas_call x1 -> x2, Pallas kernels: 0.7 us -> 2.12 us  [the longest x1 1.3 us: on_device(): pl.pallas_call(pack_kernel, out_shape=(pltpu.HBM((rows, WIDE), BF),) * 8,...]
    all_to_all x1, waiting for transfers between devices: 3.5 us -> 4.83 us  [on_device(): far = lax.all_to_all(inner, 'chip', split_axis=0, concat_axis=0, tiled=True)]
  transfers between devices with their start and end apart: 18 -> 18, of which waited for: 8 -> 8; matrix products, arithmetic and copies ran while one was open for 1% -> 1% of each run, Pallas kernels for 18% -> 16%
where the time goes in v3:
time: 108 us; the launch traced here: 106 us
  starting transfers between devices  40.1 us (37%)
  waiting for transfers between devices  39.9 us (37%)
  Pallas kernels  19.5 us (18%)
  other arithmetic  2.48 us (2%)
  local copies, waits for them, and re-layouts  2.37 us (2%)
  between operations  1.51 us (1%)
    ppermute x14, waiting for transfers between devices, exchange(): piece = lax.ppermute(piece, GROUP_AXES, pairs)  15.6 us
    ppermute x14, starting transfers between devices, exchange(): piece = lax.ppermute(piece, GROUP_AXES, pairs)  15.1 us
    pallas_call x2, Pallas kernels, attend(): pl.pallas_call(functools.partial(attention_kernel, dc), out_shape=out_sha...  14 us
    all_to_all x1, starting transfers between devices, on_device(): lax.all_to_all(pieces, ALL, split_axis=0, concat_axis=0, tiled=True)  11.1 us
    all_to_all x1, waiting for transfers between devices, on_device(): sums = lax.all_to_all(sums, ALL, split_axis=0, concat_axis=0, tiled=True)  7.31 us
    all_to_all x1, waiting for transfers between devices, on_device(): lax.all_to_all(pieces, ALL, split_axis=0, concat_axis=0, tiled=True)  7.27 us
    all_to_all x1, starting transfers between devices, on_device(): lax.all_to_all(terms, 'chip', split_axis=0, concat_axis=0, tiled=True)  4.98 us
    all_to_all x1, starting transfers between devices, on_device(): sums = lax.all_to_all(sums, ALL, split_axis=0, concat_axis=0, tiled=True)  4.98 us
  transfers between devices with their start and end apart: 18, of which 8 were waited for; matrix products, arithmetic and copies ran while one was open for 1% of the time, Pallas kernels for 16%

profile of v3, /device:TPU:0, one launch (start us, length us, event | category | flops | bytes accessed | tf_op | source)
XLA Modules:
  0.0 105.9 jit_solution(12900751627128097849)
XLA Ops:
  0.6 1.8 %pad_maximum_fusion = bf16[128,1024]{1,0:T(8,128)(2,1)} fusion(bf16[64,1024]{1,0:T(8,128)(2,1)} %values.1, bf16[64,1024]{1,0:T(8,128)(2,1)} %keys.1), kind=kLoop, calls=%fused_computation | loop fusion | flops 524288 | bytes 524288 | tf_op jit(solution)/shard_map/concatenate | solution.py:246
  2.4 11.1 %all-to-all-start = ((bf16[128,8,128]{2,1,0:T(8,128)(2,1)}), bf16[128,8,128]{2,1,0:T(8,128)(2,1)S(1)}, u32[]{:S(2)}, u32[]{:S(2)}) async-start(bf16[128,8,128]{2,1,0:T(8,128)(2,1)} %bitcast.2), calls=%async_computation | async-start | bytes 524288 | tf_op jit(solution)/shard_map/all_to_all | solution.py:248
  15.5 1.3 %pack.1 = (bf16[64,1536]{1,0:T(8,128)(2,1)}, bf16[64,1536]{1,0:T(8,128)(2,1)}, bf16[64,1536]{1,0:T(8,128)(2,1)}, bf16[64,1536]{1,0:T(8,128)(2,1)}, bf16[64,1536]...) custom-call(s32[131]{0:T(256)S(4)} %info.1, ...), custom_call_target="tpu_custom_call" | custom-call | tf_op jit(solution)/shard_map/pack/pallas_call | solution.py:250
  16.8 7.3 %all-to-all-done = bf16[128,8,128]{2,1,0:T(8,128)(2,1)S(1)} async-done(((bf16[128,8,128]{2,1,0:T(8,128)(2,1)}), bf16[128,8,128]{2,1,0:T(8,128)(2,1)S(1)}, u32[]{:S(2)}, u32[]{:S(2)}) %all-to-all-start) | async-done | bytes 262176 | tf_op jit(solution)/shard_map/all_to_all | solution.py:248
  24.1 1.2 %select_inner.1 = bf16[16,256,128]{2,1,0:T(8,128)(2,1)} custom-call(s32[131]{0:T(256)S(4)} %info.1, bf16[32,32,128]{2,1,0:T(8,128)(2,1)S(1)} %bitcast.19), custom_call_target="tpu_custom_call" | custom-call | tf_op jit(solution)/shard_map/select_inner/pallas_call | solution.py:259
  25.3 3.9 %all-to-all-start.1 = ((bf16[16,256,128]{2,1,0:T(8,128)(2,1)}), bf16[16,256,128]{2,1,0:T(8,128)(2,1)S(1)}, u32[]{:S(2)}, u32[]{:S(2)}) async-start(bf16[16,256,128]{2,1,0:T(8,128)(2,1)} %select_inner.1), calls=%async_computation.1 | async-start | bytes 2097152 | tf_op jit(solution)/shard_map/all_to_all | solution.py:267
  29.2 1.3 %collective-permute-start.4 = (bf16[64,1536]{1,0:T(8,128)(2,1)S(1)}, bf16[64,1536]{1,0:T(8,128)(2,1)S(1)}, u32[]{:S(2)}, u32[]{:S(2)}) collective-permute-start(bf16[64,1536]{1,0:T(8,128)(2,1)S(1)} %copy-done.14), channel_id=1, source_target_pairs={{0,2},{1,3},{2,0},{3,1},{4,6},{5,7},{6,4},{7,5},{8,10},{9,11},{10,... | collective-permute-start | bytes 589832 | tf_op jit(solution)/shard_map/ppermute | solution.py:110
  31.6 2.1 %collective-permute-start.6 = (bf16[64,1536]{1,0:T(8,128)(2,1)S(1)}, bf16[64,1536]{1,0:T(8,128)(2,1)S(1)}, u32[]{:S(2)}, u32[]{:S(2)}) collective-permute-start(bf16[64,1536]{1,0:T(8,128)(2,1)S(1)} %copy-done.9), channel_id=1, source_target_pairs={{0,3},{1,0},{2,1},{3,2},{4,7},{5,4},{6,5},{7,6},{8,11},{9,8},{10,9... | collective-permute-start | bytes 589832 | tf_op jit(solution)/shard_map/ppermute | solution.py:110
  33.7 1.2 %collective-permute-start.1 = (bf16[64,1536]{1,0:T(8,128)(2,1)S(1)}, bf16[64,1536]{1,0:T(8,128)(2,1)S(1)}, u32[]{:S(2)}, u32[]{:S(2)}) collective-permute-start(bf16[64,1536]{1,0:T(8,128)(2,1)S(1)} %copy-done.7), channel_id=1, source_target_pairs={{0,6},{1,7},{2,4},{3,5},{4,2},{5,3},{6,0},{7,1},{8,14},{9,15},{10,... | collective-permute-start | bytes 589832 | tf_op jit(solution)/shard_map/ppermute | solution.py:110
  35.0 3.6 %collective-permute-done.4.refs_1_ = bf16[64,1536]{1,0:T(8,128)(2,1)S(1)} collective-permute-done((bf16[64,1536]{1,0:T(8,128)(2,1)S(1)}, bf16[64,1536]{1,0:T(8,128)(2,1)S(1)}, u32[]{:S(2)}, u32[]{:S(2)}) %collective-permute-start.4) | collective-permute-done | bytes 196640 | tf_op jit(solution)/shard_map/ppermute | solution.py:110
  38.6 4.1 %collective-permute-done.5.refs_2_ = bf16[64,1536]{1,0:T(8,128)(2,1)S(1)} collective-permute-done((bf16[64,1536]{1,0:T(8,128)(2,1)S(1)}, bf16[64,1536]{1,0:T(8,128)(2,1)S(1)}, u32[]{:S(2)}, u32[]{:S(2)}) %collective-permute-start.5) | collective-permute-done | bytes 196640 | tf_op jit(solution)/shard_map/ppermute | solution.py:110
  42.7 4.8 %all-to-all-done.1.far = bf16[16,256,128]{2,1,0:T(8,128)(2,1)S(1)} async-done(((bf16[16,256,128]{2,1,0:T(8,128)(2,1)}), bf16[16,256,128]{2,1,0:T(8,128)(2,1)S(1)}, u32[]{:S(2)}, u32[]{:S(2)}) %all-to-all-start.1) | async-done | bytes 1048608 | tf_op jit(solution)/shard_map/all_to_all | solution.py:267
  47.5 6.8 %attention.2 = (bf16[64,1536]{1,0:T(8,128)(2,1)S(1)}, bf16[64,1536]{1,0:T(8,128)(2,1)S(1)}, bf16[64,1536]{1,0:T(8,128)(2,1)S(1)}, bf16[64,1536]{1,0:T(8,128)(2,1...) custom-call(s32[131]{0:T(256)S(4)} %info.1, bf16[16,256,128]{2,1,0:T(8,128)(2,1)S(1)} %all-to-all-done.1.far, ...), custom_call_target="tpu_custom_call" | custom-call | flops 6710886400 | bytes 6291456 | tf_op jit(solution)/shard_map/attention/pallas_call | solution.py:294
  56.4 2.1 %collective-permute-start.9 = (bf16[64,1536]{1,0:T(8,128)(2,1)S(1)}, bf16[64,1536]{1,0:T(8,128)(2,1)S(1)}, u32[]{:S(2)}, u32[]{:S(2)}) collective-permute-start(bf16[64,1536]{1,0:T(8,128)(2,1)S(1)} %get-tuple-element.78), channel_id=1, source_target_pairs={{0,3},{1,0},{2,1},{3,2},{4,7},{5,4},{6,5},{7,6},{8,11},{9,8},{10,9... | collective-permute-start | bytes 589832 | tf_op jit(solution)/shard_map/ppermute | solution.py:110
  58.5 7.2 %attention.3 = (bf16[64,1536]{1,0:T(8,128)(2,1)S(1)}, bf16[64,1536]{1,0:T(8,128)(2,1)S(1)}, bf16[64,1536]{1,0:T(8,128)(2,1)S(1)}, bf16[64,1536]{1,0:T(8,128)(2,1)S(1)}, bf16[16,256,128]{2,1,0:T(8,128)(2,1)}) custom-call(s32[131]{0:T(256)S(4)} %info.1, bf16[16,256,128]{2,1,0:T(8,128)(2,1)S(1)} %all-to-all-done.1.far, ...), custom_call_target="tpu_custom_call" | custom-call | flops 6710886400 | bytes 6291456 | tf_op jit(solution)/shard_map/attention/pallas_call | solution.py:294
  65.8 5.0 %all-to-all-start.2 = ((bf16[16,256,128]{2,1,0:T(8,128)(2,1)}), bf16[16,256,128]{2,1,0:T(8,128)(2,1)S(1)}, u32[]{:S(2)}, u32[]{:S(2)}) async-start(bf16[16,256,128]{2,1,0:T(8,128)(2,1)} %get-tuple-element.79), calls=%async_computation.2 | async-start | bytes 2097152 | tf_op jit(solution)/shard_map/all_to_all | solution.py:314
  70.9 2.1 %collective-permute-start.11 = (bf16[64,1536]{1,0:T(8,128)(2,1)S(1)}, bf16[64,1536]{1,0:T(8,128)(2,1)S(1)}, u32[]{:S(2)}, u32[]{:S(2)}) collective-permute-start(bf16[64,1536]{1,0:T(8,128)(2,1)S(1)} %get-tuple-element.85), channel_id=1, source_target_pairs={{0,6},{1,7},{2,4},{3,5},{4,2},{5,3},{6,0},{7,1},{8,14},{9,15},{10,... | collective-permute-start | bytes 589832 | tf_op jit(solution)/shard_map/ppermute | solution.py:110
  73.0 3.0 %collective-permute-start.13 = (bf16[64,1536]{1,0:T(8,128)(2,1)S(1)}, bf16[64,1536]{1,0:T(8,128)(2,1)S(1)}, u32[]{:S(2)}, u32[]{:S(2)}) collective-permute-start(bf16[64,1536]{1,0:T(8,128)(2,1)S(1)} %get-tuple-element.87), channel_id=1, source_target_pairs={{0,7},{1,4},{2,5},{3,6},{4,3},{5,0},{6,1},{7,2},{8,15},{9,12},{10,... | collective-permute-start | bytes 589832 | tf_op jit(solution)/shard_map/ppermute | solution.py:110
  76.0 3.2 %collective-permute-done.11.refs_5_ = bf16[64,1536]{1,0:T(8,128)(2,1)S(1)} collective-permute-done((bf16[64,1536]{1,0:T(8,128)(2,1)S(1)}, bf16[64,1536]{1,0:T(8,128)(2,1)S(1)}, u32[]{:S(2)}, u32[]{:S(2)}) %collective-permute-start.11) | collective-permute-done | bytes 196640 | tf_op jit(solution)/shard_map/ppermute | solution.py:110
  79.2 4.7 %collective-permute-done.12.refs_6_ = bf16[64,1536]{1,0:T(8,128)(2,1)S(1)} collective-permute-done((bf16[64,1536]{1,0:T(8,128)(2,1)S(1)}, bf16[64,1536]{1,0:T(8,128)(2,1)S(1)}, u32[]{:S(2)}, u32[]{:S(2)}) %collective-permute-start.12) | collective-permute-done | bytes 196640 | tf_op jit(solution)/shard_map/ppermute | solution.py:110
  83.9 4.9 %all-to-all-done.2.parts = bf16[16,256,128]{2,1,0:T(8,128)(2,1)S(1)} async-done(((bf16[16,256,128]{2,1,0:T(8,128)(2,1)}), bf16[16,256,128]{2,1,0:T(8,128)(2,1)S(1)}, u32[]{:S(2)}, u32[]{:S(2)}) %all-to-all-start.2) | async-done | bytes 1048608 | tf_op jit(solution)/shard_map/all_to_all | solution.py:314
  89.7 5.0 %all-to-all-start.3 = ((bf16[128,8,128]{2,1,0:T(8,128)(2,1)}), bf16[128,8,128]{2,1,0:T(8,128)(2,1)S(1)}, u32[]{:S(2)}, u32[]{:S(2)}) async-start(bf16[128,8,128]{2,1,0:T(8,128)(2,1)} %bitcast.4), calls=%async_computation.3 | async-start | bytes 524288 | tf_op jit(solution)/shard_map/all_to_all | solution.py:326
  96.6 1.3 %unpack.1 = (bf16[64,5120]{1,0:T(8,128)(2,1)}, bf16[64,5120]{1,0:T(8,128)(2,1)}, bf16[64,1024]{1,0:T(8,128)(2,1)S(1)}, bf16[64,1024]{1,0:T(8,128)(2,1)S(1)}) custom-call(s32[131]{0:T(256)S(4)} %info.1, bf16[64,1536]{1,0:T(8,128)(2,1)S(1)} %get-tuple-element.89.refs_0_, bf16[64,1536]{1,0:T(8,128)(2,1)S(1)} %collective-permute-done.7.refs_1_, ...), custom_call_target="tpu_custom_call" | custom-call | tf_op jit(solution)/shard_map/unpack/pallas_call | solution.py:330
  97.9 7.3 %all-to-all-done.3 = bf16[128,8,128]{2,1,0:T(8,128)(2,1)S(1)} async-done(((bf16[128,8,128]{2,1,0:T(8,128)(2,1)}), bf16[128,8,128]{2,1,0:T(8,128)(2,1)S(1)}, u32[]{:S(2)}, u32[]{:S(2)}) %all-to-all-start.3) | async-done | bytes 262176 | tf_op jit(solution)/shard_map/all_to_all | solution.py:326
  (52 shorter events, 8.1 us)
Async XLA Ops:
  0.6 13.7 %copy-start = (bf16[64,5120]{1,0:T(8,128)(2,1)S(1)}, bf16[64,5120]{1,0:T(8,128)(2,1)}, u32[]{:S(2)}) copy-start(bf16[64,5120]{1,0:T(8,128)(2,1)} %queries.1) | copy-start | bytes 1966084
  2.4 12.0 %copy-start.2 = (bf16[64,1024]{1,0:T(8,128)(2,1)S(1)}, bf16[64,1024]{1,0:T(8,128)(2,1)}, u32[]{:S(2)}) copy-start(bf16[64,1024]{1,0:T(8,128)(2,1)} %values.1) | copy-start | bytes 393220
  2.4 12.0 %copy-start.3 = (bf16[64,1024]{1,0:T(8,128)(2,1)S(1)}, bf16[64,1024]{1,0:T(8,128)(2,1)}, u32[]{:S(2)}) copy-start(bf16[64,1024]{1,0:T(8,128)(2,1)} %keys.1) | copy-start | bytes 393220
  2.4 21.7 %all-to-all-start = ((bf16[128,8,128]{2,1,0:T(8,128)(2,1)}), bf16[128,8,128]{2,1,0:T(8,128)(2,1)S(1)}, u32[]{:S(2)}, u32[]{:S(2)}) async-start(bf16[128,8,128]{2,1,0:T(8,128)(2,1)} %bitcast.2), calls=%async_computation | async-start | bytes 524288 | tf_op jit(solution)/shard_map/all_to_all | solution.py:248
  25.3 13.3 %copy-start.6 = (bf16[64,1536]{1,0:T(8,128)(2,1)S(1)}, bf16[64,1536]{1,0:T(8,128)(2,1)}, u32[]{:S(2)}) copy-start(bf16[64,1536]{1,0:T(8,128)(2,1)} %get-tuple-element.66) | copy-start | bytes 589828
  25.3 17.4 %copy-start.5 = (bf16[64,1536]{1,0:T(8,128)(2,1)S(1)}, bf16[64,1536]{1,0:T(8,128)(2,1)}, u32[]{:S(2)}) copy-start(bf16[64,1536]{1,0:T(8,128)(2,1)} %get-tuple-element.67) | copy-start | bytes 589828
  25.3 22.2 %all-to-all-start.1 = ((bf16[16,256,128]{2,1,0:T(8,128)(2,1)}), bf16[16,256,128]{2,1,0:T(8,128)(2,1)S(1)}, u32[]{:S(2)}, u32[]{:S(2)}) async-start(bf16[16,256,128]{2,1,0:T(8,128)(2,1)} %select_inner.1), calls=%async_computation.1 | async-start | bytes 2097152 | tf_op jit(solution)/shard_map/all_to_all | solution.py:267
  29.2 9.4 %collective-permute-start.4 = (bf16[64,1536]{1,0:T(8,128)(2,1)S(1)}, bf16[64,1536]{1,0:T(8,128)(2,1)S(1)}, u32[]{:S(2)}, u32[]{:S(2)}) collective-permute-start(bf16[64,1536]{1,0:T(8,128)(2,1)S(1)} %copy-done.14), channel_id=1, source_target_pairs={{0,2},{1,3},{2,0},{3,1},{4,6},{5,7},{6,4},{7,5},{8,10},{9,11},{10,... | collective-permute-start | bytes 589832 | tf_op jit(solution)/shard_map/ppermute | solution.py:110
  30.5 12.2 %collective-permute-start.5 = (bf16[64,1536]{1,0:T(8,128)(2,1)S(1)}, bf16[64,1536]{1,0:T(8,128)(2,1)S(1)}, u32[]{:S(2)}, u32[]{:S(2)}) collective-permute-start(bf16[64,1536]{1,0:T(8,128)(2,1)S(1)} %copy-done.11), channel_id=1, source_target_pairs={{0,1},{1,2},{2,3},{3,0},{4,5},{5,6},{6,7},{7,4},{8,9},{9,10},{10,1... | collective-permute-start | bytes 589832 | tf_op jit(solution)/shard_map/ppermute | solution.py:110
  31.6 11.1 %collective-permute-start.6 = (bf16[64,1536]{1,0:T(8,128)(2,1)S(1)}, bf16[64,1536]{1,0:T(8,128)(2,1)S(1)}, u32[]{:S(2)}, u32[]{:S(2)}) collective-permute-start(bf16[64,1536]{1,0:T(8,128)(2,1)S(1)} %copy-done.9), channel_id=1, source_target_pairs={{0,3},{1,0},{2,1},{3,2},{4,7},{5,4},{6,5},{7,6},{8,11},{9,8},{10,9... | collective-permute-start | bytes 589832 | tf_op jit(solution)/shard_map/ppermute | solution.py:110
  33.7 21.6 %collective-permute-start = (bf16[64,1536]{1,0:T(8,128)(2,1)S(1)}, bf16[64,1536]{1,0:T(8,128)(2,1)S(1)}, u32[]{:S(2)}, u32[]{:S(2)}) collective-permute-start(bf16[64,1536]{1,0:T(8,128)(2,1)S(1)} %copy-done.8), channel_id=1, source_target_pairs={{0,4},{1,5},{2,6},{3,7},{4,0},{5,1},{6,2},{7,3},{8,12},{9,13},{10,... | collective-permute-start | bytes 589832 | tf_op jit(solution)/shard_map/ppermute | solution.py:110
  33.7 22.7 %collective-permute-start.1 = (bf16[64,1536]{1,0:T(8,128)(2,1)S(1)}, bf16[64,1536]{1,0:T(8,128)(2,1)S(1)}, u32[]{:S(2)}, u32[]{:S(2)}) collective-permute-start(bf16[64,1536]{1,0:T(8,128)(2,1)S(1)} %copy-done.7), channel_id=1, source_target_pairs={{0,6},{1,7},{2,4},{3,5},{4,2},{5,3},{6,0},{7,1},{8,14},{9,15},{10,... | collective-permute-start | bytes 589832 | tf_op jit(solution)/shard_map/ppermute | solution.py:110
  38.6 9.0 %copy-start.10 = (bf16[64,1536]{1,0:T(8,128)(2,1)}, bf16[64,1536]{1,0:T(8,128)(2,1)S(1)}, u32[]{:S(2)}) copy-start(bf16[64,1536]{1,0:T(8,128)(2,1)S(1)} %collective-permute-done.4.refs_1_) | copy-start | bytes 589828
  38.6 20.0 %collective-permute-start.2 = (bf16[64,1536]{1,0:T(8,128)(2,1)S(1)}, bf16[64,1536]{1,0:T(8,128)(2,1)S(1)}, u32[]{:S(2)}, u32[]{:S(2)}) collective-permute-start(bf16[64,1536]{1,0:T(8,128)(2,1)S(1)} %copy-done.6), channel_id=1, source_target_pairs={{0,5},{1,6},{2,7},{3,4},{4,1},{5,2},{6,3},{7,0},{8,13},{9,14},{10,... | collective-permute-start | bytes 589832 | tf_op jit(solution)/shard_map/ppermute | solution.py:110
  42.7 15.8 %collective-permute-start.3 = (bf16[64,1536]{1,0:T(8,128)(2,1)S(1)}, bf16[64,1536]{1,0:T(8,128)(2,1)S(1)}, u32[]{:S(2)}, u32[]{:S(2)}) collective-permute-start(bf16[64,1536]{1,0:T(8,128)(2,1)S(1)} %copy-done.5), channel_id=1, source_target_pairs={{0,7},{1,4},{2,5},{3,6},{4,3},{5,0},{6,1},{7,2},{8,15},{9,12},{10,... | collective-permute-start | bytes 589832 | tf_op jit(solution)/shard_map/ppermute | solution.py:110
  54.3 11.4 %collective-permute-start.7 = (bf16[64,1536]{1,0:T(8,128)(2,1)S(1)}, bf16[64,1536]{1,0:T(8,128)(2,1)S(1)}, u32[]{:S(2)}, u32[]{:S(2)}) collective-permute-start(bf16[64,1536]{1,0:T(8,128)(2,1)S(1)} %get-tuple-element.76), channel_id=1, source_target_pairs={{0,2},{1,3},{2,0},{3,1},{4,6},{5,7},{6,4},{7,5},{8,10},{9,11},{10,... | collective-permute-start | bytes 589832 | tf_op jit(solution)/shard_map/ppermute | solution.py:110
  55.3 10.5 %collective-permute-start.8 = (bf16[64,1536]{1,0:T(8,128)(2,1)S(1)}, bf16[64,1536]{1,0:T(8,128)(2,1)S(1)}, u32[]{:S(2)}, u32[]{:S(2)}) collective-permute-start(bf16[64,1536]{1,0:T(8,128)(2,1)S(1)} %get-tuple-element.77), channel_id=1, source_target_pairs={{0,1},{1,2},{2,3},{3,0},{4,5},{5,6},{6,7},{7,4},{8,9},{9,10},{10,1... | collective-permute-start | bytes 589832 | tf_op jit(solution)/shard_map/ppermute | solution.py:110
  56.4 9.4 %collective-permute-start.9 = (bf16[64,1536]{1,0:T(8,128)(2,1)S(1)}, bf16[64,1536]{1,0:T(8,128)(2,1)S(1)}, u32[]{:S(2)}, u32[]{:S(2)}) collective-permute-start(bf16[64,1536]{1,0:T(8,128)(2,1)S(1)} %get-tuple-element.78), channel_id=1, source_target_pairs={{0,3},{1,0},{2,1},{3,2},{4,7},{5,4},{6,5},{7,6},{8,11},{9,8},{10,9... | collective-permute-start | bytes 589832 | tf_op jit(solution)/shard_map/ppermute | solution.py:110
  65.8 23.0 %all-to-all-start.2 = ((bf16[16,256,128]{2,1,0:T(8,128)(2,1)}), bf16[16,256,128]{2,1,0:T(8,128)(2,1)S(1)}, u32[]{:S(2)}, u32[]{:S(2)}) async-start(bf16[16,256,128]{2,1,0:T(8,128)(2,1)} %get-tuple-element.79), calls=%async_computation.2 | async-start | bytes 2097152 | tf_op jit(solution)/shard_map/all_to_all | solution.py:314
  70.8 5.2 %collective-permute-start.10 = (bf16[64,1536]{1,0:T(8,128)(2,1)S(1)}, bf16[64,1536]{1,0:T(8,128)(2,1)S(1)}, u32[]{:S(2)}, u32[]{:S(2)}) collective-permute-start(bf16[64,1536]{1,0:T(8,128)(2,1)S(1)} %get-tuple-element.84), channel_id=1, source_target_pairs={{0,4},{1,5},{2,6},{3,7},{4,0},{5,1},{6,2},{7,3},{8,12},{9,13},{10,... | collective-permute-start | bytes 589832 | tf_op jit(solution)/shard_map/ppermute | solution.py:110
  70.9 8.3 %collective-permute-start.11 = (bf16[64,1536]{1,0:T(8,128)(2,1)S(1)}, bf16[64,1536]{1,0:T(8,128)(2,1)S(1)}, u32[]{:S(2)}, u32[]{:S(2)}) collective-permute-start(bf16[64,1536]{1,0:T(8,128)(2,1)S(1)} %get-tuple-element.85), channel_id=1, source_target_pairs={{0,6},{1,7},{2,4},{3,5},{4,2},{5,3},{6,0},{7,1},{8,14},{9,15},{10,... | collective-permute-start | bytes 589832 | tf_op jit(solution)/shard_map/ppermute | solution.py:110
  73.0 10.8 %collective-permute-start.12 = (bf16[64,1536]{1,0:T(8,128)(2,1)S(1)}, bf16[64,1536]{1,0:T(8,128)(2,1)S(1)}, u32[]{:S(2)}, u32[]{:S(2)}) collective-permute-start(bf16[64,1536]{1,0:T(8,128)(2,1)S(1)} %get-tuple-element.86), channel_id=1, source_target_pairs={{0,5},{1,6},{2,7},{3,4},{4,1},{5,2},{6,3},{7,0},{8,13},{9,14},{10,... | collective-permute-start | bytes 589832 | tf_op jit(solution)/shard_map/ppermute | solution.py:110
  73.0 10.8 %collective-permute-start.13 = (bf16[64,1536]{1,0:T(8,128)(2,1)S(1)}, bf16[64,1536]{1,0:T(8,128)(2,1)S(1)}, u32[]{:S(2)}, u32[]{:S(2)}) collective-permute-start(bf16[64,1536]{1,0:T(8,128)(2,1)S(1)} %get-tuple-element.87), channel_id=1, source_target_pairs={{0,7},{1,4},{2,5},{3,6},{4,3},{5,0},{6,1},{7,2},{8,15},{9,12},{10,... | collective-permute-start | bytes 589832 | tf_op jit(solution)/shard_map/ppermute | solution.py:110
  89.7 15.5 %all-to-all-start.3 = ((bf16[128,8,128]{2,1,0:T(8,128)(2,1)}), bf16[128,8,128]{2,1,0:T(8,128)(2,1)S(1)}, u32[]{:S(2)}, u32[]{:S(2)}) async-start(bf16[128,8,128]{2,1,0:T(8,128)(2,1)} %bitcast.4), calls=%async_computation.3 | async-start | bytes 524288 | tf_op jit(solution)/shard_map/all_to_all | solution.py:326
  (9 other events, 43.9 us)

commit v4 on v3

--- a/solution.py
+++ b/solution.py
@@ -119,17 +119,11 @@
     else:
         first_key, first_value, leaving, terms, refs = refs[0], refs[1], refs[2:6], refs[6], refs[7:]
     mine, out, key_all, value_all, bias, probs_all, dscores_all = refs[:7]
-    sems = refs[7]
     quarters = [
         pl.ds(pl.multiple_of(lax.rem(info[PLACE + 2] + 4 - dx, 4) * 64, 64), 64) for dx in SHIFTS
     ]
-    copies = []
-    for n, (quarter, piece) in enumerate(zip(quarters, arrived)):
-        if dc == 0:
-            copies.append(pltpu.make_async_copy(piece, mine.at[quarter, :], sems.at[n]))
-            copies[-1].start()
-        else:
-            mine[quarter, :] = piece[...]
+    for quarter, piece in zip(quarters, arrived):
+        mine[quarter, :] = piece[...]
     row = lax.broadcasted_iota(jnp.int32, (SEG, SEG), 0)
     token = lax.broadcasted_iota(jnp.int32, (SEG, SEG), 1)
     bias[:, 0:SEG] = jnp.where(token <= row, 0.0, -jnp.inf)
@@ -160,7 +154,7 @@
                     acc[8 + piece, rows, :] += value_part[first : first + 8]
 
     if dc == 1:
-        acc = refs[8]
+        acc = refs[7]
         acc[...] = jnp.zeros_like(acc)
         accumulate(lineage(0), first_key, first_value)
 
@@ -172,8 +166,6 @@
         key_all[here, :] = far[0:8, rows, :].reshape(SEG, HD)
         value_all[here, :] = far[8:16, rows, :].reshape(SEG, HD)
         bias[:, here] = jnp.where(tile < live, 0.0, -jnp.inf)
-    for copy in copies:
-        copy.wait()
     key_all[0:SEG, :] = mine[:, 2 * QW : 2 * QW + HD]
     value_all[0:SEG, :] = mine[:, 2 * QW + HD : WIDE]
 
@@ -265,8 +257,9 @@
         name="select_inner",
     )(info, pieces.reshape(NODES, 32, HD))
     far = lax.all_to_all(inner, "chip", split_axis=0, concat_axis=0, tiled=True)
-    arrived = exchange(packed, PIECES)
-    arrived[:4] = [pltpu.with_memory_space_constraint(piece, pltpu.HBM) for piece in arrived[:4]]
+    arrived = exchange(packed[:5], PIECES[:5])
+    later, arrived[1] = lax.optimization_barrier((packed[5:], arrived[1]))
+    arrived += exchange(later, PIECES[5:])
 
     half = jax.ShapeDtypeStruct((4 * SEG, HD), F32)
 
@@ -282,7 +275,6 @@
             pltpu.VMEM((SEG, 4 * SEG), F32),
             pltpu.VMEM((GROUP * SEG, 4 * SEG), BF),
             pltpu.VMEM((GROUP * SEG, 4 * SEG), BF),
-            pltpu.SemaphoreType.DMA((4,)),
         ]
         if last:
             out_shape += (jax.ShapeDtypeStruct((CHIPS, INNER * 32, HD), BF),)
@@ -294,7 +286,7 @@
         return pl.pallas_call(
             functools.partial(attention_kernel, dc),
             out_shape=out_shape,
-            in_specs=[smem(), vmem()] + ([vmem()] * 6 if last else [hbm()] * 4),
+            in_specs=[smem()] + [vmem()] * (7 if last else 5),
             out_specs=out_specs,
             scratch_shapes=scratch_shapes,
             compiler_params=pltpu.CompilerParams(vmem_limit_bytes=20 * MIB),
@@ -312,7 +304,8 @@
     terms, first_back = lax.optimization_barrier((terms, first_back))
 
     parts = lax.all_to_all(terms, "chip", split_axis=0, concat_axis=0, tiled=True)
-    back = first_back + exchange(others, PIECES[4:])
+    far_back = exchange(others[1:], PIECES[5:])
+    back = first_back + exchange(others[:1], PIECES[4:5]) + far_back
     parts, back = lax.optimization_barrier((parts, back))
     sums = pl.pallas_call(
         sum_kernel,

time: 108 us -> 105 us (0.972)
  starting transfers between devices: 40.1 us -> 38.9 us
  Pallas kernels: 19.5 us -> 18.3 us
    pallas_call x2, Pallas kernels: 14 us -> 12.8 us  [attend(): pl.pallas_call(functools.partial(attention_kernel, dc), out_shape=out_sha...]
    all_to_all x1, starting transfers between devices: 4.98 us -> 3.83 us  [on_device(): lax.all_to_all(terms, 'chip', split_axis=0, concat_axis=0, tiled=True)]
where the time goes in v4:
time: 105 us; the launch traced here: 103 us
  waiting for transfers between devices  39.6 us (38%)
  starting transfers between devices  38.9 us (37%)
  Pallas kernels  18.3 us (17%)
  other arithmetic  2.48 us (2%)
  local copies, waits for them, and re-layouts  2.36 us (2%)
  between operations  1.46 us (1%)
    ppermute x14, starting transfers between devices, exchange(): piece = lax.ppermute(piece, GROUP_AXES, pairs)  15.5 us
    ppermute x14, waiting for transfers between devices, exchange(): piece = lax.ppermute(piece, GROUP_AXES, pairs)  14.5 us
    pallas_call x2, Pallas kernels, attend(): pl.pallas_call(functools.partial(attention_kernel, dc), out_shape=out_sha...  12.8 us
    all_to_all x1, starting transfers between devices, on_device(): lax.all_to_all(pieces, ALL, split_axis=0, concat_axis=0, tiled=True)  11.1 us
    all_to_all x1, waiting for transfers between devices, on_device(): sums = lax.all_to_all(sums, ALL, split_axis=0, concat_axis=0, tiled=True)  7.31 us
    all_to_all x1, waiting for transfers between devices, on_device(): lax.all_to_all(pieces, ALL, split_axis=0, concat_axis=0, tiled=True)  7.28 us
    all_to_all x1, waiting for transfers between devices, on_device(): far = lax.all_to_all(inner, 'chip', split_axis=0, concat_axis=0, tiled=True)  5.56 us
    all_to_all x1, waiting for transfers between devices, on_device(): lax.all_to_all(terms, 'chip', split_axis=0, concat_axis=0, tiled=True)  4.91 us
  transfers between devices with their start and end apart: 18, of which 8 were waited for; matrix products, arithmetic and copies ran while one was open for 1% of the time, Pallas kernels for 16%

profile of v4, /device:TPU:0, one launch (start us, length us, event | category | flops | bytes accessed | tf_op | source)
XLA Modules:
  0.0 103.1 jit_solution(12016601196995103098)
XLA Ops:
  0.6 1.8 %pad_maximum_fusion = bf16[128,1024]{1,0:T(8,128)(2,1)} fusion(bf16[64,1024]{1,0:T(8,128)(2,1)} %values.1, bf16[64,1024]{1,0:T(8,128)(2,1)} %keys.1), kind=kLoop, calls=%fused_computation | loop fusion | flops 524288 | bytes 524288 | tf_op jit(solution)/shard_map/concatenate | solution.py:238
  2.4 11.1 %all-to-all-start = ((bf16[128,8,128]{2,1,0:T(8,128)(2,1)}), bf16[128,8,128]{2,1,0:T(8,128)(2,1)S(1)}, u32[]{:S(2)}, u32[]{:S(2)}) async-start(bf16[128,8,128]{2,1,0:T(8,128)(2,1)} %bitcast.2), calls=%async_computation | async-start | bytes 524288 | tf_op jit(solution)/shard_map/all_to_all | solution.py:240
  15.5 1.3 %pack.1 = (bf16[64,1536]{1,0:T(8,128)(2,1)}, bf16[64,1536]{1,0:T(8,128)(2,1)}, bf16[64,1536]{1,0:T(8,128)(2,1)}, bf16[64,1536]{1,0:T(8,128)(2,1)}, bf16[64,1536]...) custom-call(s32[131]{0:T(256)S(4)} %info.1, ...), custom_call_target="tpu_custom_call" | custom-call | tf_op jit(solution)/shard_map/pack/pallas_call | solution.py:242
  16.8 7.3 %all-to-all-done = bf16[128,8,128]{2,1,0:T(8,128)(2,1)S(1)} async-done(((bf16[128,8,128]{2,1,0:T(8,128)(2,1)}), bf16[128,8,128]{2,1,0:T(8,128)(2,1)S(1)}, u32[]{:S(2)}, u32[]{:S(2)}) %all-to-all-start) | async-done | bytes 262176 | tf_op jit(solution)/shard_map/all_to_all | solution.py:240
  24.1 1.2 %select_inner.1 = bf16[16,256,128]{2,1,0:T(8,128)(2,1)} custom-call(s32[131]{0:T(256)S(4)} %info.1, bf16[32,32,128]{2,1,0:T(8,128)(2,1)S(1)} %bitcast.19), custom_call_target="tpu_custom_call" | custom-call | tf_op jit(solution)/shard_map/select_inner/pallas_call | solution.py:251
  25.3 3.9 %all-to-all-start.1 = ((bf16[16,256,128]{2,1,0:T(8,128)(2,1)}), bf16[16,256,128]{2,1,0:T(8,128)(2,1)S(1)}, u32[]{:S(2)}, u32[]{:S(2)}) async-start(bf16[16,256,128]{2,1,0:T(8,128)(2,1)} %select_inner.1), calls=%async_computation.1 | async-start | bytes 2097152 | tf_op jit(solution)/shard_map/all_to_all | solution.py:259
  29.2 1.3 %collective-permute-start.1 = (bf16[64,1536]{1,0:T(8,128)(2,1)S(1)}, bf16[64,1536]{1,0:T(8,128)(2,1)S(1)}, u32[]{:S(2)}, u32[]{:S(2)}) collective-permute-start(bf16[64,1536]{1,0:T(8,128)(2,1)S(1)} %copy-done.11), channel_id=1, source_target_pairs={{0,2},{1,3},{2,0},{3,1},{4,6},{5,7},{6,4},{7,5},{8,10},{9,11},{10,... | collective-permute-start | bytes 589832 | tf_op jit(solution)/shard_map/ppermute | solution.py:110
  31.6 2.1 %collective-permute-start.6 = (bf16[64,1536]{1,0:T(8,128)(2,1)S(1)}, bf16[64,1536]{1,0:T(8,128)(2,1)S(1)}, u32[]{:S(2)}, u32[]{:S(2)}) collective-permute-start(bf16[64,1536]{1,0:T(8,128)(2,1)S(1)} %copy-done.9), channel_id=1, source_target_pairs={{0,3},{1,0},{2,1},{3,2},{4,7},{5,4},{6,5},{7,6},{8,11},{9,8},{10,9... | collective-permute-start | bytes 589832 | tf_op jit(solution)/shard_map/ppermute | solution.py:110
  33.7 4.8 %collective-permute-done.1.refs_1_ = bf16[64,1536]{1,0:T(8,128)(2,1)S(1)} collective-permute-done((bf16[64,1536]{1,0:T(8,128)(2,1)S(1)}, bf16[64,1536]{1,0:T(8,128)(2,1)S(1)}, u32[]{:S(2)}, u32[]{:S(2)}) %collective-permute-start.1) | collective-permute-done | bytes 196640 | tf_op jit(solution)/shard_map/ppermute | solution.py:110
  38.5 2.1 %collective-permute-start.3 = (bf16[64,1536]{1,0:T(8,128)(2,1)S(1)}, bf16[64,1536]{1,0:T(8,128)(2,1)S(1)}, u32[]{:S(2)}, u32[]{:S(2)}) collective-permute-start(bf16[64,1536]{1,0:T(8,128)(2,1)S(1)} %copy-done.7), channel_id=1, source_target_pairs={{0,5},{1,6},{2,7},{3,4},{4,1},{5,2},{6,3},{7,0},{8,13},{9,14},{10,... | collective-permute-start | bytes 589832 | tf_op jit(solution)/shard_map/ppermute | solution.py:110
  40.6 1.3 %collective-permute-done.5.refs_2_ = bf16[64,1536]{1,0:T(8,128)(2,1)S(1)} collective-permute-done((bf16[64,1536]{1,0:T(8,128)(2,1)S(1)}, bf16[64,1536]{1,0:T(8,128)(2,1)S(1)}, u32[]{:S(2)}, u32[]{:S(2)}) %collective-permute-start.5) | collective-permute-done | bytes 196640 | tf_op jit(solution)/shard_map/ppermute | solution.py:110
  42.0 5.6 %all-to-all-done.1.far = bf16[16,256,128]{2,1,0:T(8,128)(2,1)S(1)} async-done(((bf16[16,256,128]{2,1,0:T(8,128)(2,1)}), bf16[16,256,128]{2,1,0:T(8,128)(2,1)S(1)}, u32[]{:S(2)}, u32[]{:S(2)}) %all-to-all-start.1) | async-done | bytes 1048608 | tf_op jit(solution)/shard_map/all_to_all | solution.py:259
  47.5 5.6 %attention.2 = (bf16[64,1536]{1,0:T(8,128)(2,1)S(1)}, bf16[64,1536]{1,0:T(8,128)(2,1)S(1)}, bf16[64,1536]{1,0:T(8,128)(2,1)S(1)}, bf16[64,1536]{1,0:T(8,128)(2,1...) custom-call(s32[131]{0:T(256)S(4)} %info.1, bf16[16,256,128]{2,1,0:T(8,128)(2,1)S(1)} %all-to-all-done.1.far, ...), custom_call_target="tpu_custom_call" | custom-call | flops 6710886400 | bytes 6291456 | tf_op jit(solution)/shard_map/attention/pallas_call | solution.py:286
  55.2 2.1 %collective-permute-start.9 = (bf16[64,1536]{1,0:T(8,128)(2,1)S(1)}, bf16[64,1536]{1,0:T(8,128)(2,1)S(1)}, u32[]{:S(2)}, u32[]{:S(2)}) collective-permute-start(bf16[64,1536]{1,0:T(8,128)(2,1)S(1)} %get-tuple-element.86), channel_id=1, source_target_pairs={{0,3},{1,0},{2,1},{3,2},{4,7},{5,4},{6,5},{7,6},{8,11},{9,8},{10,9... | collective-permute-start | bytes 589832 | tf_op jit(solution)/shard_map/ppermute | solution.py:110
  57.3 7.2 %attention.3 = (bf16[64,1536]{1,0:T(8,128)(2,1)S(1)}, bf16[64,1536]{1,0:T(8,128)(2,1)S(1)}, bf16[64,1536]{1,0:T(8,128)(2,1)S(1)}, bf16[64,1536]{1,0:T(8,128)(2,1)S(1)}, bf16[16,256,128]{2,1,0:T(8,128)(2,1)}) custom-call(s32[131]{0:T(256)S(4)} %info.1, bf16[16,256,128]{2,1,0:T(8,128)(2,1)S(1)} %all-to-all-done.1.far, ...), custom_call_target="tpu_custom_call" | custom-call | flops 6710886400 | bytes 6291456 | tf_op jit(solution)/shard_map/attention/pallas_call | solution.py:286
  64.5 3.8 %all-to-all-start.2 = ((bf16[16,256,128]{2,1,0:T(8,128)(2,1)}), bf16[16,256,128]{2,1,0:T(8,128)(2,1)S(1)}, u32[]{:S(2)}, u32[]{:S(2)}) async-start(bf16[16,256,128]{2,1,0:T(8,128)(2,1)} %get-tuple-element.87), calls=%async_computation.2 | async-start | bytes 2097152 | tf_op jit(solution)/shard_map/all_to_all | solution.py:306
  68.5 1.6 %collective-permute-start.11 = (bf16[64,1536]{1,0:T(8,128)(2,1)S(1)}, bf16[64,1536]{1,0:T(8,128)(2,1)S(1)}, u32[]{:S(2)}, u32[]{:S(2)}) collective-permute-start(bf16[64,1536]{1,0:T(8,128)(2,1)S(1)} %get-tuple-element.93), channel_id=1, source_target_pairs={{0,6},{1,7},{2,4},{3,5},{4,2},{5,3},{6,0},{7,1},{8,14},{9,15},{10,... | collective-permute-start | bytes 589832 | tf_op jit(solution)/shard_map/ppermute | solution.py:110
  70.2 2.8 %collective-permute-start.13 = (bf16[64,1536]{1,0:T(8,128)(2,1)S(1)}, bf16[64,1536]{1,0:T(8,128)(2,1)S(1)}, u32[]{:S(2)}, u32[]{:S(2)}) collective-permute-start(bf16[64,1536]{1,0:T(8,128)(2,1)S(1)} %get-tuple-element.95), channel_id=1, source_target_pairs={{0,7},{1,4},{2,5},{3,6},{4,3},{5,0},{6,1},{7,2},{8,15},{9,12},{10,... | collective-permute-start | bytes 589832 | tf_op jit(solution)/shard_map/ppermute | solution.py:110
  73.1 3.7 %collective-permute-done.11.refs_5_ = bf16[64,1536]{1,0:T(8,128)(2,1)S(1)} collective-permute-done((bf16[64,1536]{1,0:T(8,128)(2,1)S(1)}, bf16[64,1536]{1,0:T(8,128)(2,1)S(1)}, u32[]{:S(2)}, u32[]{:S(2)}) %collective-permute-start.11) | collective-permute-done | bytes 196640 | tf_op jit(solution)/shard_map/ppermute | solution.py:110
  76.8 4.7 %collective-permute-done.12.refs_6_ = bf16[64,1536]{1,0:T(8,128)(2,1)S(1)} collective-permute-done((bf16[64,1536]{1,0:T(8,128)(2,1)S(1)}, bf16[64,1536]{1,0:T(8,128)(2,1)S(1)}, u32[]{:S(2)}, u32[]{:S(2)}) %collective-permute-start.12) | collective-permute-done | bytes 196640 | tf_op jit(solution)/shard_map/ppermute | solution.py:110
  81.4 4.9 %all-to-all-done.2.parts = bf16[16,256,128]{2,1,0:T(8,128)(2,1)S(1)} async-done(((bf16[16,256,128]{2,1,0:T(8,128)(2,1)}), bf16[16,256,128]{2,1,0:T(8,128)(2,1)S(1)}, u32[]{:S(2)}, u32[]{:S(2)}) %all-to-all-start.2) | async-done | bytes 1048608 | tf_op jit(solution)/shard_map/all_to_all | solution.py:306
  87.2 4.6 %all-to-all-start.3 = ((bf16[128,8,128]{2,1,0:T(8,128)(2,1)}), bf16[128,8,128]{2,1,0:T(8,128)(2,1)S(1)}, u32[]{:S(2)}, u32[]{:S(2)}) async-start(bf16[128,8,128]{2,1,0:T(8,128)(2,1)} %bitcast.4), calls=%async_computation.3 | async-start | bytes 524288 | tf_op jit(solution)/shard_map/all_to_all | solution.py:319
  93.7 1.3 %unpack.1 = (bf16[64,5120]{1,0:T(8,128)(2,1)}, bf16[64,5120]{1,0:T(8,128)(2,1)}, bf16[64,1024]{1,0:T(8,128)(2,1)S(1)}, bf16[64,1024]{1,0:T(8,128)(2,1)S(1)}) custom-call(s32[131]{0:T(256)S(4)} %info.1, bf16[64,1536]{1,0:T(8,128)(2,1)S(1)} %get-tuple-element.97.refs_0_, bf16[64,1536]{1,0:T(8,128)(2,1)S(1)} %collective-permute-done.7.refs_1_, ...), custom_call_target="tpu_custom_call" | custom-call | tf_op jit(solution)/shard_map/unpack/pallas_call | solution.py:323
  95.0 7.3 %all-to-all-done.3 = bf16[128,8,128]{2,1,0:T(8,128)(2,1)S(1)} async-done(((bf16[128,8,128]{2,1,0:T(8,128)(2,1)}), bf16[128,8,128]{2,1,0:T(8,128)(2,1)S(1)}, u32[]{:S(2)}, u32[]{:S(2)}) %all-to-all-start.3) | async-done | bytes 262176 | tf_op jit(solution)/shard_map/all_to_all | solution.py:319
  (46 shorter events, 8.3 us)
Async XLA Ops:
  0.6 13.7 %copy-start = (bf16[64,5120]{1,0:T(8,128)(2,1)S(1)}, bf16[64,5120]{1,0:T(8,128)(2,1)}, u32[]{:S(2)}) copy-start(bf16[64,5120]{1,0:T(8,128)(2,1)} %queries.1) | copy-start | bytes 1966084
  2.4 12.0 %copy-start.3 = (bf16[64,1024]{1,0:T(8,128)(2,1)S(1)}, bf16[64,1024]{1,0:T(8,128)(2,1)}, u32[]{:S(2)}) copy-start(bf16[64,1024]{1,0:T(8,128)(2,1)} %keys.1) | copy-start | bytes 393220
  2.4 21.7 %all-to-all-start = ((bf16[128,8,128]{2,1,0:T(8,128)(2,1)}), bf16[128,8,128]{2,1,0:T(8,128)(2,1)S(1)}, u32[]{:S(2)}, u32[]{:S(2)}) async-start(bf16[128,8,128]{2,1,0:T(8,128)(2,1)} %bitcast.2), calls=%async_computation | async-start | bytes 524288 | tf_op jit(solution)/shard_map/all_to_all | solution.py:240
  25.2 13.3 %copy-start.8 = (bf16[64,1536]{1,0:T(8,128)(2,1)S(1)}, bf16[64,1536]{1,0:T(8,128)(2,1)}, u32[]{:S(2)}) copy-start(bf16[64,1536]{1,0:T(8,128)(2,1)} %get-tuple-element.73) | copy-start | bytes 589828
  25.3 13.3 %copy-start.7 = (bf16[64,1536]{1,0:T(8,128)(2,1)S(1)}, bf16[64,1536]{1,0:T(8,128)(2,1)}, u32[]{:S(2)}) copy-start(bf16[64,1536]{1,0:T(8,128)(2,1)} %get-tuple-element.74) | copy-start | bytes 589828
  25.3 16.7 %copy-start.6 = (bf16[64,1536]{1,0:T(8,128)(2,1)S(1)}, bf16[64,1536]{1,0:T(8,128)(2,1)}, u32[]{:S(2)}) copy-start(bf16[64,1536]{1,0:T(8,128)(2,1)} %get-tuple-element.75) | copy-start | bytes 589828
  25.3 22.2 %copy-start.4 = (bf16[64,1536]{1,0:T(8,128)(2,1)S(1)}, bf16[64,1536]{1,0:T(8,128)(2,1)}, u32[]{:S(2)}) copy-start(bf16[64,1536]{1,0:T(8,128)(2,1)} %get-tuple-element.76.refs_0_) | copy-start | bytes 589828
  25.3 22.2 %all-to-all-start.1 = ((bf16[16,256,128]{2,1,0:T(8,128)(2,1)}), bf16[16,256,128]{2,1,0:T(8,128)(2,1)S(1)}, u32[]{:S(2)}, u32[]{:S(2)}) async-start(bf16[16,256,128]{2,1,0:T(8,128)(2,1)} %select_inner.1), calls=%async_computation.1 | async-start | bytes 2097152 | tf_op jit(solution)/shard_map/all_to_all | solution.py:259
  29.2 9.4 %collective-permute-start.1 = (bf16[64,1536]{1,0:T(8,128)(2,1)S(1)}, bf16[64,1536]{1,0:T(8,128)(2,1)S(1)}, u32[]{:S(2)}, u32[]{:S(2)}) collective-permute-start(bf16[64,1536]{1,0:T(8,128)(2,1)S(1)} %copy-done.11), channel_id=1, source_target_pairs={{0,2},{1,3},{2,0},{3,1},{4,6},{5,7},{6,4},{7,5},{8,10},{9,11},{10,... | collective-permute-start | bytes 589832 | tf_op jit(solution)/shard_map/ppermute | solution.py:110
  30.5 11.5 %collective-permute-start.5 = (bf16[64,1536]{1,0:T(8,128)(2,1)S(1)}, bf16[64,1536]{1,0:T(8,128)(2,1)S(1)}, u32[]{:S(2)}, u32[]{:S(2)}) collective-permute-start(bf16[64,1536]{1,0:T(8,128)(2,1)S(1)} %copy-done.10), channel_id=1, source_target_pairs={{0,1},{1,2},{2,3},{3,0},{4,5},{5,6},{6,7},{7,4},{8,9},{9,10},{10,1... | collective-permute-start | bytes 589832 | tf_op jit(solution)/shard_map/ppermute | solution.py:110
  31.6 10.3 %collective-permute-start.6 = (bf16[64,1536]{1,0:T(8,128)(2,1)S(1)}, bf16[64,1536]{1,0:T(8,128)(2,1)S(1)}, u32[]{:S(2)}, u32[]{:S(2)}) collective-permute-start(bf16[64,1536]{1,0:T(8,128)(2,1)S(1)} %copy-done.9), channel_id=1, source_target_pairs={{0,3},{1,0},{2,1},{3,2},{4,7},{5,4},{6,5},{7,6},{8,11},{9,8},{10,9... | collective-permute-start | bytes 589832 | tf_op jit(solution)/shard_map/ppermute | solution.py:110
  33.7 20.4 %collective-permute-start = (bf16[64,1536]{1,0:T(8,128)(2,1)}, bf16[64,1536]{1,0:T(8,128)(2,1)S(1)}, u32[]{:S(2)}, u32[]{:S(2)}) collective-permute-start(bf16[64,1536]{1,0:T(8,128)(2,1)} %get-tuple-element.68), channel_id=1, source_target_pairs={{0,4},{1,5},{2,6},{3,7},{4,0},{5,1},{6,2},{7,3},{8,12},{9,13},{10,... | collective-permute-start | bytes 589832 | tf_op jit(solution)/shard_map/ppermute | solution.py:110
  38.5 16.7 %collective-permute-start.2 = (bf16[64,1536]{1,0:T(8,128)(2,1)S(1)}, bf16[64,1536]{1,0:T(8,128)(2,1)S(1)}, u32[]{:S(2)}, u32[]{:S(2)}) collective-permute-start(bf16[64,1536]{1,0:T(8,128)(2,1)S(1)} %copy-done.8), channel_id=1, source_target_pairs={{0,6},{1,7},{2,4},{3,5},{4,2},{5,3},{6,0},{7,1},{8,14},{9,15},{10,... | collective-permute-start | bytes 589832 | tf_op jit(solution)/shard_map/ppermute | solution.py:110
  38.5 18.8 %collective-permute-start.3 = (bf16[64,1536]{1,0:T(8,128)(2,1)S(1)}, bf16[64,1536]{1,0:T(8,128)(2,1)S(1)}, u32[]{:S(2)}, u32[]{:S(2)}) collective-permute-start(bf16[64,1536]{1,0:T(8,128)(2,1)S(1)} %copy-done.7), channel_id=1, source_target_pairs={{0,5},{1,6},{2,7},{3,4},{4,1},{5,2},{6,3},{7,0},{8,13},{9,14},{10,... | collective-permute-start | bytes 589832 | tf_op jit(solution)/shard_map/ppermute | solution.py:110
  42.0 15.4 %collective-permute-start.4 = (bf16[64,1536]{1,0:T(8,128)(2,1)S(1)}, bf16[64,1536]{1,0:T(8,128)(2,1)S(1)}, u32[]{:S(2)}, u32[]{:S(2)}) collective-permute-start(bf16[64,1536]{1,0:T(8,128)(2,1)S(1)} %copy-done.6), channel_id=1, source_target_pairs={{0,7},{1,4},{2,5},{3,6},{4,3},{5,0},{6,1},{7,2},{8,15},{9,12},{10,... | collective-permute-start | bytes 589832 | tf_op jit(solution)/shard_map/ppermute | solution.py:110
  53.1 11.4 %collective-permute-start.7 = (bf16[64,1536]{1,0:T(8,128)(2,1)S(1)}, bf16[64,1536]{1,0:T(8,128)(2,1)S(1)}, u32[]{:S(2)}, u32[]{:S(2)}) collective-permute-start(bf16[64,1536]{1,0:T(8,128)(2,1)S(1)} %get-tuple-element.84), channel_id=1, source_target_pairs={{0,2},{1,3},{2,0},{3,1},{4,6},{5,7},{6,4},{7,5},{8,10},{9,11},{10,... | collective-permute-start | bytes 589832 | tf_op jit(solution)/shard_map/ppermute | solution.py:110
  54.1 10.4 %collective-permute-start.8 = (bf16[64,1536]{1,0:T(8,128)(2,1)S(1)}, bf16[64,1536]{1,0:T(8,128)(2,1)S(1)}, u32[]{:S(2)}, u32[]{:S(2)}) collective-permute-start(bf16[64,1536]{1,0:T(8,128)(2,1)S(1)} %get-tuple-element.85), channel_id=1, source_target_pairs={{0,1},{1,2},{2,3},{3,0},{4,5},{5,6},{6,7},{7,4},{8,9},{9,10},{10,1... | collective-permute-start | bytes 589832 | tf_op jit(solution)/shard_map/ppermute | solution.py:110
  55.2 9.3 %collective-permute-start.9 = (bf16[64,1536]{1,0:T(8,128)(2,1)S(1)}, bf16[64,1536]{1,0:T(8,128)(2,1)S(1)}, u32[]{:S(2)}, u32[]{:S(2)}) collective-permute-start(bf16[64,1536]{1,0:T(8,128)(2,1)S(1)} %get-tuple-element.86), channel_id=1, source_target_pairs={{0,3},{1,0},{2,1},{3,2},{4,7},{5,4},{6,5},{7,6},{8,11},{9,8},{10,9... | collective-permute-start | bytes 589832 | tf_op jit(solution)/shard_map/ppermute | solution.py:110
  64.5 21.8 %all-to-all-start.2 = ((bf16[16,256,128]{2,1,0:T(8,128)(2,1)}), bf16[16,256,128]{2,1,0:T(8,128)(2,1)S(1)}, u32[]{:S(2)}, u32[]{:S(2)}) async-start(bf16[16,256,128]{2,1,0:T(8,128)(2,1)} %get-tuple-element.87), calls=%async_computation.2 | async-start | bytes 2097152 | tf_op jit(solution)/shard_map/all_to_all | solution.py:306
  68.4 4.7 %collective-permute-start.10 = (bf16[64,1536]{1,0:T(8,128)(2,1)S(1)}, bf16[64,1536]{1,0:T(8,128)(2,1)S(1)}, u32[]{:S(2)}, u32[]{:S(2)}) collective-permute-start(bf16[64,1536]{1,0:T(8,128)(2,1)S(1)} %get-tuple-element.92), channel_id=1, source_target_pairs={{0,4},{1,5},{2,6},{3,7},{4,0},{5,1},{6,2},{7,3},{8,12},{9,13},{10,... | collective-permute-start | bytes 589832 | tf_op jit(solution)/shard_map/ppermute | solution.py:110
  68.5 8.3 %collective-permute-start.11 = (bf16[64,1536]{1,0:T(8,128)(2,1)S(1)}, bf16[64,1536]{1,0:T(8,128)(2,1)S(1)}, u32[]{:S(2)}, u32[]{:S(2)}) collective-permute-start(bf16[64,1536]{1,0:T(8,128)(2,1)S(1)} %get-tuple-element.93), channel_id=1, source_target_pairs={{0,6},{1,7},{2,4},{3,5},{4,2},{5,3},{6,0},{7,1},{8,14},{9,15},{10,... | collective-permute-start | bytes 589832 | tf_op jit(solution)/shard_map/ppermute | solution.py:110
  70.1 11.3 %collective-permute-start.12 = (bf16[64,1536]{1,0:T(8,128)(2,1)S(1)}, bf16[64,1536]{1,0:T(8,128)(2,1)S(1)}, u32[]{:S(2)}, u32[]{:S(2)}) collective-permute-start(bf16[64,1536]{1,0:T(8,128)(2,1)S(1)} %get-tuple-element.94), channel_id=1, source_target_pairs={{0,5},{1,6},{2,7},{3,4},{4,1},{5,2},{6,3},{7,0},{8,13},{9,14},{10,... | collective-permute-start | bytes 589832 | tf_op jit(solution)/shard_map/ppermute | solution.py:110
  70.2 11.2 %collective-permute-start.13 = (bf16[64,1536]{1,0:T(8,128)(2,1)S(1)}, bf16[64,1536]{1,0:T(8,128)(2,1)S(1)}, u32[]{:S(2)}, u32[]{:S(2)}) collective-permute-start(bf16[64,1536]{1,0:T(8,128)(2,1)S(1)} %get-tuple-element.95), channel_id=1, source_target_pairs={{0,7},{1,4},{2,5},{3,6},{4,3},{5,0},{6,1},{7,2},{8,15},{9,12},{10,... | collective-permute-start | bytes 589832 | tf_op jit(solution)/shard_map/ppermute | solution.py:110
  87.2 15.1 %all-to-all-start.3 = ((bf16[128,8,128]{2,1,0:T(8,128)(2,1)}), bf16[128,8,128]{2,1,0:T(8,128)(2,1)S(1)}, u32[]{:S(2)}, u32[]{:S(2)}) async-start(bf16[128,8,128]{2,1,0:T(8,128)(2,1)} %bitcast.4), calls=%async_computation.3 | async-start | bytes 524288 | tf_op jit(solution)/shard_map/all_to_all | solution.py:319
  (6 other events, 29.2 us)

commit v5 on v4

--- a/solution.py
+++ b/solution.py
@@ -22,7 +22,6 @@
 BF = jnp.bfloat16
 F32 = jnp.float32
 MIB = 1024 * 1024
-LOG2_E = 1.4426950408889634
 
 PARENT, NODE_OF_SLOT, LIVE_TILES, SLOT_OF_NODE, PLACE = 0, 32, 64, 96, 128
 INFO_SIZE = 131
@@ -137,26 +136,21 @@
             chain.append(jnp.where(current >= 0, info[PARENT + jnp.maximum(current, 0)], -1))
         return chain
 
-    def accumulate(chain, key_part, value_part):
+    def accumulate(chain, part, first):
         for step in range(1, 4):
             rows = pl.ds(pl.multiple_of(jnp.maximum(chain[step], 0) * 32, 32), 32)
             here = slice(step * SEG, (step + 1) * SEG)
-            acc[0:8, rows, :] += key_part[here].reshape(8, 32, HD)
-            acc[8:16, rows, :] += value_part[here].reshape(8, 32, HD)
-
-        @pl.when(chain[0] < INNER)
-        def _():
-            for piece in range(8):
-                for quarter in range(4):
-                    first = quarter * 64 + piece * 8
-                    rows = pl.ds(pl.multiple_of(chain[0] * 32 + quarter * 8, 8), 8)
-                    acc[piece, rows, :] += key_part[first : first + 8]
-                    acc[8 + piece, rows, :] += value_part[first : first + 8]
+            acc[first : first + 8, rows, :] += part[here].reshape(8, 32, HD)
+        rows = pl.ds(pl.multiple_of(jnp.minimum(chain[0], INNER) * 32, 32), 32)
+        own = part[0:SEG].reshape(4, 8, 8, HD)
+        for piece in range(8):
+            acc[first + piece, rows, :] += own[:, piece].reshape(32, HD)
 
     if dc == 1:
         acc = refs[7]
         acc[...] = jnp.zeros_like(acc)
-        accumulate(lineage(0), first_key, first_value)
+        accumulate(lineage(0), first_key[...], 0)
+        accumulate(lineage(0), first_value[...], 8)
 
     for step, node in enumerate(lineage(dc)[1:], 1):
         safe = jnp.maximum(node, 0)
@@ -180,11 +174,11 @@
         grad = mine[:, grad_columns]
         queries_t.append(query.T)
         grads_t.append(grad.T)
-        scores = nt_dot(query, keys) * (SCALE * LOG2_E) + bias[...]
+        scores = nt_dot(query, keys) * SCALE + bias[...]
         peak = jnp.max(scores, axis=1, keepdims=True)
-        weight = jnp.exp2(scores - peak)
+        weight = jnp.exp(scores - peak)
         total = jnp.sum(weight, axis=1, keepdims=True)
-        probs = weight * (1.0 / total)
+        probs = weight * jnp.exp(peak - (peak + jnp.log(total)))
         probs_b = probs.astype(BF)
         attended = nn_dot(probs_b, values).astype(BF)
         out[:, columns] = attended
@@ -195,8 +189,8 @@
         out[:, grad_columns] = query_grad.astype(BF)
         probs_all[g * SEG : (g + 1) * SEG, :] = probs_b
         dscores_all[g * SEG : (g + 1) * SEG, :] = dscores
+    value_terms = nn_dot(jnp.concatenate(grads_t, 1), probs_all[...]).T
     key_terms = nn_dot(jnp.concatenate(queries_t, 1), dscores_all[...]).T * SCALE
-    value_terms = nn_dot(jnp.concatenate(grads_t, 1), probs_all[...]).T
     out[:, 2 * QW : 2 * QW + HD] = key_terms[0:SEG].astype(BF)
     out[:, 2 * QW + HD : WIDE] = value_terms[0:SEG].astype(BF)
     quarters = [
@@ -209,8 +203,9 @@
         key_out[...] = key_terms
         value_out[...] = value_terms
     else:
-        accumulate(lineage(1), key_terms, value_terms)
-        terms[...] = acc[...].astype(BF)
+        accumulate(lineage(1), value_terms, 8)
+        accumulate(lineage(1), key_terms, 0)
+        terms[...] = acc[:, 0 : INNER * 32, :].astype(BF)
 
 
 def sum_kernel(info, parts, out):
@@ -279,7 +274,7 @@
         if last:
             out_shape += (jax.ShapeDtypeStruct((CHIPS, INNER * 32, HD), BF),)
             out_specs += (vmem(),)
-            scratch_shapes.append(pltpu.VMEM((CHIPS, INNER * 32, HD), F32))
+            scratch_shapes.append(pltpu.VMEM((CHIPS, (INNER + 1) * 32, HD), F32))
         else:
             out_shape += (half, half)
             out_specs += (vmem(), vmem())

time: 105 us -> 105 us (level)
  no operation moved by 1% of the time
where the time goes in v5:
time: 105 us; the launch traced here: 103 us
  waiting for transfers between devices  39.6 us (38%)
  starting transfers between devices  39 us (37%)
  Pallas kernels  18.4 us (18%)
  other arithmetic  2.48 us (2%)
  local copies, waits for them, and re-layouts  2.36 us (2%)
  between operations  1.46 us (1%)
    ppermute x14, starting transfers between devices, exchange(): piece = lax.ppermute(piece, GROUP_AXES, pairs)  15.4 us
    ppermute x14, waiting for transfers between devices, exchange(): piece = lax.ppermute(piece, GROUP_AXES, pairs)  14.5 us
    pallas_call x2, Pallas kernels, attend(): pl.pallas_call(functools.partial(attention_kernel, dc), out_shape=out_sha...  12.9 us
    all_to_all x1, starting transfers between devices, on_device(): lax.all_to_all(pieces, ALL, split_axis=0, concat_axis=0, tiled=True)  11.1 us
    all_to_all x1, waiting for transfers between devices, on_device(): sums = lax.all_to_all(sums, ALL, split_axis=0, concat_axis=0, tiled=True)  7.31 us
    all_to_all x1, waiting for transfers between devices, on_device(): lax.all_to_all(pieces, ALL, split_axis=0, concat_axis=0, tiled=True)  7.28 us
    all_to_all x1, waiting for transfers between devices, on_device(): far = lax.all_to_all(inner, 'chip', split_axis=0, concat_axis=0, tiled=True)  5.56 us
    all_to_all x1, waiting for transfers between devices, on_device(): lax.all_to_all(terms, 'chip', split_axis=0, concat_axis=0, tiled=True)  4.91 us
  transfers between devices with their start and end apart: 18, of which 8 were waited for; matrix products, arithmetic and copies ran while one was open for 1% of the time, Pallas kernels for 16%

profile of v5, /device:TPU:0, one launch (start us, length us, event | category | flops | bytes accessed | tf_op | source)
XLA Modules:
  0.0 103.3 jit_solution(17175883815600188392)
XLA Ops:
  0.6 1.8 %pad_maximum_fusion = bf16[128,1024]{1,0:T(8,128)(2,1)} fusion(bf16[64,1024]{1,0:T(8,128)(2,1)} %values.1, bf16[64,1024]{1,0:T(8,128)(2,1)} %keys.1), kind=kLoop, calls=%fused_computation | loop fusion | flops 524288 | bytes 524288 | tf_op jit(solution)/shard_map/concatenate | solution.py:233
  2.4 11.1 %all-to-all-start = ((bf16[128,8,128]{2,1,0:T(8,128)(2,1)}), bf16[128,8,128]{2,1,0:T(8,128)(2,1)S(1)}, u32[]{:S(2)}, u32[]{:S(2)}) async-start(bf16[128,8,128]{2,1,0:T(8,128)(2,1)} %bitcast.2), calls=%async_computation | async-start | bytes 524288 | tf_op jit(solution)/shard_map/all_to_all | solution.py:235
  15.5 1.3 %pack.1 = (bf16[64,1536]{1,0:T(8,128)(2,1)}, bf16[64,1536]{1,0:T(8,128)(2,1)}, bf16[64,1536]{1,0:T(8,128)(2,1)}, bf16[64,1536]{1,0:T(8,128)(2,1)}, bf16[64,1536]...) custom-call(s32[131]{0:T(256)S(4)} %info.1, ...), custom_call_target="tpu_custom_call" | custom-call | tf_op jit(solution)/shard_map/pack/pallas_call | solution.py:237
  16.8 7.3 %all-to-all-done = bf16[128,8,128]{2,1,0:T(8,128)(2,1)S(1)} async-done(((bf16[128,8,128]{2,1,0:T(8,128)(2,1)}), bf16[128,8,128]{2,1,0:T(8,128)(2,1)S(1)}, u32[]{:S(2)}, u32[]{:S(2)}) %all-to-all-start) | async-done | bytes 262176 | tf_op jit(solution)/shard_map/all_to_all | solution.py:235
  24.1 1.2 %select_inner.1 = bf16[16,256,128]{2,1,0:T(8,128)(2,1)} custom-call(s32[131]{0:T(256)S(4)} %info.1, bf16[32,32,128]{2,1,0:T(8,128)(2,1)S(1)} %bitcast.19), custom_call_target="tpu_custom_call" | custom-call | tf_op jit(solution)/shard_map/select_inner/pallas_call | solution.py:246
  25.3 3.9 %all-to-all-start.1 = ((bf16[16,256,128]{2,1,0:T(8,128)(2,1)}), bf16[16,256,128]{2,1,0:T(8,128)(2,1)S(1)}, u32[]{:S(2)}, u32[]{:S(2)}) async-start(bf16[16,256,128]{2,1,0:T(8,128)(2,1)} %select_inner.1), calls=%async_computation.1 | async-start | bytes 2097152 | tf_op jit(solution)/shard_map/all_to_all | solution.py:254
  29.2 1.3 %collective-permute-start.1 = (bf16[64,1536]{1,0:T(8,128)(2,1)S(1)}, bf16[64,1536]{1,0:T(8,128)(2,1)S(1)}, u32[]{:S(2)}, u32[]{:S(2)}) collective-permute-start(bf16[64,1536]{1,0:T(8,128)(2,1)S(1)} %copy-done.11), channel_id=1, source_target_pairs={{0,2},{1,3},{2,0},{3,1},{4,6},{5,7},{6,4},{7,5},{8,10},{9,11},{10,... | collective-permute-start | bytes 589832 | tf_op jit(solution)/shard_map/ppermute | solution.py:109
  31.6 2.1 %collective-permute-start.6 = (bf16[64,1536]{1,0:T(8,128)(2,1)S(1)}, bf16[64,1536]{1,0:T(8,128)(2,1)S(1)}, u32[]{:S(2)}, u32[]{:S(2)}) collective-permute-start(bf16[64,1536]{1,0:T(8,128)(2,1)S(1)} %copy-done.9), channel_id=1, source_target_pairs={{0,3},{1,0},{2,1},{3,2},{4,7},{5,4},{6,5},{7,6},{8,11},{9,8},{10,9... | collective-permute-start | bytes 589832 | tf_op jit(solution)/shard_map/ppermute | solution.py:109
  33.7 4.8 %collective-permute-done.1.refs_1_ = bf16[64,1536]{1,0:T(8,128)(2,1)S(1)} collective-permute-done((bf16[64,1536]{1,0:T(8,128)(2,1)S(1)}, bf16[64,1536]{1,0:T(8,128)(2,1)S(1)}, u32[]{:S(2)}, u32[]{:S(2)}) %collective-permute-start.1) | collective-permute-done | bytes 196640 | tf_op jit(solution)/shard_map/ppermute | solution.py:109
  38.5 2.1 %collective-permute-start.3 = (bf16[64,1536]{1,0:T(8,128)(2,1)S(1)}, bf16[64,1536]{1,0:T(8,128)(2,1)S(1)}, u32[]{:S(2)}, u32[]{:S(2)}) collective-permute-start(bf16[64,1536]{1,0:T(8,128)(2,1)S(1)} %copy-done.7), channel_id=1, source_target_pairs={{0,5},{1,6},{2,7},{3,4},{4,1},{5,2},{6,3},{7,0},{8,13},{9,14},{10,... | collective-permute-start | bytes 589832 | tf_op jit(solution)/shard_map/ppermute | solution.py:109
  40.6 1.3 %collective-permute-done.5.refs_2_ = bf16[64,1536]{1,0:T(8,128)(2,1)S(1)} collective-permute-done((bf16[64,1536]{1,0:T(8,128)(2,1)S(1)}, bf16[64,1536]{1,0:T(8,128)(2,1)S(1)}, u32[]{:S(2)}, u32[]{:S(2)}) %collective-permute-start.5) | collective-permute-done | bytes 196640 | tf_op jit(solution)/shard_map/ppermute | solution.py:109
  42.0 5.6 %all-to-all-done.1.far = bf16[16,256,128]{2,1,0:T(8,128)(2,1)S(1)} async-done(((bf16[16,256,128]{2,1,0:T(8,128)(2,1)}), bf16[16,256,128]{2,1,0:T(8,128)(2,1)S(1)}, u32[]{:S(2)}, u32[]{:S(2)}) %all-to-all-start.1) | async-done | bytes 1048608 | tf_op jit(solution)/shard_map/all_to_all | solution.py:254
  47.5 5.8 %attention.2 = (bf16[64,1536]{1,0:T(8,128)(2,1)S(1)}, bf16[64,1536]{1,0:T(8,128)(2,1)S(1)}, bf16[64,1536]{1,0:T(8,128)(2,1)S(1)}, bf16[64,1536]{1,0:T(8,128)(2,1...) custom-call(s32[131]{0:T(256)S(4)} %info.1, bf16[16,256,128]{2,1,0:T(8,128)(2,1)S(1)} %all-to-all-done.1.far, ...), custom_call_target="tpu_custom_call" | custom-call | flops 6710886400 | bytes 6291456 | tf_op jit(solution)/shard_map/attention/pallas_call | solution.py:281
  55.4 2.1 %collective-permute-start.9 = (bf16[64,1536]{1,0:T(8,128)(2,1)S(1)}, bf16[64,1536]{1,0:T(8,128)(2,1)S(1)}, u32[]{:S(2)}, u32[]{:S(2)}) collective-permute-start(bf16[64,1536]{1,0:T(8,128)(2,1)S(1)} %get-tuple-element.86), channel_id=1, source_target_pairs={{0,3},{1,0},{2,1},{3,2},{4,7},{5,4},{6,5},{7,6},{8,11},{9,8},{10,9... | collective-permute-start | bytes 589832 | tf_op jit(solution)/shard_map/ppermute | solution.py:109
  57.5 7.1 %attention.3 = (bf16[64,1536]{1,0:T(8,128)(2,1)S(1)}, bf16[64,1536]{1,0:T(8,128)(2,1)S(1)}, bf16[64,1536]{1,0:T(8,128)(2,1)S(1)}, bf16[64,1536]{1,0:T(8,128)(2,1)S(1)}, bf16[16,256,128]{2,1,0:T(8,128)(2,1)}) custom-call(s32[131]{0:T(256)S(4)} %info.1, bf16[16,256,128]{2,1,0:T(8,128)(2,1)S(1)} %all-to-all-done.1.far, ...), custom_call_target="tpu_custom_call" | custom-call | flops 6710886400 | bytes 6291456 | tf_op jit(solution)/shard_map/attention/pallas_call | solution.py:281
  64.6 3.9 %all-to-all-start.2 = ((bf16[16,256,128]{2,1,0:T(8,128)(2,1)}), bf16[16,256,128]{2,1,0:T(8,128)(2,1)S(1)}, u32[]{:S(2)}, u32[]{:S(2)}) async-start(bf16[16,256,128]{2,1,0:T(8,128)(2,1)} %get-tuple-element.87), calls=%async_computation.2 | async-start | bytes 2097152 | tf_op jit(solution)/shard_map/all_to_all | solution.py:301
  68.6 1.6 %collective-permute-start.11 = (bf16[64,1536]{1,0:T(8,128)(2,1)S(1)}, bf16[64,1536]{1,0:T(8,128)(2,1)S(1)}, u32[]{:S(2)}, u32[]{:S(2)}) collective-permute-start(bf16[64,1536]{1,0:T(8,128)(2,1)S(1)} %get-tuple-element.93), channel_id=1, source_target_pairs={{0,6},{1,7},{2,4},{3,5},{4,2},{5,3},{6,0},{7,1},{8,14},{9,15},{10,... | collective-permute-start | bytes 589832 | tf_op jit(solution)/shard_map/ppermute | solution.py:109
  70.4 2.8 %collective-permute-start.13 = (bf16[64,1536]{1,0:T(8,128)(2,1)S(1)}, bf16[64,1536]{1,0:T(8,128)(2,1)S(1)}, u32[]{:S(2)}, u32[]{:S(2)}) collective-permute-start(bf16[64,1536]{1,0:T(8,128)(2,1)S(1)} %get-tuple-element.95), channel_id=1, source_target_pairs={{0,7},{1,4},{2,5},{3,6},{4,3},{5,0},{6,1},{7,2},{8,15},{9,12},{10,... | collective-permute-start | bytes 589832 | tf_op jit(solution)/shard_map/ppermute | solution.py:109
  73.2 3.7 %collective-permute-done.11.refs_5_ = bf16[64,1536]{1,0:T(8,128)(2,1)S(1)} collective-permute-done((bf16[64,1536]{1,0:T(8,128)(2,1)S(1)}, bf16[64,1536]{1,0:T(8,128)(2,1)S(1)}, u32[]{:S(2)}, u32[]{:S(2)}) %collective-permute-start.11) | collective-permute-done | bytes 196640 | tf_op jit(solution)/shard_map/ppermute | solution.py:109
  77.0 4.7 %collective-permute-done.12.refs_6_ = bf16[64,1536]{1,0:T(8,128)(2,1)S(1)} collective-permute-done((bf16[64,1536]{1,0:T(8,128)(2,1)S(1)}, bf16[64,1536]{1,0:T(8,128)(2,1)S(1)}, u32[]{:S(2)}, u32[]{:S(2)}) %collective-permute-start.12) | collective-permute-done | bytes 196640 | tf_op jit(solution)/shard_map/ppermute | solution.py:109
  81.6 4.9 %all-to-all-done.2.parts = bf16[16,256,128]{2,1,0:T(8,128)(2,1)S(1)} async-done(((bf16[16,256,128]{2,1,0:T(8,128)(2,1)}), bf16[16,256,128]{2,1,0:T(8,128)(2,1)S(1)}, u32[]{:S(2)}, u32[]{:S(2)}) %all-to-all-start.2) | async-done | bytes 1048608 | tf_op jit(solution)/shard_map/all_to_all | solution.py:301
  87.4 4.6 %all-to-all-start.3 = ((bf16[128,8,128]{2,1,0:T(8,128)(2,1)}), bf16[128,8,128]{2,1,0:T(8,128)(2,1)S(1)}, u32[]{:S(2)}, u32[]{:S(2)}) async-start(bf16[128,8,128]{2,1,0:T(8,128)(2,1)} %bitcast.4), calls=%async_computation.3 | async-start | bytes 524288 | tf_op jit(solution)/shard_map/all_to_all | solution.py:314
  93.9 1.3 %unpack.1 = (bf16[64,5120]{1,0:T(8,128)(2,1)}, bf16[64,5120]{1,0:T(8,128)(2,1)}, bf16[64,1024]{1,0:T(8,128)(2,1)S(1)}, bf16[64,1024]{1,0:T(8,128)(2,1)S(1)}) custom-call(s32[131]{0:T(256)S(4)} %info.1, bf16[64,1536]{1,0:T(8,128)(2,1)S(1)} %get-tuple-element.97.refs_0_, bf16[64,1536]{1,0:T(8,128)(2,1)S(1)} %collective-permute-done.7.refs_1_, ...), custom_call_target="tpu_custom_call" | custom-call | tf_op jit(solution)/shard_map/unpack/pallas_call | solution.py:318
  95.2 7.3 %all-to-all-done.3 = bf16[128,8,128]{2,1,0:T(8,128)(2,1)S(1)} async-done(((bf16[128,8,128]{2,1,0:T(8,128)(2,1)}), bf16[128,8,128]{2,1,0:T(8,128)(2,1)S(1)}, u32[]{:S(2)}, u32[]{:S(2)}) %all-to-all-start.3) | async-done | bytes 262176 | tf_op jit(solution)/shard_map/all_to_all | solution.py:314
  (46 shorter events, 8.2 us)
Async XLA Ops:
  0.6 13.7 %copy-start = (bf16[64,5120]{1,0:T(8,128)(2,1)S(1)}, bf16[64,5120]{1,0:T(8,128)(2,1)}, u32[]{:S(2)}) copy-start(bf16[64,5120]{1,0:T(8,128)(2,1)} %queries.1) | copy-start | bytes 1966084
  2.4 12.0 %copy-start.3 = (bf16[64,1024]{1,0:T(8,128)(2,1)S(1)}, bf16[64,1024]{1,0:T(8,128)(2,1)}, u32[]{:S(2)}) copy-start(bf16[64,1024]{1,0:T(8,128)(2,1)} %keys.1) | copy-start | bytes 393220
  2.4 21.7 %all-to-all-start = ((bf16[128,8,128]{2,1,0:T(8,128)(2,1)}), bf16[128,8,128]{2,1,0:T(8,128)(2,1)S(1)}, u32[]{:S(2)}, u32[]{:S(2)}) async-start(bf16[128,8,128]{2,1,0:T(8,128)(2,1)} %bitcast.2), calls=%async_computation | async-start | bytes 524288 | tf_op jit(solution)/shard_map/all_to_all | solution.py:235
  25.2 13.3 %copy-start.8 = (bf16[64,1536]{1,0:T(8,128)(2,1)S(1)}, bf16[64,1536]{1,0:T(8,128)(2,1)}, u32[]{:S(2)}) copy-start(bf16[64,1536]{1,0:T(8,128)(2,1)} %get-tuple-element.73) | copy-start | bytes 589828
  25.3 13.3 %copy-start.7 = (bf16[64,1536]{1,0:T(8,128)(2,1)S(1)}, bf16[64,1536]{1,0:T(8,128)(2,1)}, u32[]{:S(2)}) copy-start(bf16[64,1536]{1,0:T(8,128)(2,1)} %get-tuple-element.74) | copy-start | bytes 589828
  25.3 16.7 %copy-start.6 = (bf16[64,1536]{1,0:T(8,128)(2,1)S(1)}, bf16[64,1536]{1,0:T(8,128)(2,1)}, u32[]{:S(2)}) copy-start(bf16[64,1536]{1,0:T(8,128)(2,1)} %get-tuple-element.75) | copy-start | bytes 589828
  25.3 22.2 %copy-start.4 = (bf16[64,1536]{1,0:T(8,128)(2,1)S(1)}, bf16[64,1536]{1,0:T(8,128)(2,1)}, u32[]{:S(2)}) copy-start(bf16[64,1536]{1,0:T(8,128)(2,1)} %get-tuple-element.76.refs_0_) | copy-start | bytes 589828
  25.3 22.2 %all-to-all-start.1 = ((bf16[16,256,128]{2,1,0:T(8,128)(2,1)}), bf16[16,256,128]{2,1,0:T(8,128)(2,1)S(1)}, u32[]{:S(2)}, u32[]{:S(2)}) async-start(bf16[16,256,128]{2,1,0:T(8,128)(2,1)} %select_inner.1), calls=%async_computation.1 | async-start | bytes 2097152 | tf_op jit(solution)/shard_map/all_to_all | solution.py:254
  29.2 9.4 %collective-permute-start.1 = (bf16[64,1536]{1,0:T(8,128)(2,1)S(1)}, bf16[64,1536]{1,0:T(8,128)(2,1)S(1)}, u32[]{:S(2)}, u32[]{:S(2)}) collective-permute-start(bf16[64,1536]{1,0:T(8,128)(2,1)S(1)} %copy-done.11), channel_id=1, source_target_pairs={{0,2},{1,3},{2,0},{3,1},{4,6},{5,7},{6,4},{7,5},{8,10},{9,11},{10,... | collective-permute-start | bytes 589832 | tf_op jit(solution)/shard_map/ppermute | solution.py:109
  30.5 11.5 %collective-permute-start.5 = (bf16[64,1536]{1,0:T(8,128)(2,1)S(1)}, bf16[64,1536]{1,0:T(8,128)(2,1)S(1)}, u32[]{:S(2)}, u32[]{:S(2)}) collective-permute-start(bf16[64,1536]{1,0:T(8,128)(2,1)S(1)} %copy-done.10), channel_id=1, source_target_pairs={{0,1},{1,2},{2,3},{3,0},{4,5},{5,6},{6,7},{7,4},{8,9},{9,10},{10,1... | collective-permute-start | bytes 589832 | tf_op jit(solution)/shard_map/ppermute | solution.py:109
  31.6 10.3 %collective-permute-start.6 = (bf16[64,1536]{1,0:T(8,128)(2,1)S(1)}, bf16[64,1536]{1,0:T(8,128)(2,1)S(1)}, u32[]{:S(2)}, u32[]{:S(2)}) collective-permute-start(bf16[64,1536]{1,0:T(8,128)(2,1)S(1)} %copy-done.9), channel_id=1, source_target_pairs={{0,3},{1,0},{2,1},{3,2},{4,7},{5,4},{6,5},{7,6},{8,11},{9,8},{10,9... | collective-permute-start | bytes 589832 | tf_op jit(solution)/shard_map/ppermute | solution.py:109
  33.7 20.5 %collective-permute-start = (bf16[64,1536]{1,0:T(8,128)(2,1)}, bf16[64,1536]{1,0:T(8,128)(2,1)S(1)}, u32[]{:S(2)}, u32[]{:S(2)}) collective-permute-start(bf16[64,1536]{1,0:T(8,128)(2,1)} %get-tuple-element.68), channel_id=1, source_target_pairs={{0,4},{1,5},{2,6},{3,7},{4,0},{5,1},{6,2},{7,3},{8,12},{9,13},{10,... | collective-permute-start | bytes 589832 | tf_op jit(solution)/shard_map/ppermute | solution.py:109
  38.5 16.9 %collective-permute-start.2 = (bf16[64,1536]{1,0:T(8,128)(2,1)S(1)}, bf16[64,1536]{1,0:T(8,128)(2,1)S(1)}, u32[]{:S(2)}, u32[]{:S(2)}) collective-permute-start(bf16[64,1536]{1,0:T(8,128)(2,1)S(1)} %copy-done.8), channel_id=1, source_target_pairs={{0,6},{1,7},{2,4},{3,5},{4,2},{5,3},{6,0},{7,1},{8,14},{9,15},{10,... | collective-permute-start | bytes 589832 | tf_op jit(solution)/shard_map/ppermute | solution.py:109
  38.5 18.9 %collective-permute-start.3 = (bf16[64,1536]{1,0:T(8,128)(2,1)S(1)}, bf16[64,1536]{1,0:T(8,128)(2,1)S(1)}, u32[]{:S(2)}, u32[]{:S(2)}) collective-permute-start(bf16[64,1536]{1,0:T(8,128)(2,1)S(1)} %copy-done.7), channel_id=1, source_target_pairs={{0,5},{1,6},{2,7},{3,4},{4,1},{5,2},{6,3},{7,0},{8,13},{9,14},{10,... | collective-permute-start | bytes 589832 | tf_op jit(solution)/shard_map/ppermute | solution.py:109
  42.0 15.5 %collective-permute-start.4 = (bf16[64,1536]{1,0:T(8,128)(2,1)S(1)}, bf16[64,1536]{1,0:T(8,128)(2,1)S(1)}, u32[]{:S(2)}, u32[]{:S(2)}) collective-permute-start(bf16[64,1536]{1,0:T(8,128)(2,1)S(1)} %copy-done.6), channel_id=1, source_target_pairs={{0,7},{1,4},{2,5},{3,6},{4,3},{5,0},{6,1},{7,2},{8,15},{9,12},{10,... | collective-permute-start | bytes 589832 | tf_op jit(solution)/shard_map/ppermute | solution.py:109
  53.3 11.3 %collective-permute-start.7 = (bf16[64,1536]{1,0:T(8,128)(2,1)S(1)}, bf16[64,1536]{1,0:T(8,128)(2,1)S(1)}, u32[]{:S(2)}, u32[]{:S(2)}) collective-permute-start(bf16[64,1536]{1,0:T(8,128)(2,1)S(1)} %get-tuple-element.84), channel_id=1, source_target_pairs={{0,2},{1,3},{2,0},{3,1},{4,6},{5,7},{6,4},{7,5},{8,10},{9,11},{10,... | collective-permute-start | bytes 589832 | tf_op jit(solution)/shard_map/ppermute | solution.py:109
  54.2 10.4 %collective-permute-start.8 = (bf16[64,1536]{1,0:T(8,128)(2,1)S(1)}, bf16[64,1536]{1,0:T(8,128)(2,1)S(1)}, u32[]{:S(2)}, u32[]{:S(2)}) collective-permute-start(bf16[64,1536]{1,0:T(8,128)(2,1)S(1)} %get-tuple-element.85), channel_id=1, source_target_pairs={{0,1},{1,2},{2,3},{3,0},{4,5},{5,6},{6,7},{7,4},{8,9},{9,10},{10,1... | collective-permute-start | bytes 589832 | tf_op jit(solution)/shard_map/ppermute | solution.py:109
  55.4 9.2 %collective-permute-start.9 = (bf16[64,1536]{1,0:T(8,128)(2,1)S(1)}, bf16[64,1536]{1,0:T(8,128)(2,1)S(1)}, u32[]{:S(2)}, u32[]{:S(2)}) collective-permute-start(bf16[64,1536]{1,0:T(8,128)(2,1)S(1)} %get-tuple-element.86), channel_id=1, source_target_pairs={{0,3},{1,0},{2,1},{3,2},{4,7},{5,4},{6,5},{7,6},{8,11},{9,8},{10,9... | collective-permute-start | bytes 589832 | tf_op jit(solution)/shard_map/ppermute | solution.py:109
  64.6 21.9 %all-to-all-start.2 = ((bf16[16,256,128]{2,1,0:T(8,128)(2,1)}), bf16[16,256,128]{2,1,0:T(8,128)(2,1)S(1)}, u32[]{:S(2)}, u32[]{:S(2)}) async-start(bf16[16,256,128]{2,1,0:T(8,128)(2,1)} %get-tuple-element.87), calls=%async_computation.2 | async-start | bytes 2097152 | tf_op jit(solution)/shard_map/all_to_all | solution.py:301
  68.5 4.7 %collective-permute-start.10 = (bf16[64,1536]{1,0:T(8,128)(2,1)S(1)}, bf16[64,1536]{1,0:T(8,128)(2,1)S(1)}, u32[]{:S(2)}, u32[]{:S(2)}) collective-permute-start(bf16[64,1536]{1,0:T(8,128)(2,1)S(1)} %get-tuple-element.92), channel_id=1, source_target_pairs={{0,4},{1,5},{2,6},{3,7},{4,0},{5,1},{6,2},{7,3},{8,12},{9,13},{10,... | collective-permute-start | bytes 589832 | tf_op jit(solution)/shard_map/ppermute | solution.py:109
  68.6 8.3 %collective-permute-start.11 = (bf16[64,1536]{1,0:T(8,128)(2,1)S(1)}, bf16[64,1536]{1,0:T(8,128)(2,1)S(1)}, u32[]{:S(2)}, u32[]{:S(2)}) collective-permute-start(bf16[64,1536]{1,0:T(8,128)(2,1)S(1)} %get-tuple-element.93), channel_id=1, source_target_pairs={{0,6},{1,7},{2,4},{3,5},{4,2},{5,3},{6,0},{7,1},{8,14},{9,15},{10,... | collective-permute-start | bytes 589832 | tf_op jit(solution)/shard_map/ppermute | solution.py:109
  70.3 11.4 %collective-permute-start.12 = (bf16[64,1536]{1,0:T(8,128)(2,1)S(1)}, bf16[64,1536]{1,0:T(8,128)(2,1)S(1)}, u32[]{:S(2)}, u32[]{:S(2)}) collective-permute-start(bf16[64,1536]{1,0:T(8,128)(2,1)S(1)} %get-tuple-element.94), channel_id=1, source_target_pairs={{0,5},{1,6},{2,7},{3,4},{4,1},{5,2},{6,3},{7,0},{8,13},{9,14},{10,... | collective-permute-start | bytes 589832 | tf_op jit(solution)/shard_map/ppermute | solution.py:109
  70.4 11.2 %collective-permute-start.13 = (bf16[64,1536]{1,0:T(8,128)(2,1)S(1)}, bf16[64,1536]{1,0:T(8,128)(2,1)S(1)}, u32[]{:S(2)}, u32[]{:S(2)}) collective-permute-start(bf16[64,1536]{1,0:T(8,128)(2,1)S(1)} %get-tuple-element.95), channel_id=1, source_target_pairs={{0,7},{1,4},{2,5},{3,6},{4,3},{5,0},{6,1},{7,2},{8,15},{9,12},{10,... | collective-permute-start | bytes 589832 | tf_op jit(solution)/shard_map/ppermute | solution.py:109
  87.4 15.1 %all-to-all-start.3 = ((bf16[128,8,128]{2,1,0:T(8,128)(2,1)}), bf16[128,8,128]{2,1,0:T(8,128)(2,1)S(1)}, u32[]{:S(2)}, u32[]{:S(2)}) async-start(bf16[128,8,128]{2,1,0:T(8,128)(2,1)} %bitcast.4), calls=%async_computation.3 | async-start | bytes 524288 | tf_op jit(solution)/shard_map/all_to_all | solution.py:314
  (6 other events, 29.2 us)
